TPU v7x, 256 devices: a whole 4x4x8 slice. The times are simulated.
256 devices in a mesh: tm: 32 (over z, x_hi, core), tok: 8 (over x_lo, y).
Axes of the slice: x: 4 (x_hi: 2, x_lo: 2; x = x_hi * 2 + x_lo), y: 4, z: 8, core: 2. Of those that a mesh axis runs over, the one named last changes fastest.
Arguments:
- latents: bfloat16 [64, 1024, 1536], P('tm', 'tok'), may hold values from -6 to 6
- fresh_noise: bfloat16 [1024, 1536], P('tok'), may hold values from -6 to 6
- noise_levels: int32 [64], replicated, may hold values from 0 to 31
- offset: int32 [1], replicated, may hold values from 0 to 63
- block_ids: int32 [64], replicated, may hold values from 0 to 31, never falling along the last dimension, each value on 1 to 4 neighbouring positions
- mod_table: float32 [32, 3, 1536], replicated, may hold values from -4 to 4
- step_sizes: float32 [32], replicated, may hold values from 0.25 to 1
- w_query: bfloat16 [1536, 768], replicated, as said below
- w_key: bfloat16 [1536, 768], replicated, as said below
- w_value: bfloat16 [1536, 768], replicated, may hold values from -0.15625 to 0.15625
- w_out: bfloat16 [768, 1536], replicated, may hold values from -0.21875 to 0.21875
Outputs:
- velocity: bfloat16 [64, 1024, 1536], P('tm', 'tok')
- next_window: bfloat16 [64, 1024, 1536], P('tm', 'tok')
Inputs may be any that keep to these rules, and one draw needn't show every extreme that they name: `block_ids`: never falling along the window; each block holds 1 to 4 consecutive frames. `w_query`: entries lie within 20 over the square root of 1536 in magnitude. `w_key`: entries lie within 20 over the square root of 1536 in magnitude.
All inputs are finite; a program needn't handle non-finite values.
Results may differ from a plain program's by a relative error of at most 0.008.
Values may be sent and summed in bfloat16 or wider, within the bound.
No kernel may reach another device: no remote copies, remote signals or barrier semaphores. Data moves between devices by JAX's collectives and lax.ppermute only.
A program may use at most 128 MiB of HBM per device.

v0:
```python
import jax
import jax.numpy as jnp
from jax import lax
from jax.sharding import PartitionSpec as P

HEAD_DIM = 128
HEADS = 6


NEG_FILL = -1e30


def passed_along(block, axis, distance):
    devices = range(lax.axis_size(axis))
    route = [(i - distance, i) for i in devices if i - distance in devices]
    return lax.ppermute(block, axis, route)


def modulation(frame_ids, noise_levels, offset, mod_table, step_sizes):
    total_frames = noise_levels.shape[0]
    slots = (frame_ids + offset[0]) % total_frames
    slot_hits = slots[:, None] == jnp.arange(total_frames, dtype=jnp.int32)[None, :]
    level_ids = jnp.sum(jnp.where(slot_hits, noise_levels[None, :], 0), axis=1)
    level_count = mod_table.shape[0]
    one_hot = (level_ids[:, None] == jnp.arange(level_count, dtype=jnp.int32)[None, :]).astype(
        jnp.float32
    )
    mods = jnp.dot(one_hot, mod_table.reshape(level_count, -1), precision=lax.Precision.HIGHEST)
    mods = mods.reshape(frame_ids.shape[0], 3, mod_table.shape[2])
    steps_now = jnp.dot(one_hot, step_sizes[:, None], precision=lax.Precision.HIGHEST)[:, 0]
    return (mods[:, 0], mods[:, 1], mods[:, 2], steps_now)


def project(latents, shift, scale, w_query, w_key, w_value):
    values = latents.astype(jnp.float32)
    center = jnp.mean(values, axis=-1, keepdims=True)
    spread = jnp.mean(jnp.square(values - center), axis=-1, keepdims=True)
    normed = (values - center) * lax.rsqrt(spread + 1e-06) * (1.0 + scale[:, None, :]) + shift[
        :, None, :
    ]
    normed = normed.astype(jnp.bfloat16)
    flattened = normed.reshape(-1, normed.shape[-1])
    projected = [
        jnp.dot(flattened, weight, preferred_element_type=jnp.float32).astype(jnp.bfloat16)
        for weight in (w_query, w_key, w_value)
    ]
    return (values, projected)


def online_update(carry, scores, mask_now):
    run_max, run_sum, run_acc = carry
    scores = jnp.where(mask_now, scores, NEG_FILL)
    new_max = jnp.maximum(run_max, jnp.max(scores, axis=-1))
    weights = jnp.where(mask_now, jnp.exp(scores - new_max[..., None]), 0.0)
    rescale = jnp.exp(run_max - new_max)
    return (
        new_max,
        run_sum * rescale + jnp.sum(weights, axis=-1),
        run_acc * rescale[..., None],
        weights.astype(jnp.bfloat16),
    )


def body(
    latents,
    fresh_noise,
    noise_levels,
    offset,
    block_ids,
    mod_table,
    step_sizes,
    w_query,
    w_key,
    w_value,
    w_out,
):
    frame_dev, tok_dev, width = latents.shape
    time_count = lax.axis_size("tm")
    first_frame = lax.axis_index("tm") * frame_dev
    frame_ids = first_frame + jnp.arange(frame_dev, dtype=jnp.int32)
    shift, scale, gate, steps_now = modulation(
        frame_ids, noise_levels, offset, mod_table, step_sizes
    )
    values, projected = project(latents, shift, scale, w_query, w_key, w_value)
    queries, key_rows, value_rows = [
        part.reshape(frame_dev, tok_dev, HEADS, HEAD_DIM) for part in projected
    ]
    score_scale = HEAD_DIM ** (-0.5)
    my_blocks = lax.dynamic_slice_in_dim(block_ids, first_frame, frame_dev)
    empty = (
        jnp.full((frame_dev, tok_dev, HEADS), NEG_FILL, jnp.float32),
        jnp.zeros((frame_dev, tok_dev, HEADS), jnp.float32),
        jnp.zeros((frame_dev, tok_dev, HEADS, HEAD_DIM), jnp.float32),
    )
    key_piece = lax.all_gather(key_rows, "tok", axis=1, tiled=True)
    value_piece = lax.all_gather(value_rows, "tok", axis=1, tiled=True)
    scores = (
        jnp.einsum("fphd,fkhd->fphk", queries, key_piece, preferred_element_type=jnp.float32)
        * score_scale
    )
    full_mask = jnp.ones((1, 1, 1, scores.shape[3]), dtype=bool)
    new_max, new_sum, scaled_acc, weights = online_update(empty, scores, full_mask)
    added = jnp.einsum("fphk,fkhd->fphd", weights, value_piece, preferred_element_type=jnp.float32)
    carry = (new_max, new_sum, added)
    key_piece = lax.all_gather(key_rows, "tm", axis=0, tiled=True)
    value_piece = lax.all_gather(value_rows, "tm", axis=0, tiled=True)
    count_now = key_piece.shape[0]
    piece_frames = jnp.arange(count_now, dtype=jnp.int32)
    allowed = (block_ids[None, :] <= my_blocks[:, None]) & (
        piece_frames[None, :] != frame_ids[:, None]
    )
    scores = (
        jnp.einsum("fphd,gphd->fphg", queries, key_piece, preferred_element_type=jnp.float32)
        * score_scale
    )
    temporal_new_max, temporal_new_sum, scaled_acc, weights = online_update(
        carry, scores, allowed[:, None, None, :]
    )
    temporal_added = jnp.einsum(
        "fphg,gphd->fphd", weights, value_piece, preferred_element_type=jnp.float32
    )
    attended = ((scaled_acc + temporal_added) / temporal_new_sum[..., None]).astype(jnp.bfloat16)
    flat_attended = attended.reshape(-1, HEADS * HEAD_DIM)
    projected_out = jnp.dot(flat_attended, w_out, preferred_element_type=jnp.float32).reshape(
        frame_dev, tok_dev, width
    )
    moving = gate[:, None, :] * projected_out
    advanced = (values + steps_now[:, None, None] * moving).astype(jnp.bfloat16)
    received = passed_along(advanced[0:1], "tm", -1)
    is_last = lax.axis_index("tm") == time_count - 1
    incoming = jnp.where(is_last, fresh_noise[None], received)
    next_window = jnp.concatenate([advanced[1:], incoming], axis=0)
    return (moving.astype(jnp.bfloat16), next_window)


def solution(mesh):
    in_specs = (P("tm", "tok", None), P("tok", None), P(), P(), P(), P(), P(), P(), P(), P(), P())
    out_specs = (P("tm", "tok", None), P("tm", "tok", None))
    return jax.shard_map(body, mesh=mesh, in_specs=in_specs, out_specs=out_specs, check_vma=False)
```

profile of v0, /device:TPU:5, one launch (start us, length us, event | category | flops | bytes accessed | tf_op | source)
XLA Modules:
  0.0 383.7 jit_solution(7923611449927389545)
XLA Ops:
  7.2 0.0 all-gather.7.cloned.1.call-start
  8.1 1.0 fusion.51
  9.0 1.4 fusion.43
  10.4 1.3 convert_reduce_fusion
  11.8 1.5 fusion.14
  13.3 1.5 fusion.17
  14.8 0.9 copy-done.2
  15.7 0.8 convolution_convert_fusion.1
  16.4 0.5 reshape.140
  16.9 0.8 copy.81
  17.7 0.0 all-gather.7.cloned.1.call-update
  17.7 0.0 all-gather.9.cloned.1.call-start
  17.8 0.7 all-gather.9.cloned.1.call-update
  18.5 0.0 all-gather.11.cloned.1.call-start
  18.5 2.7 convolution_convert_fusion.2
  21.2 0.2 copy.78
  21.4 0.1 reshape.133
  21.5 1.0 copy.89
  22.6 0.0 all-gather.5.cloned.1.call-start
  22.6 0.8 copy.79
  23.5 0.0 all-gather.5.cloned.1.call-update
  23.5 2.7 convolution_convert_fusion
  26.2 0.2 copy.82
  26.4 0.1 reshape.135
  26.5 0.5 copy.87
  27.0 0.1 dynamic_slice.3
  27.1 0.2 convolution_bitcast_fusion
  27.3 0.1 compare_and_fusion
  27.4 36.9 %all-gather.7.cloned.1.call-done = bf16[2,1024,6,128]{3,1,2,0:T(8,128)(2,1)} async-done(((bf16[2,128,6,128]{3,1,2,0:T(8,128)(2,1)}), bf16[2,1024,6,128]{3,1,2,0:T(8,128)(2,1)}) %all-gather.7.cloned.1.call-update) | async-done | bytes 3145744 | tf_op jit(solution)/shard_map/all_gather | solution.py:95
  64.3 5.6 %bitcast_reduce_fusion = (f32[2,128,6]{1,2,0:T(8,128)S(1)}, f32[2,6,1024,128]{3,2,1,0:T(8,128)}) fusion(bf16[2,1024,6,128]{3,1,2,0:T(8,128)(2,1)} %all-gather.7.cloned.1.call-done, bf16[2,128,6,128]{1,0,3,2:T(2,128)(2,1)S(1)} %reshape.135), kind=kOutput, calls=%fused_computation.5 | convolution fusion | flops 405797376 | bytes 9836544 | tf_op jit(solution)/shard_map/fphd,fkhd->fphk/dot_general | solution.py:98
  69.8 116.2 %all-gather.9.cloned.1.call-done = bf16[64,128,6,128]{3,1,2,0:T(8,128)(2,1)} async-done(((bf16[2,128,6,128]{3,1,2,0:T(8,128)(2,1)}), bf16[64,128,6,128]{3,1,2,0:T(8,128)(2,1)}) %all-gather.9.cloned.1.call-update) | async-done | bytes 12582928 | tf_op jit(solution)/shard_map/all_gather | solution.py:105
  186.0 30.1 %fusion.60 = (f32[2,128,6]{0,2,1:T(8,128)S(1)}, f32[2,128,6,64]{3,0,2,1:T(2,128)}) fusion(bf16[2,128,6,128]{3,0,2,1:T(2,128)(2,1)S(1)} %copy.87, bf16[64,128,6,128]{3,1,2,0:T(8,128)(2,1)} %all-gather.9.cloned.1.call-done, pred[2,64]{1,0:T(4,128)(4,1)S(1)} %compare_and_fusion), kind=kOutput, calls=%fused_computation.71 | convolution fusion | flops 25459200 | bytes 13375616 | tf_op jit(solution)/shard_map/fphd,gphd->fphg/dot_general | solution.py:113
  216.1 0.2 copy.88
  216.4 0.3 copy.90
  216.6 2.8 fusion.58
  219.5 0.2 copy.93
  219.7 83.5 %all-gather.11.cloned.1.call-done = bf16[64,128,6,128]{3,1,2,0:T(8,128)(2,1)} async-done(((bf16[2,128,6,128]{3,1,2,0:T(8,128)(2,1)}), bf16[64,128,6,128]{3,1,2,0:T(8,128)(2,1)}) %all-gather.11.cloned.1.call-update) | async-done | bytes 12582928 | tf_op jit(solution)/shard_map/all_gather | solution.py:106
  303.1 31.2 %fusion = f32[128,6,128,2]{2,3,1,0:T(2,128)} fusion(bf16[64,128,6,128]{3,1,2,0:T(8,128)(2,1)} %all-gather.11.cloned.1.call-done, f32[2,128,6,64]{3,0,2,1:T(2,128)} %get-tuple-element.15, pred[2,64]{1,0:T(4,128)(4,1)S(1)} %compare_and_fusion, f32[2,128,6]{0,2,1:T(8,128)S(1)} %copy.90), kind=kOutput, calls=%fused_computation | convolution fusion | flops 25460736 | bytes 13768832 | tf_op jit(solution)/shard_map/fphg,gphd->fphd/dot_general | solution.py:119
  334.4 1.4 copy.92
  335.8 3.9 %fusion.5 = f32[2,128,6]{1,2,0:T(8,128)S(1)} fusion(f32[2,6,1024,128]{3,2,1,0:T(8,128)} %get-tuple-element.13, f32[2,128,6]{1,2,0:T(8,128)S(1)} %get-tuple-element.11), kind=kLoop, calls=%fused_computation.7 | loop fusion | flops 4717056 | bytes 6303744 | tf_op jit(solution)/shard_map/reduce_sum | solution.py:58
  339.6 14.4 %all-gather.5.cloned.1.call-done = bf16[2,1024,6,128]{1,3,2,0:T(8,128)(2,1)} async-done(((bf16[2,128,6,128]{1,3,2,0:T(8,128)(2,1)}), bf16[2,1024,6,128]{1,3,2,0:T(8,128)(2,1)}) %all-gather.5.cloned.1.call-update) | async-done | bytes 3145744 | tf_op jit(solution)/shard_map/all_gather | solution.py:96
  354.1 5.6 %fusion.37 = bf16[2,128,6,128]{1,3,2,0:T(8,128)(2,1)S(1)} fusion(bf16[2,1024,6,128]{1,3,2,0:T(8,128)(2,1)} %all-gather.5.cloned.1.call-done, f32[2,6,1024,128]{3,2,1,0:T(8,128)} %get-tuple-element.13, f32[2,128,6]{1,2,0:T(8,128)S(1)} %get-tuple-element.11, f32[128,6,128,2]{0,2,1,3:T(8,128)S(1)} %copy.92, f32[2,128,6]{1,2,0:T(8,128)S(1)} %multiply_add_fusion, ...), kind=kOutput, calls=%fused_computation.34 | convolution fusion | flops 408158208 | bytes 10635264 | tf_op jit(solution)/shard_map/fphk,fkhd->fphd/dot_general | solution.py:103
  359.7 1.7 fusion.18
  361.4 0.1 fusion.59
  361.5 6.7 %collective-permute-start = (bf16[1,128,1536]{2,1,0:T(8,128)(2,1)S(1)}, bf16[1,128,1536]{2,1,0:T(8,128)(2,1)}, u32[]{:S(2)}, u32[]{:S(2)}) collective-permute-start(bf16[1,128,1536]{2,1,0:T(8,128)(2,1)S(1)} %get-tuple-element.5), channel_id=1, source_target_pairs={{8,0},{16,8},{24,16},{32,24},{40,32},{48,40},{56,48},{64,56},{72,6... | collective-permute-start | bytes 1179656 | tf_op jit(solution)/shard_map/ppermute | solution.py:16
  368.2 6.8 %collective-permute-done = bf16[1,128,1536]{2,1,0:T(8,128)(2,1)} collective-permute-done((bf16[1,128,1536]{2,1,0:T(8,128)(2,1)S(1)}, bf16[1,128,1536]{2,1,0:T(8,128)(2,1)}, u32[]{:S(2)}, u32[]{:S(2)}) %collective-permute-start) | collective-permute-done | bytes 393248 | tf_op jit(solution)/shard_map/ppermute | solution.py:16
  374.9 1.0 bitcast_select_fusion
  376.0 0.9 pad_maximum_fusion
  (21 shorter events, 0.1 us)
Async XLA Ops:
  7.2 352.5 %copy-start = (bf16[768,1536]{1,0:T(8,128)(2,1)S(1)}, bf16[768,1536]{1,0:T(8,128)(2,1)}, u32[]{:S(2)}) copy-start(bf16[768,1536]{1,0:T(8,128)(2,1)} %param.21) | copy-start | bytes 7077892
  7.2 57.1 %all-gather.7.cloned.1.call-start = ((), (), s32[]{:S(2)}) async-start(), calls=%async_computation.1 | async-start | bytes 3538944 | tf_op jit(solution)/shard_map/all_gather | solution.py:95
  8.0 7.6 %copy-start.5 = (bf16[1536,768]{1,0:T(8,128)(2,1)S(1)}, bf16[1536,768]{1,0:T(8,128)(2,1)}, u32[]{:S(2)}) copy-start(bf16[1536,768]{1,0:T(8,128)(2,1)} %param.19) | copy-start | bytes 7077892
  14.8 0.9 copy-start.2
  17.7 168.3 %all-gather.9.cloned.1.call-start = ((), (), s32[]{:S(2)}) async-start(), calls=%async_computation.2 | async-start | bytes 12976128 | tf_op jit(solution)/shard_map/all_gather | solution.py:105
  18.5 284.6 %all-gather.11.cloned.1.call-start = ((), (), s32[]{:S(2)}) async-start(), calls=%async_computation.3 | async-start | bytes 12976128 | tf_op jit(solution)/shard_map/all_gather | solution.py:106
  22.6 331.5 %all-gather.5.cloned.1.call-start = ((), (), s32[]{:S(2)}) async-start(), calls=%async_computation | async-start | bytes 3538944 | tf_op jit(solution)/shard_map/all_gather | solution.py:96
  23.5 3.5 copy-start.4
  23.5 3.6 copy-start.6
  354.1 5.6 %copy-start.1 = (bf16[2,128,1536]{2,1,0:T(8,128)(2,1)S(1)}, bf16[2,128,1536]{2,1,0:T(8,128)(2,1)}, u32[]{:S(2)}) copy-start(bf16[2,128,1536]{2,1,0:T(8,128)(2,1)} %param.11) | copy-start | bytes 2359300
  359.7 15.2 %copy-start.3 = (bf16[128,1536]{1,0:T(8,128)(2,1)S(1)}, bf16[128,1536]{1,0:T(8,128)(2,1)}, u32[]{:S(2)}) copy-start(bf16[128,1536]{1,0:T(8,128)(2,1)} %param.12) | copy-start | bytes 1179652
  361.5 13.4 %collective-permute-start = (bf16[1,128,1536]{2,1,0:T(8,128)(2,1)S(1)}, bf16[1,128,1536]{2,1,0:T(8,128)(2,1)}, u32[]{:S(2)}, u32[]{:S(2)}) collective-permute-start(bf16[1,128,1536]{2,1,0:T(8,128)(2,1)S(1)} %get-tuple-element.5), channel_id=1, source_target_pairs={{8,0},{16,8},{24,16},{32,24},{40,32},{48,40},{56,48},{64,56},{72,6... | collective-permute-start | bytes 1179656 | tf_op jit(solution)/shard_map/ppermute | solution.py:16
Sparse Core Ops, SparseCore 0:
  17.9 46.3 all-gather.6
  67.6 118.3 all-gather.8
  188.8 114.2 all-gather.10
  304.7 49.3 all-gather.4
where the time goes:
time: 391 us; the launch traced here: 384 us
  waiting for transfers between devices  259 us (66%)
  matrix products  81.9 us (21%)
  between operations  15 us (4%)
  other arithmetic  14.1 us (4%)
  local copies, waits for them, and re-layouts  7.24 us (2%)
  starting transfers between devices  6.82 us (2%)
    all_gather x1, waiting for transfers between devices, body(): key_piece = lax.all_gather(key_rows, 'tm', axis=0, tiled=True)  116 us
    all_gather x1, waiting for transfers between devices, body(): value_piece = lax.all_gather(value_rows, 'tm', axis=0, tiled=True)  83.5 us
    all_gather x1, waiting for transfers between devices, body(): key_piece = lax.all_gather(key_rows, 'tok', axis=1, tiled=True)  36.9 us
    dot_general x1, matrix products, body(): jnp.einsum('fphg,gphd->fphd', weights, value_piece, preferred_element_typ...  31.2 us
    dot_general x1, matrix products, body(): jnp.einsum('fphd,gphd->fphg', queries, key_piece, preferred_element_type=...  30.1 us
    all_gather x1, waiting for transfers between devices, body(): value_piece = lax.all_gather(value_rows, 'tok', axis=1, tiled=True)  14.4 us
  transfers between devices with their start and end apart: 5, of which 5 were waited for; matrix products, arithmetic and copies ran while one was open for 22% of the time, Pallas kernels for 0%

commit v1 on v0

v1 whole, which is shorter than its diff:
```python
import math

import jax
import jax.numpy as jnp
from jax import lax
from jax.experimental import pallas as pl
from jax.experimental.pallas import tpu as pltpu
from jax.sharding import PartitionSpec as P

HEAD_DIM = 128
HEADS = 6
FULL = 4
BASE2 = HEAD_DIM ** (-0.5) * math.log2(math.e)
MASKED = -1e30
FLOOR = -1e29
MIB = 1 << 20
STAT_ROWS = 16


def whole():
    return pl.BlockSpec(memory_space=pltpu.VMEM)


def normalise(x, scale1, shift):
    values = x.astype(jnp.float32)
    center = jnp.mean(values, axis=-1, keepdims=True)
    values = values - center
    spread = jnp.mean(values * values, axis=-1, keepdims=True)
    return (values * lax.rsqrt(spread + 1e-06) * scale1 + shift).astype(jnp.bfloat16)


def matmul(a, b):
    return jnp.dot(a, b, preferred_element_type=jnp.float32)


def attend(q, k, v, bias=None):
    scores = lax.dot_general(q, k, (((1,), (1,)), ((), ())), preferred_element_type=jnp.float32)
    if bias is not None:
        scores = scores + bias
    top = jnp.max(scores, axis=-1, keepdims=True)
    if bias is not None:
        top = jnp.maximum(top, FLOOR)
    weights = jnp.exp2((scores - top) * BASE2)
    total = jnp.sum(weights, axis=-1, keepdims=True)
    mixed = matmul(weights.astype(jnp.bfloat16), v)
    if bias is None:
        return mixed / total, top * BASE2 + jnp.log2(total)
    some = total > 0.0
    safe = jnp.where(some, total, 1.0)
    return mixed / safe, jnp.where(some, top * BASE2 + jnp.log2(safe), MASKED)


def split3(x):
    one = x.astype(jnp.bfloat16).astype(jnp.float32)
    rest = x - one
    two = rest.astype(jnp.bfloat16).astype(jnp.float32)
    return one, two, rest - two


def home_kernel(x_ref, mods_ref, wq_ref, wk_ref, wv_ref, out_ref):
    frames, tokens, _ = x_ref.shape
    rows = []
    for f in range(frames):
        rows.append(normalise(x_ref[f], mods_ref[f, 1:2, :] + 1.0, mods_ref[f, 0:1, :]))
    normed = jnp.concatenate(rows, axis=0)
    half = tokens // 2
    q, k, v = [matmul(normed, w[...]).astype(jnp.bfloat16) for w in (wq_ref, wk_ref, wv_ref)]
    for j in range(2 * FULL):
        f, unit = j // FULL, j % FULL
        r = slice(f * tokens, (f + 1) * tokens)
        own = slice(unit * HEAD_DIM, (unit + 1) * HEAD_DIM)
        pair = FULL + unit // 2
        shared = slice(pair * HEAD_DIM, (pair + 1) * HEAD_DIM)
        out_ref[j, 0:tokens] = q[r, own]
        out_ref[j, tokens : 2 * tokens] = k[r, own]
        out_ref[j, 2 * tokens : 3 * tokens] = v[r, own]
        out_ref[j, 3 * tokens : 4 * tokens] = k[r, shared]
        out_ref[j, 4 * tokens : 5 * tokens] = v[r, shared]
        begin = f * tokens + (unit % 2) * half
        out_ref[j, 5 * tokens : 5 * tokens + half] = q[begin : begin + half, shared]


def spatial_kernel(in_ref, out_ref):
    count = in_ref.shape[0]
    tokens, half = HEAD_DIM, HEAD_DIM // 2

    def part(first, rows):
        return in_ref[:, first : first + rows, :].reshape(count * rows, HEAD_DIM)

    keys, vals = part(tokens, tokens), part(2 * tokens, tokens)
    shared_keys, shared_vals = part(3 * tokens, tokens), part(4 * tokens, tokens)
    lane = lax.broadcasted_iota(jnp.int32, (tokens, HEAD_DIM), 1)
    for s in range(0, count, 2):
        q = in_ref[s : s + 2, 0:tokens, :].reshape(2 * tokens, HEAD_DIM)
        mixed, logs = attend(q, keys, vals)
        q2 = in_ref[s : s + 2, 5 * tokens : 5 * tokens + half, :].reshape(2 * half, HEAD_DIM)
        mixed2, logs2 = attend(q2, shared_keys, shared_vals)
        mixed, mixed2 = mixed.astype(jnp.bfloat16), mixed2.astype(jnp.bfloat16)
        for d in range(2):
            out_ref[s + d, 0:tokens] = mixed[d * tokens : (d + 1) * tokens]
            out_ref[s + d, tokens : tokens + half] = mixed2[d * half : (d + 1) * half]
            stats = jnp.zeros((tokens, HEAD_DIM), jnp.float32)
            for n, piece in enumerate(split3(logs[d * tokens : (d + 1) * tokens])):
                stats = jnp.where(lane == n, piece, stats)
            own = logs2[d * half : (d + 1) * half]
            for n, piece in enumerate(split3(jnp.concatenate([own, own], axis=0))):
                stats = jnp.where(lane == 3 + n, piece, stats)
            turned = jnp.transpose(stats)[0:STAT_ROWS]
            out_ref[s + d, tokens + half : tokens + half + STAT_ROWS] = turned.astype(jnp.bfloat16)


def temporal_kernel(x_ref, scale_ref, shift_ref, bias_ref, wq_ref, wk_ref, wv_ref, out_ref):
    normed = normalise(x_ref[...], scale_ref[...] + 1.0, shift_ref[...])
    q, k, v = [matmul(normed, w[...]).astype(jnp.bfloat16) for w in (wq_ref, wk_ref, wv_ref)]
    bias = bias_ref[...]
    rows = x_ref.shape[0]
    lane = lax.broadcasted_iota(jnp.int32, (rows, HEAD_DIM), 1)
    stats = jnp.zeros((rows, HEAD_DIM), jnp.float32)
    for h in range(HEADS):
        own = slice(h * HEAD_DIM, (h + 1) * HEAD_DIM)
        mixed, logs = attend(q[:, own], k[:, own], v[:, own], bias)
        out_ref[:, own] = mixed.astype(jnp.bfloat16)
        for n, piece in enumerate(split3(logs)):
            stats = jnp.where(lane == 8 * n + h, piece, stats)
    out_ref[:, HEADS * HEAD_DIM :] = stats.astype(jnp.bfloat16)


def merge_kernel(steps_ref, x_ref, gate_ref, space_ref, time_ref, wout_ref, vel_ref, next_ref, first_ref):
    frames, tokens, _ = x_ref.shape
    half = tokens // 2
    width = time_ref.shape[1]
    turned = time_ref[...].astype(jnp.float32).reshape(tokens // 8, 2, 8, width)
    low = lax.broadcasted_iota(jnp.int32, (tokens // 8, 8, width), 1) < 4
    even, odd = turned[:, 0], turned[:, 1]
    by_frame = [
        jnp.where(low, even, pltpu.roll(odd, 4, 1)).reshape(tokens, width),
        jnp.where(low, pltpu.roll(even, 4, 1), odd).reshape(tokens, width),
    ]
    lane = lax.broadcasted_iota(jnp.int32, (1, HEAD_DIM), 1)
    attended = []
    for f in range(frames):
        stats = by_frame[f][:, HEADS * HEAD_DIM :]
        time_log = stats[:, 0:8] + stats[:, 8:16] + stats[:, 16:24]
        log_rows = []
        for h in range(FULL):
            log_rows.append(log_row(space_ref, f * FULL + h, 0))
        for h in range(HEADS - FULL):
            j = f * FULL + 2 * h
            log_rows.append(jnp.where(lane < half, log_row(space_ref, j, 3), log_row(space_ref, j + 1, 3)))
        log_rows.append(jnp.zeros((8 - HEADS, HEAD_DIM), jnp.float32))
        space_log = jnp.transpose(jnp.concatenate(log_rows, axis=0))
        of_space = 1.0 / (1.0 + jnp.exp2(time_log - space_log))
        of_time = 1.0 / (1.0 + jnp.exp2(space_log - time_log))
        parts = []
        for h in range(HEADS):
            if h < FULL:
                near = space_ref[f * FULL + h, 0:tokens]
            else:
                j = f * FULL + 2 * (h - FULL)
                near = jnp.concatenate(
                    [space_ref[j + side, tokens : tokens + half] for side in range(2)], axis=0
                )
            far = by_frame[f][:, h * HEAD_DIM : (h + 1) * HEAD_DIM]
            mixed = of_space[:, h : h + 1] * near.astype(jnp.float32) + of_time[:, h : h + 1] * far
            parts.append(mixed.astype(jnp.bfloat16))
        attended.append(jnp.concatenate(parts, axis=1))
    projected = matmul(jnp.concatenate(attended, axis=0), wout_ref[...])
    for f in range(frames):
        moving = projected[f * tokens : (f + 1) * tokens] * gate_ref[f : f + 1, :]
        vel_ref[f] = moving.astype(jnp.bfloat16)
        advanced = (x_ref[f].astype(jnp.float32) + steps_ref[f] * moving).astype(jnp.bfloat16)
        if f == 0:
            first_ref[...] = advanced
        else:
            next_ref[f - 1] = advanced


def log_row(space_ref, j, first):
    begin = space_ref.shape[1] - STAT_ROWS
    st = space_ref[j, begin : begin + STAT_ROWS].astype(jnp.float32)
    return st[first : first + 1] + st[first + 1 : first + 2] + st[first + 2 : first + 3]


def kernel_call(kernel, out_shapes, flops, nbytes, vmem=32, smem_first=False):
    def call(*args):
        specs = [whole() for _ in args]
        if smem_first:
            specs[0] = pl.BlockSpec(memory_space=pltpu.SMEM)
        single = not isinstance(out_shapes, tuple)
        return pl.pallas_call(
            kernel,
            out_shape=out_shapes,
            in_specs=specs,
            out_specs=whole() if single else tuple(whole() for _ in out_shapes),
            compiler_params=pltpu.CompilerParams(vmem_limit_bytes=vmem * MIB),
            cost_estimate=pl.CostEstimate(flops=flops, bytes_accessed=nbytes, transcendentals=0),
        )(*args)

    return call


def modulation(noise_levels, offset, mod_table, step_sizes):
    total = noise_levels.shape[0]
    frame_ids = jnp.arange(total, dtype=jnp.int32)
    slots = (frame_ids + offset[0]) % total
    slot_hits = slots[:, None] == frame_ids[None, :]
    level_ids = jnp.sum(jnp.where(slot_hits, noise_levels[None, :], 0), axis=1)
    count = mod_table.shape[0]
    one_hot = (level_ids[:, None] == jnp.arange(count, dtype=jnp.int32)[None, :]).astype(jnp.float32)
    mods = jnp.dot(one_hot, mod_table.reshape(count, -1), precision=lax.Precision.HIGHEST)
    steps = jnp.sum(one_hot * step_sizes[None, :], axis=1)
    return mods.reshape(total, 3, -1), steps


def body(
    latents,
    fresh_noise,
    noise_levels,
    offset,
    block_ids,
    mod_table,
    step_sizes,
    w_query,
    w_key,
    w_value,
    w_out,
):
    frames, tokens, width = latents.shape
    times = lax.axis_size("tm")
    share = tokens // times
    total = frames * times
    inner = HEADS * HEAD_DIM
    sds = jax.ShapeDtypeStruct
    bf16 = jnp.bfloat16
    half = tokens // 2

    outgoing = latents.reshape(frames, times, share, width).transpose(1, 0, 2, 3)
    outgoing = outgoing.reshape(times, frames * share, width)
    column = lax.all_to_all(outgoing, "tm", 0, 0)

    mods, steps = modulation(noise_levels, offset, mod_table, step_sizes)
    first_frame = lax.axis_index("tm") * frames
    my_mods = lax.dynamic_slice_in_dim(mods, first_frame, frames)
    my_steps = lax.dynamic_slice_in_dim(steps, first_frame, frames)

    units = kernel_call(
        home_kernel,
        sds((2 * FULL, 5 * tokens + half, HEAD_DIM), bf16),
        2 * frames * tokens * width * 3 * inner,
        10 * MIB,
    )(latents, my_mods, w_query, w_key, w_value)
    units = lax.all_to_all(units, "tok", 0, 0)

    row = jnp.arange(total * share, dtype=jnp.int32)
    row_frame, row_token = row // share, row % share
    row_block = jnp.repeat(block_ids, share)
    allowed = (
        (row_token[:, None] == row_token[None, :])
        & (row_block[None, :] <= row_block[:, None])
        & (row_frame[:, None] != row_frame[None, :])
    )
    bias = jnp.where(allowed, 0.0, MASKED).astype(jnp.float32)
    row_scale = jnp.repeat(mods[:, 1], share, axis=0)
    row_shift = jnp.repeat(mods[:, 0], share, axis=0)

    back = kernel_call(
        temporal_kernel,
        sds((total * share, inner + HEAD_DIM), bf16),
        2 * total * share * width * 3 * inner,
        10 * MIB,
    )(column.reshape(total * share, width), row_scale, row_shift, bias, w_query, w_key, w_value)
    back = lax.all_to_all(back.reshape(times, frames * share, inner + HEAD_DIM), "tm", 0, 0)

    near = kernel_call(
        spatial_kernel,
        sds((2 * FULL, tokens + half + STAT_ROWS, HEAD_DIM), bf16),
        3 * 2 * 1024 * 1024 * HEAD_DIM,
        3 * MIB,
    )(units)
    near = lax.all_to_all(near, "tok", 0, 0)

    velocity, following, first = kernel_call(
        merge_kernel,
        (
            sds((frames, tokens, width), bf16),
            sds((frames, tokens, width), bf16),
            sds((tokens, width), bf16),
        ),
        2 * frames * tokens * width * inner,
        7 * MIB,
        smem_first=True,
    )(
        my_steps,
        latents,
        my_mods[:, 2],
        near,
        back.reshape(times * frames * share, inner + HEAD_DIM),
        w_out,
    )
    received = lax.ppermute(first, "tm", [(i, i - 1) for i in range(1, times)])
    is_last = lax.axis_index("tm") == times - 1
    incoming = jnp.where(is_last, fresh_noise, received)
    return velocity, lax.dynamic_update_slice(following, incoming[None], (frames - 1, 0, 0))


def solution(mesh):
    in_specs = (P("tm", "tok", None), P("tok", None), P(), P(), P(), P(), P(), P(), P(), P(), P())
    out_specs = (P("tm", "tok", None), P("tm", "tok", None))
    return jax.shard_map(body, mesh=mesh, in_specs=in_specs, out_specs=out_specs, check_vma=False)
```

time: 391 us -> 128 us (0.33); the launches traced: 384 us -> 126 us
  waiting for transfers between devices: 259 us -> 50.3 us
  matrix products: 81.9 us -> 0.68 us
  starting transfers between devices: 6.82 us -> 29.1 us
  local copies, waits for them, and re-layouts: 7.24 us -> 26.8 us
  Pallas kernels: 0 us -> 15.7 us
  between operations: 15 us -> 1.6 us
  other arithmetic: 14.1 us -> 1.94 us
    all_gather x4 -> x0, waiting for transfers between devices: 251 us -> none  [the longest x1 116 us: body(): key_piece = lax.all_gather(key_rows, 'tm', axis=0, tiled=True)]
    dot_general x10 -> x1, matrix products: 81.9 us -> 0.68 us  [modulation(): jnp.dot(one_hot, mod_table.reshape(count, -1), precision=lax.Precision.HI...]
    all_to_all x0 -> x4, waiting for transfers between devices: none -> 42 us  [the longest x1 15.6 us: body(): units = lax.all_to_all(units, 'tok', 0, 0)]
    all_to_all x0 -> x4, starting transfers between devices: none -> 26 us  [the longest x1 12.1 us: body(): column = lax.all_to_all(outgoing, 'tm', 0, 0)]
    unnamed x14 -> x38, local copies, waits for them, and re-layouts: 0.91 us -> 17.1 us
    pallas_call x0 -> x4, Pallas kernels: none -> 15.7 us  [call(): pl.pallas_call(kernel, out_shape=out_shapes, in_specs=specs, out_specs=wh...]
    reduce_sum x4 -> x1, other arithmetic: 9.51 us -> 0.09 us  [modulation(): steps = jnp.sum(one_hot * step_sizes[None, :], axis=1)]
  transfers between devices with their start and end apart: 5 -> 5, of which waited for: 5 -> 4; matrix products, arithmetic and copies ran while one was open for 22% -> 8% of each run, Pallas kernels for 0% -> 7%
where the time goes in v1:
time: 128 us; the launch traced here: 126 us
  waiting for transfers between devices  50.3 us (39%)
  starting transfers between devices  29.1 us (23%)
  local copies, waits for them, and re-layouts  26.8 us (21%)
  Pallas kernels  15.7 us (12%)
  other arithmetic  1.94 us (2%)
  between operations  1.6 us (1%)
    unnamed x38, local copies, waits for them, and re-layouts  17.1 us
    pallas_call x4, Pallas kernels, call(): pl.pallas_call(kernel, out_shape=out_shapes, in_specs=specs, out_specs=wh...  15.7 us
    all_to_all x1, waiting for transfers between devices, body(): units = lax.all_to_all(units, 'tok', 0, 0)  15.6 us
    all_to_all x1, waiting for transfers between devices, body(): lax.all_to_all(back.reshape(times, frames * share, inner + HEAD_DIM), 'tm...  14.4 us
    all_to_all x1, starting transfers between devices, body(): column = lax.all_to_all(outgoing, 'tm', 0, 0)  12.1 us
    all_to_all x1, waiting for transfers between devices, body(): column = lax.all_to_all(outgoing, 'tm', 0, 0)  11.9 us
    ppermute x1, waiting for transfers between devices, body(): received = lax.ppermute(first, 'tm', [(i, i - 1) for i in range(1, times)])  8.32 us
    all_to_all x1, starting transfers between devices, body(): lax.all_to_all(back.reshape(times, frames * share, inner + HEAD_DIM), 'tm...  5.4 us
  transfers between devices with their start and end apart: 5, of which 4 were waited for; matrix products, arithmetic and copies ran while one was open for 8% of the time, Pallas kernels for 7%

profile of v1, /device:TPU:5, one launch (start us, length us, event | category | flops | bytes accessed | tf_op | source)
XLA Modules:
  0.0 126.1 jit_solution(3316076083324908509)
XLA Ops:
  0.6 0.0 copy-start
  0.6 0.0 copy-start.7
  1.4 0.8 select_reduce_fusion
  2.3 0.7 fusion
  3.0 1.0 copy-done.15
  4.0 0.0 copy-start.1
  4.0 1.7 %copy-done.1 = bf16[1536,768]{1,0:T(8,128)(2,1)S(1)} copy-done((bf16[1536,768]{1,0:T(8,128)(2,1)S(1)}, bf16[1536,768]{1,0:T(8,128)(2,1)}, u32[]{:S(2)}) %copy-start.1) | copy-done | bytes 2359320
  5.7 1.7 %copy-done.3 = bf16[1536,768]{1,0:T(8,128)(2,1)S(1)} copy-done((bf16[1536,768]{1,0:T(8,128)(2,1)S(1)}, bf16[1536,768]{1,0:T(8,128)(2,1)}, u32[]{:S(2)}) %copy-start.3) | copy-done | bytes 2359320
  7.4 1.7 %copy-done.5 = bf16[1536,768]{1,0:T(8,128)(2,1)S(1)} copy-done((bf16[1536,768]{1,0:T(8,128)(2,1)S(1)}, bf16[1536,768]{1,0:T(8,128)(2,1)}, u32[]{:S(2)}) %copy-start.5) | copy-done | bytes 2359320
  9.0 3.5 %shard_map.122 = bf16[8,704,128]{2,1,0:T(8,128)(2,1)} custom-call(bf16[2,128,1536]{2,1,0:T(8,128)(2,1)S(1)} %copy-done.7, f32[2,3,1536]{2,1,0:T(4,128)S(1)} %copy.21.mods_ref, bf16[1536,768]{1,0:T(8,128)(2,1)S(1)} %copy-done.1, bf16[1536,768]{1,0:T(8,128)(2,1)S(1)} %copy-done.3, bf16[1536,768]{1,0:T(8,128)(2,1)S(1)} %copy-done.5), custom_call_target="tpu_custom_call" | custom-call | flops 1811939328 | bytes 10485760 | tf_op jit(solution)/shard_map/pallas_call | solution.py:190
  12.6 4.8 %all-to-all-start = ((bf16[8,704,128]{2,1,0:T(8,128)(2,1)}), bf16[8,704,128]{2,1,0:T(8,128)(2,1)S(1)}, u32[]{:S(2)}, u32[]{:S(2)}) async-start(bf16[8,704,128]{2,1,0:T(8,128)(2,1)} %shard_map.122), calls=%async_computation | async-start | bytes 2883584 | tf_op jit(solution)/shard_map/all_to_all | solution.py:252
  17.4 1.1 reshape.95
  18.4 1.4 %copy.22 = bf16[32,2,4,1536]{3,2,1,0:T(4,128)(2,1)S(1)} copy(bf16[32,2,4,1536]{3,2,0,1:T(4,128)(2,1)} %bitcast.33) | data formatting | bytes 1572864 | tf_op jit(solution)/shard_map/transpose | solution.py:237
  19.8 1.1 reshape.96
  20.9 15.6 %all-to-all-done.in_ref = bf16[8,704,128]{2,1,0:T(8,128)(2,1)S(1)} async-done(((bf16[8,704,128]{2,1,0:T(8,128)(2,1)}), bf16[8,704,128]{2,1,0:T(8,128)(2,1)S(1)}, u32[]{:S(2)}, u32[]{:S(2)}) %all-to-all-start) | async-done | bytes 1441824 | tf_op jit(solution)/shard_map/all_to_all | solution.py:252
  36.5 12.1 %all-to-all-start.2 = ((bf16[32,8,1536]{2,1,0:T(8,128)(2,1)}), bf16[32,8,1536]{2,1,0:T(8,128)(2,1)}, u32[]{:S(2)}, u32[]{:S(2)}) async-start(bf16[32,8,1536]{2,1,0:T(8,128)(2,1)} %reshape.96), calls=%async_computation.2 | async-start | bytes 1572864 | tf_op jit(solution)/shard_map/all_to_all | solution.py:239
  48.6 1.2 slice_bitcast_fusion
  49.8 0.3 broadcast_in_dim.44
  50.1 1.7 %reshape.98.scale_ref = f32[256,1536]{1,0:T(8,128)} reshape(f32[64,4,1536]{2,1,0:T(4,128)S(1)} %broadcast_in_dim.44) | data formatting | bytes 3145728 | tf_op jit(solution)/shard_map/reshape | solution.py:263
  51.8 0.3 broadcast_in_dim.45
  52.1 0.0 copy-start.17
  52.1 1.7 %reshape.99.shift_ref = f32[256,1536]{1,0:T(8,128)} reshape(f32[64,4,1536]{2,1,0:T(4,128)S(1)} %broadcast_in_dim.45) | data formatting | bytes 3145728 | tf_op jit(solution)/shard_map/reshape | solution.py:264
  53.8 0.1 broadcast_in_dim.46
  53.9 0.1 le.15
  54.0 1.4 %copy-done.13 = bf16[8,704,128]{2,1,0:T(8,128)(2,1)S(1)} copy-done((bf16[8,704,128]{2,1,0:T(8,128)(2,1)S(1)}, bf16[8,704,128]{2,1,0:T(8,128)(2,1)}, u32[]{:S(2)}) %copy-start.13) | copy-done | bytes 1441816
  55.3 3.5 %shard_map.123 = bf16[8,208,128]{2,1,0:T(8,128)(2,1)S(1)} custom-call(bf16[8,704,128]{2,1,0:T(8,128)(2,1)S(1)} %copy-done.13), custom_call_target="tpu_custom_call" | custom-call | flops 805306368 | bytes 3145728 | tf_op jit(solution)/shard_map/pallas_call | solution.py:190
  58.9 0.8 copy-done.14
  59.7 11.9 %all-to-all-done.2 = bf16[32,8,1536]{2,1,0:T(8,128)(2,1)} async-done(((bf16[32,8,1536]{2,1,0:T(8,128)(2,1)}), bf16[32,8,1536]{2,1,0:T(8,128)(2,1)}, u32[]{:S(2)}, u32[]{:S(2)}) %all-to-all-start.2) | async-done | bytes 786464 | tf_op jit(solution)/shard_map/all_to_all | solution.py:239
  71.6 3.6 %all-to-all-start.1 = ((bf16[8,208,128]{2,1,0:T(8,128)(2,1)}), bf16[8,208,128]{2,1,0:T(8,128)(2,1)S(1)}, u32[]{:S(2)}, u32[]{:S(2)}) async-start(bf16[8,208,128]{2,1,0:T(8,128)(2,1)} %copy-done.14), calls=%async_computation.1 | async-start | bytes 851968 | tf_op jit(solution)/shard_map/all_to_all | solution.py:280
  75.2 0.2 and_select_fusion.bias_ref
  75.4 0.0 copy-start.4
  75.4 1.7 %copy-done.4 = bf16[1536,768]{1,0:T(8,128)(2,1)S(1)} copy-done((bf16[1536,768]{1,0:T(8,128)(2,1)S(1)}, bf16[1536,768]{1,0:T(8,128)(2,1)}, u32[]{:S(2)}) %copy-start.4) | copy-done | bytes 2359320
  77.1 1.7 %copy-done.6 = bf16[1536,768]{1,0:T(8,128)(2,1)S(1)} copy-done((bf16[1536,768]{1,0:T(8,128)(2,1)S(1)}, bf16[1536,768]{1,0:T(8,128)(2,1)}, u32[]{:S(2)}) %copy-start.6) | copy-done | bytes 2359320
  78.8 1.4 %copy-done.9 = f32[256,1536]{1,0:T(8,128)S(1)} copy-done((f32[256,1536]{1,0:T(8,128)S(1)}, f32[256,1536]{1,0:T(8,128)}, u32[]{:S(2)}) %copy-start.9) | copy-done | bytes 1572888
  80.2 1.4 %copy-done.10 = f32[256,1536]{1,0:T(8,128)S(1)} copy-done((f32[256,1536]{1,0:T(8,128)S(1)}, f32[256,1536]{1,0:T(8,128)}, u32[]{:S(2)}) %copy-start.10) | copy-done | bytes 1572888
  81.6 5.5 %shard_map.124 = bf16[256,896]{1,0:T(8,128)(2,1)} custom-call(bf16[256,1536]{1,0:T(8,128)(2,1)} %bitcast.5.x_ref, f32[256,1536]{1,0:T(8,128)S(1)} %copy-done.9, f32[256,1536]{1,0:T(8,128)S(1)} %copy-done.10, f32[256,256]{1,0:T(8,128)S(1)} %and_select_fusion.bias_ref, bf16[1536,768]{1,0:T(8,128)(2,1)S(1)} %copy-done.2, bf16[1536,768]{1,0:T(8,128)(2,1)S(1)} %copy-done.4, ...), custom_call_target="tpu_custom_call" | custom-call | flops 1811939328 | bytes 10485760 | tf_op jit(solution)/shard_map/pallas_call | solution.py:190
  87.0 0.0 all-to-all-done.1.space_ref
  87.1 5.4 %all-to-all-start.3 = ((bf16[32,8,896]{2,1,0:T(8,128)(2,1)}), bf16[32,8,896]{2,1,0:T(8,128)(2,1)S(1)}, u32[]{:S(2)}, u32[]{:S(2)}) async-start(bf16[32,8,896]{2,1,0:T(8,128)(2,1)} %bitcast.8), calls=%async_computation.3 | async-start | bytes 917504 | tf_op jit(solution)/shard_map/all_to_all | solution.py:272
  92.5 0.1 select_reduce_fusion.1
  92.6 0.1 dynamic_slice.6.steps_ref
  92.6 0.8 dynamic-slice_bitcast_fusion.gate_ref
  93.4 14.4 %all-to-all-done.3 = bf16[32,8,896]{2,1,0:T(8,128)(2,1)S(1)} async-done(((bf16[32,8,896]{2,1,0:T(8,128)(2,1)}), bf16[32,8,896]{2,1,0:T(8,128)(2,1)S(1)}, u32[]{:S(2)}, u32[]{:S(2)}) %all-to-all-start.3) | async-done | bytes 458784 | tf_op jit(solution)/shard_map/all_to_all | solution.py:272
  107.9 1.1 copy-done.8
  109.0 1.7 %copy-done.11 = bf16[768,1536]{1,0:T(8,128)(2,1)S(1)} copy-done((bf16[768,1536]{1,0:T(8,128)(2,1)S(1)}, bf16[768,1536]{1,0:T(8,128)(2,1)}, u32[]{:S(2)}) %copy-start.11) | copy-done | bytes 2359320
  110.7 3.2 %shard_map.125 = (bf16[2,128,1536]{2,1,0:T(8,128)(2,1)}, bf16[2,128,1536]{2,1,0:T(8,128)(2,1)}, bf16[128,1536]{1,0:T(8,128)(2,1)S(1)}) custom-call(f32[2]{0:T(128)S(1)} %dynamic_slice.6.steps_ref, bf16[2,128,1536]{2,1,0:T(8,128)(2,1)S(1)} %copy-done.8, f32[2,1536]{1,0:T(2,128)S(1)} %dynamic-slice_bitcast_fusion.gate_ref, ...), custom_call_target="tpu_custom_call" | custom-call | flops 603979776 | bytes 7340032 | tf_op jit(solution)/shard_map/pallas_call | solution.py:190
  113.8 3.2 %collective-permute-start = (bf16[128,1536]{1,0:T(8,128)(2,1)S(1)}, bf16[128,1536]{1,0:T(8,128)(2,1)S(1)}, u32[]{:S(2)}, u32[]{:S(2)}) collective-permute-start(bf16[128,1536]{1,0:T(8,128)(2,1)S(1)} %get-tuple-element.7), channel_id=1, source_target_pairs={{8,0},{16,8},{24,16},{32,24},{40,32},{48,40},{56,48},{64,56},{72,6... | collective-permute-start | bytes 1179656 | tf_op jit(solution)/shard_map/ppermute | solution.py:300
  117.0 8.3 %collective-permute-done = bf16[128,1536]{1,0:T(8,128)(2,1)S(1)} collective-permute-done((bf16[128,1536]{1,0:T(8,128)(2,1)S(1)}, bf16[128,1536]{1,0:T(8,128)(2,1)S(1)}, u32[]{:S(2)}, u32[]{:S(2)}) %collective-permute-start) | collective-permute-done | bytes 393248 | tf_op jit(solution)/shard_map/ppermute | solution.py:300
  125.3 0.8 bitcast_dynamic-update-slice_fusion
  (25 shorter events, 0.1 us)
Async XLA Ops:
  0.6 1.6 %copy-start = (f32[32,3,1536]{2,0,1:T(8,128)S(1)}, f32[32,3,1536]{2,0,1:T(8,128)}, u32[]{:S(2)}) copy-start(f32[32,3,1536]{2,0,1:T(8,128)} %param.16) | copy-start | bytes 1769476
  0.6 3.4 %copy-start.7 = (bf16[2,128,1536]{2,1,0:T(8,128)(2,1)S(1)}, bf16[2,128,1536]{2,1,0:T(8,128)(2,1)}, u32[]{:S(2)}) copy-start(bf16[2,128,1536]{2,1,0:T(8,128)(2,1)} %x_ref.3) | copy-start | bytes 2359300
  3.0 1.0 copy-start.15
  4.0 1.7 %copy-start.1 = (bf16[1536,768]{1,0:T(8,128)(2,1)S(1)}, bf16[1536,768]{1,0:T(8,128)(2,1)}, u32[]{:S(2)}) copy-start(bf16[1536,768]{1,0:T(8,128)(2,1)} %wq_ref.3) | copy-start | bytes 7077892
  5.7 1.7 %copy-start.3 = (bf16[1536,768]{1,0:T(8,128)(2,1)S(1)}, bf16[1536,768]{1,0:T(8,128)(2,1)}, u32[]{:S(2)}) copy-start(bf16[1536,768]{1,0:T(8,128)(2,1)} %wk_ref.3) | copy-start | bytes 7077892
  7.4 1.7 %copy-start.5 = (bf16[1536,768]{1,0:T(8,128)(2,1)S(1)}, bf16[1536,768]{1,0:T(8,128)(2,1)}, u32[]{:S(2)}) copy-start(bf16[1536,768]{1,0:T(8,128)(2,1)} %wv_ref.3) | copy-start | bytes 7077892
  12.6 23.9 %all-to-all-start = ((bf16[8,704,128]{2,1,0:T(8,128)(2,1)}), bf16[8,704,128]{2,1,0:T(8,128)(2,1)S(1)}, u32[]{:S(2)}, u32[]{:S(2)}) async-start(bf16[8,704,128]{2,1,0:T(8,128)(2,1)} %shard_map.122), calls=%async_computation | async-start | bytes 2883584 | tf_op jit(solution)/shard_map/all_to_all | solution.py:252
  36.5 13.3 %copy-start.12 = (bf16[8,704,128]{2,1,0:T(8,128)(2,1)}, bf16[8,704,128]{2,1,0:T(8,128)(2,1)S(1)}, u32[]{:S(2)}) copy-start(bf16[8,704,128]{2,1,0:T(8,128)(2,1)S(1)} %all-to-all-done.in_ref) | copy-start | bytes 4325380
  36.5 35.1 %all-to-all-start.2 = ((bf16[32,8,1536]{2,1,0:T(8,128)(2,1)}), bf16[32,8,1536]{2,1,0:T(8,128)(2,1)}, u32[]{:S(2)}, u32[]{:S(2)}) async-start(bf16[32,8,1536]{2,1,0:T(8,128)(2,1)} %reshape.96), calls=%async_computation.2 | async-start | bytes 1572864 | tf_op jit(solution)/shard_map/all_to_all | solution.py:239
  52.1 1.7 %copy-start.17 = (s32[64]{0:T(128)S(1)}, s32[64]{0:T(128)}, u32[]{:S(2)}) copy-start(s32[64]{0:T(128)} %param.15) | copy-start | bytes 772
  54.0 1.4 %copy-start.13 = (bf16[8,704,128]{2,1,0:T(8,128)(2,1)S(1)}, bf16[8,704,128]{2,1,0:T(8,128)(2,1)}, u32[]{:S(2)}) copy-start(bf16[8,704,128]{2,1,0:T(8,128)(2,1)} %copy-done.12) | copy-start | bytes 4325380
  55.3 20.1 %copy-start.2 = (bf16[1536,768]{1,0:T(8,128)(2,1)S(1)}, bf16[1536,768]{1,0:T(8,128)(2,1)}, u32[]{:S(2)}) copy-start(bf16[1536,768]{1,0:T(8,128)(2,1)} %wq_ref.3) | copy-start | bytes 7077892
  58.9 0.8 copy-start.14
  71.6 15.5 %all-to-all-start.1 = ((bf16[8,208,128]{2,1,0:T(8,128)(2,1)}), bf16[8,208,128]{2,1,0:T(8,128)(2,1)S(1)}, u32[]{:S(2)}, u32[]{:S(2)}) async-start(bf16[8,208,128]{2,1,0:T(8,128)(2,1)} %copy-done.14), calls=%async_computation.1 | async-start | bytes 851968 | tf_op jit(solution)/shard_map/all_to_all | solution.py:280
  75.4 1.7 %copy-start.4 = (bf16[1536,768]{1,0:T(8,128)(2,1)S(1)}, bf16[1536,768]{1,0:T(8,128)(2,1)}, u32[]{:S(2)}) copy-start(bf16[1536,768]{1,0:T(8,128)(2,1)} %wk_ref.3) | copy-start | bytes 7077892
  77.1 1.7 %copy-start.6 = (bf16[1536,768]{1,0:T(8,128)(2,1)S(1)}, bf16[1536,768]{1,0:T(8,128)(2,1)}, u32[]{:S(2)}) copy-start(bf16[1536,768]{1,0:T(8,128)(2,1)} %wv_ref.3) | copy-start | bytes 7077892
  78.8 1.4 %copy-start.9 = (f32[256,1536]{1,0:T(8,128)S(1)}, f32[256,1536]{1,0:T(8,128)}, u32[]{:S(2)}) copy-start(f32[256,1536]{1,0:T(8,128)} %reshape.98.scale_ref) | copy-start | bytes 4718596
  80.2 1.4 %copy-start.10 = (f32[256,1536]{1,0:T(8,128)S(1)}, f32[256,1536]{1,0:T(8,128)}, u32[]{:S(2)}) copy-start(f32[256,1536]{1,0:T(8,128)} %reshape.99.shift_ref) | copy-start | bytes 4718596
  81.6 10.9 %copy-start.18 = (f32[32]{0:T(128)S(1)}, f32[32]{0:T(128)}, u32[]{:S(2)}) copy-start(f32[32]{0:T(128)} %param.17) | copy-start | bytes 388
  87.1 20.8 %all-to-all-start.3 = ((bf16[32,8,896]{2,1,0:T(8,128)(2,1)}), bf16[32,8,896]{2,1,0:T(8,128)(2,1)S(1)}, u32[]{:S(2)}, u32[]{:S(2)}) async-start(bf16[32,8,896]{2,1,0:T(8,128)(2,1)} %bitcast.8), calls=%async_computation.3 | async-start | bytes 917504 | tf_op jit(solution)/shard_map/all_to_all | solution.py:272
  107.9 1.1 copy-start.8
  109.0 1.7 %copy-start.11 = (bf16[768,1536]{1,0:T(8,128)(2,1)S(1)}, bf16[768,1536]{1,0:T(8,128)(2,1)}, u32[]{:S(2)}) copy-start(bf16[768,1536]{1,0:T(8,128)(2,1)} %wout_ref.1) | copy-start | bytes 7077892
  110.7 14.6 %copy-start.16 = (bf16[128,1536]{1,0:T(8,128)(2,1)S(1)}, bf16[128,1536]{1,0:T(8,128)(2,1)}, u32[]{:S(2)}) copy-start(bf16[128,1536]{1,0:T(8,128)(2,1)} %param.12) | copy-start | bytes 1179652
  113.8 11.5 %collective-permute-start = (bf16[128,1536]{1,0:T(8,128)(2,1)S(1)}, bf16[128,1536]{1,0:T(8,128)(2,1)S(1)}, u32[]{:S(2)}, u32[]{:S(2)}) collective-permute-start(bf16[128,1536]{1,0:T(8,128)(2,1)S(1)} %get-tuple-element.7), channel_id=1, source_target_pairs={{8,0},{16,8},{24,16},{32,24},{40,32},{48,40},{56,48},{64,56},{72,6... | collective-permute-start | bytes 1179656 | tf_op jit(solution)/shard_map/ppermute | solution.py:300

commit v2 on v0

v2 whole, which is shorter than its diff:
```python
import math

import jax
import jax.numpy as jnp
from jax import lax
from jax.experimental import pallas as pl
from jax.experimental.pallas import tpu as pltpu
from jax.sharding import PartitionSpec as P

HEAD_DIM = 128
HEADS = 6
SPAN = 3
RANKS = 4
BASE2 = HEAD_DIM ** (-0.5) * math.log2(math.e)
MASKED = -1e30
FLOOR = -1e29
MIB = 1 << 20
STAT_ROWS = 16
LONG = 60_000_000_000
BF16 = jnp.bfloat16
F32 = jnp.float32


def normalise(x, scale1, shift):
    values = x.astype(F32)
    center = jnp.mean(values, axis=-1, keepdims=True)
    values = values - center
    spread = jnp.mean(values * values, axis=-1, keepdims=True)
    return (values * lax.rsqrt(spread + 1e-06) * scale1 + shift).astype(BF16)


def matmul(a, b):
    return jnp.dot(a, b, preferred_element_type=F32)


def attend(q, k, v, bias=None):
    scores = lax.dot_general(q, k, (((1,), (1,)), ((), ())), preferred_element_type=F32)
    if bias is not None:
        scores = scores + bias
    top = jnp.max(scores, axis=-1, keepdims=True)
    if bias is not None:
        top = jnp.maximum(top, FLOOR)
    weights = jnp.exp2((scores - top) * BASE2)
    total = jnp.sum(weights, axis=-1, keepdims=True)
    mixed = matmul(weights.astype(BF16), v)
    if bias is None:
        return mixed / total, top * BASE2 + jnp.log2(total)
    some = total > 0.0
    safe = jnp.where(some, total, 1.0)
    return mixed / safe, jnp.where(some, top * BASE2 + jnp.log2(safe), MASKED)


def split3(x):
    one = x.astype(BF16).astype(F32)
    rest = x - one
    two = rest.astype(BF16).astype(F32)
    return one, two, rest - two


def swap_halves(even, odd):
    low = lax.broadcasted_iota(jnp.int32, even.shape, 1) < 4
    return jnp.where(low, even, pltpu.roll(odd, 4, 1)), jnp.where(low, pltpu.roll(even, 4, 1), odd)


def shuffle_kernel(x_hbm, out_hbm, x_ref, mixed_ref, in_sems, out_sems):
    _, tokens, width = x_ref.shape
    chunks = in_sems.shape[0]
    rows = tokens // chunks
    pairs = rows // 8
    ins, outs = [], []
    for c in range(chunks):
        r = pl.ds(c * rows, rows)
        ins.append(pltpu.make_async_copy(x_hbm.at[:, r], x_ref.at[:, r], in_sems.at[c]))
        ins[c].start()
    for c in range(chunks):
        ins[c].wait()
        first, second = [
            x_ref[f, c * rows : (c + 1) * rows].astype(F32).reshape(pairs, 8, width) for f in range(2)
        ]
        even, odd = swap_halves(first, second)
        mixed_ref[c * pairs : (c + 1) * pairs, 0] = even.astype(BF16)
        mixed_ref[c * pairs : (c + 1) * pairs, 1] = odd.astype(BF16)
        r = pl.ds(c * pairs, pairs)
        outs.append(pltpu.make_async_copy(mixed_ref.at[r], out_hbm.at[r], out_sems.at[c]))
        outs[c].start()
    for c in range(chunks):
        outs[c].wait()


def home_kernel(
    noise_ref,
    offset_ref,
    step_ref,
    blocks_ref,
    place_ref,
    x_ref,
    table_hbm,
    wq_hbm,
    wk_hbm,
    wv_hbm,
    size_ref,
    own_hbm,
    shift_hbm,
    scale_hbm,
    bias_hbm,
    *refs,
):
    kv_outs, q_outs = refs[:RANKS], refs[RANKS : 2 * RANKS]
    table_ref, q_ref, k_ref, v_ref, wq_ref, wk_ref, wv_ref, *refs = refs[2 * RANKS :]
    own_ref, shift_ref, scale_ref, bias_ref, sems, out_sems = refs
    loads = [
        pltpu.make_async_copy(src, dst, sems.at[n])
        for n, (src, dst) in enumerate(
            (
                (table_hbm, table_ref),
                (wq_hbm, wq_ref),
                (wk_hbm, wk_ref),
                (wv_hbm, wv_ref),
            )
        )
    ]
    for load in loads:
        load.start()
    frames, tokens, _ = x_ref.shape
    total = noise_ref.shape[0]
    share = bias_ref.shape[0] // total
    place, rank = place_ref[0], place_ref[1]

    wide = (8, total * share)
    lane = lax.broadcasted_iota(jnp.int32, wide, 1)
    block = jnp.zeros(wide, F32)
    for f in range(total):
        block = jnp.where(lane // share == f, blocks_ref[f].astype(F32), block)
    block = jnp.broadcast_to(block[0:1], bias_ref.shape)
    down = lax.broadcasted_iota(jnp.int32, bias_ref.shape, 0)
    along = lax.broadcasted_iota(jnp.int32, bias_ref.shape, 1)
    allowed = (down % share == along % share) & (down != along) & (block <= jnp.transpose(block))
    bias_ref[...] = jnp.where(allowed, 0.0, MASKED)
    stores = [
        pltpu.make_async_copy(src, dst, out_sems.at[n])
        for n, (src, dst) in enumerate(
            (
                (bias_ref, bias_hbm),
                (own_ref, own_hbm),
                (shift_ref, shift_hbm),
                (scale_ref, scale_hbm),
            )
        )
    ]
    stores[0].start()

    def level_of(frame):
        return noise_ref[lax.rem(frame + offset_ref[0], total)]

    loads[0].wait()
    for n in range(frames + 1):
        level = level_of(jnp.minimum(place * frames + n, total - 1))
        size_ref[n] = step_ref[level]
        own_ref[n : n + 1, :] = table_ref[0, pl.ds(level, 1), :]
        own_ref[n + 3 : n + 4, :] = table_ref[1, pl.ds(level, 1), :] + 1.0
        own_ref[n + 6 : n + 7, :] = table_ref[2, pl.ds(level, 1), :]
    stores[1].start()
    rows = []
    for f in range(frames):
        rows.append(normalise(x_ref[f], own_ref[f + 3 : f + 4, :], own_ref[f : f + 1, :]))
    normed = jnp.concatenate(rows, axis=0)
    for n, (ref, w) in enumerate(((q_ref, wq_ref), (k_ref, wk_ref), (v_ref, wv_ref))):
        loads[1 + n].wait()
        ref[...] = matmul(normed, w[...]).astype(BF16)
    for d in range(RANKS):
        other = rank ^ d
        r = pl.ds(pl.multiple_of((other // 2) * tokens, tokens), tokens)
        for u in range(SPAN):
            c = pl.ds(pl.multiple_of((other % 2) * SPAN * HEAD_DIM + u * HEAD_DIM, HEAD_DIM), HEAD_DIM)
            kv_outs[d][u * tokens : (u + 1) * tokens] = k_ref[r, c]
            kv_outs[d][(SPAN + u) * tokens : (SPAN + u + 1) * tokens] = v_ref[r, c]
            q_outs[d][u * tokens : (u + 1) * tokens] = q_ref[r, c]
    for f in range(total):
        level = level_of(f)
        shift_ref[f // frames, f % frames : f % frames + 1, :] = table_ref[0, pl.ds(level, 1), :]
        scale_ref[f // frames, f % frames : f % frames + 1, :] = table_ref[1, pl.ds(level, 1), :] + 1.0
    stores[2].start()
    stores[3].start()
    for store in stores:
        store.wait()


def spatial_kernel(*refs):
    kvs, qs, outs = refs[: 2 * RANKS], refs[2 * RANKS : 3 * RANKS], refs[3 * RANKS :]
    tokens = HEAD_DIM
    lane = lax.broadcasted_iota(jnp.int32, (tokens, HEAD_DIM), 1)
    stats = [jnp.zeros((tokens, HEAD_DIM), F32)] * RANKS
    for u in range(SPAN):
        r = slice(u * tokens, (u + 1) * tokens)
        keys = jnp.concatenate([ref[u * tokens : (u + 1) * tokens] for ref in kvs], axis=0)
        vals = jnp.concatenate([ref[(SPAN + u) * tokens : (SPAN + u + 1) * tokens] for ref in kvs], axis=0)
        for s in range(0, RANKS, 2):
            q = jnp.concatenate([qs[s][r], qs[s + 1][r]], axis=0)
            mixed, logs = attend(q, keys, vals)
            mixed = mixed.astype(BF16)
            for d in range(2):
                half = slice(d * tokens, (d + 1) * tokens)
                outs[s + d][r] = mixed[half]
                for n, piece in enumerate(split3(logs[half])):
                    stats[s + d] = jnp.where(lane == SPAN * u + n, piece, stats[s + d])
    for d in range(RANKS):
        turned = jnp.transpose(stats[d])[0:STAT_ROWS]
        outs[d][SPAN * tokens : SPAN * tokens + STAT_ROWS] = turned.astype(BF16)


def temporal_kernel(x_ref, *refs):
    sources, out_hbm, held, (out_ref, load_sems, sems) = refs[:6], refs[6], refs[7:13], refs[13:]
    loads = []
    for n, (src, dst) in enumerate(zip(sources, held)):
        loads.append(pltpu.make_async_copy(src, dst, load_sems.at[n]))
        loads[n].start()
    scale_ref, shift_ref, wq_ref, wk_ref, wv_ref, bias_ref = held
    groups, rows, width = x_ref.shape
    low = lax.broadcasted_iota(jnp.int32, (groups, rows, width), 1) < rows // 2

    def spread(ref):
        first = jnp.broadcast_to(ref[:, 0:1, :], low.shape)
        return jnp.where(low, first, jnp.broadcast_to(ref[:, 1:2, :], low.shape))

    loads[0].wait()
    loads[1].wait()
    normed = normalise(x_ref[...].astype(F32), spread(scale_ref), spread(shift_ref))
    normed = normed.reshape(groups * rows, width)
    projected = []
    for n, w in enumerate((wq_ref, wk_ref, wv_ref)):
        loads[2 + n].wait()
        projected.append(matmul(normed, w[...]).astype(BF16))
    q, k, v = projected
    loads[5].wait()
    bias = bias_ref[...]
    lane = lax.broadcasted_iota(jnp.int32, (groups * rows, HEAD_DIM), 1)
    stats = jnp.zeros((groups * rows, HEAD_DIM), F32)
    copies = []

    def send(n):
        c = pl.ds(n * HEAD_DIM, HEAD_DIM)
        copies.append(pltpu.make_async_copy(out_ref.at[:, c], out_hbm.at[:, c], sems.at[n]))
        copies[-1].start()

    for h in range(HEADS):
        own = slice(h * HEAD_DIM, (h + 1) * HEAD_DIM)
        mixed, logs = attend(q[:, own], k[:, own], v[:, own], bias)
        out_ref[:, own] = mixed.astype(BF16)
        send(h)
        for n, piece in enumerate(split3(logs)):
            stats = jnp.where(lane == 8 * n + h, piece, stats)
    out_ref[:, HEADS * HEAD_DIM :] = stats.astype(BF16)
    send(HEADS)
    for copy in copies:
        copy.wait()


def merged(f, rank, near_refs, time_ref, space_ref, out_ref):
    for d, ref in enumerate(near_refs):
        space_ref[rank ^ d] = ref[...]
    tokens = out_ref.shape[0]
    width = time_ref.shape[1]
    turned = time_ref[...].astype(F32).reshape(tokens // 8, 2, 8, width)
    far_rows = swap_halves(turned[:, 0], turned[:, 1])[f].reshape(tokens, width)
    stats = far_rows[:, HEADS * HEAD_DIM :]
    time_log = stats[:, 0:8] + stats[:, 8:16] + stats[:, 16:24]
    log_rows = []
    for h in range(HEADS):
        st = space_ref[2 * f + h // SPAN, SPAN * tokens : SPAN * tokens + STAT_ROWS].astype(F32)
        b = SPAN * (h % SPAN)
        log_rows.append(st[b : b + 1] + st[b + 1 : b + 2] + st[b + 2 : b + 3])
    log_rows.append(jnp.zeros((8 - HEADS, HEAD_DIM), F32))
    space_log = jnp.transpose(jnp.concatenate(log_rows, axis=0))
    of_space = 1.0 / (1.0 + jnp.exp2(time_log - space_log))
    of_time = 1.0 / (1.0 + jnp.exp2(space_log - time_log))
    for h in range(HEADS):
        own = slice(h * HEAD_DIM, (h + 1) * HEAD_DIM)
        u = h % SPAN
        near = space_ref[2 * f + h // SPAN, u * tokens : (u + 1) * tokens].astype(F32)
        mixed = of_space[:, h : h + 1] * near + of_time[:, h : h + 1] * far_rows[:, own]
        out_ref[:, own] = mixed.astype(BF16)


def first_kernel(place_ref, *refs):
    near_refs, (time_ref, sent_ref, first_ref, space_ref) = refs[:RANKS], refs[RANKS:]
    merged(0, place_ref[1], near_refs, time_ref, space_ref, first_ref)
    sent_ref[...] = first_ref[...]


def project_kernel(place_ref, size_ref, *refs):
    near_refs = refs[:RANKS]
    time_ref, first_ref, own_hbm, x_hbm, wo_hbm, vel_ref, next_ref, wo_ref = refs[RANKS : RANKS + 8]
    space_ref, second_ref, own_ref, x_ref, sems = refs[RANKS + 8 :]
    frames, tokens, _ = x_ref.shape
    loads = []
    for n, (src, dst) in enumerate(((wo_hbm, wo_ref), (x_hbm, x_ref), (own_hbm, own_ref))):
        loads.append(pltpu.make_async_copy(src, dst, sems.at[n]))
        loads[n].start()

    merged(1, place_ref[1], near_refs, time_ref, space_ref, second_ref)
    attended = jnp.concatenate([first_ref[...], second_ref[...]], axis=0)
    for load in loads:
        load.wait()
    projected = matmul(attended, wo_ref[...])
    for f in range(frames):
        moving = projected[f * tokens : (f + 1) * tokens] * own_ref[6 + f : 7 + f, :]
        vel_ref[f] = moving.astype(BF16)
        if f > 0:
            next_ref[f - 1] = (x_ref[f].astype(F32) + size_ref[f] * moving).astype(BF16)


def last_kernel(
    place_ref,
    size_ref,
    x_ref,
    att_ref,
    wo_ref,
    own_hbm,
    fresh_hbm,
    kept_ref,
    next_ref,
    out_ref,
    own_ref,
    sems,
):
    del kept_ref
    slot = next_ref.shape[0] - 1
    chunks = sems.shape[0]
    width = out_ref.shape[1] // chunks
    at_end = place_ref[0] == place_ref[2]

    @pl.when(at_end)
    def _():
        copy = pltpu.make_async_copy(fresh_hbm, next_ref.at[slot], sems.at[0])
        copy.start()
        copy.wait()

    @pl.when(jnp.logical_not(at_end))
    def _():
        load = pltpu.make_async_copy(own_hbm, own_ref, sems.at[0])
        load.start()
        load.wait()
        copies = []
        for n in range(chunks):
            c = slice(n * width, (n + 1) * width)
            moving = matmul(att_ref[...], wo_ref[:, c]) * own_ref[8:9, c]
            out_ref[:, c] = (x_ref[:, c].astype(F32) + size_ref[2] * moving).astype(BF16)
            d = pl.ds(n * width, width)
            copies.append(pltpu.make_async_copy(out_ref.at[:, d], next_ref.at[slot, :, d], sems.at[n]))
            copies[n].start()
        for copy in copies:
            copy.wait()


def whole():
    return pl.BlockSpec(memory_space=pltpu.VMEM)


def scalar():
    return pl.BlockSpec(memory_space=pltpu.SMEM)


def anywhere():
    return pl.BlockSpec(memory_space=pl.ANY)


def pinned(x):
    return pltpu.with_memory_space_constraint(x, pltpu.VMEM)


def in_hbm(x):
    return pltpu.with_memory_space_constraint(x, pltpu.HBM)


def call(kernel, args, in_specs, outs, out_specs, flops=0, nbytes=0, vmem=20, **more):
    return pl.pallas_call(
        kernel,
        out_shape=outs,
        in_specs=in_specs,
        out_specs=out_specs,
        compiler_params=pltpu.CompilerParams(vmem_limit_bytes=vmem * MIB),
        cost_estimate=pl.CostEstimate(flops=flops, bytes_accessed=nbytes, transcendentals=0),
        **more,
    )(*args)


def body(
    latents,
    fresh_noise,
    noise_levels,
    offset,
    block_ids,
    mod_table,
    step_sizes,
    w_query,
    w_key,
    w_value,
    w_out,
):
    frames, tokens, width = latents.shape
    times = lax.axis_size("tm")
    ranks = lax.axis_size("tok")
    share = tokens // times
    total = frames * times
    inner = HEADS * HEAD_DIM
    sds = jax.ShapeDtypeStruct
    dma = pltpu.SemaphoreType.DMA
    back_perm = [(i, i - 1) for i in range(1, times)]
    project_flops = 2 * frames * tokens * width * inner

    def over_y(x, d):
        return lax.ppermute(x, "tok", [(j, j ^ d) for j in range(ranks)]) if d else x

    def over_x(x):
        return lax.ppermute(x, "tok", [(j, j ^ RANKS) for j in range(ranks)])

    outgoing, x = call(
        shuffle_kernel,
        (in_hbm(latents),),
        [anywhere()],
        (pltpu.HBM((tokens // 8, 2, 8, width), BF16), pltpu.VMEM((frames, tokens, width), BF16)),
        (anywhere(), whole()),
        nbytes=2 * MIB,
        scratch_shapes=[pltpu.VMEM((tokens // 8, 2, 8, width), BF16), dma((4,)), dma((4,))],
    )
    column = lax.all_to_all(outgoing.reshape(times, frames * share, width), "tm", 0, 0)

    small = (
        pltpu.VMEM((16, width), F32),
        pltpu.VMEM((times, frames, width), F32),
        pltpu.VMEM((times, frames, width), F32),
        pltpu.VMEM((total * share, total * share), F32),
    )
    place = lax.axis_index("tm").astype(jnp.int32)
    rank = lax.axis_index("tok").astype(jnp.int32) % RANKS
    place = jnp.stack([place, rank, jnp.int32(times - 1)])
    sizes, own, shifts, scales, bias, *parts = call(
        home_kernel,
        (
            noise_levels,
            offset,
            step_sizes,
            block_ids,
            place,
            pinned(x),
            in_hbm(mod_table.transpose(1, 0, 2)),
            in_hbm(w_query),
            in_hbm(w_key),
            in_hbm(w_value),
        ),
        [scalar()] * 5 + [whole()] + [anywhere()] * 4,
        (
            sds((frames + 1,), F32),
            pltpu.HBM((16, width), F32),
            pltpu.HBM((times, frames, width), F32),
            pltpu.HBM((times, frames, width), F32),
            pltpu.HBM((total * share, total * share), F32),
            *[sds((2 * SPAN * tokens, HEAD_DIM), BF16)] * RANKS,
            *[sds((SPAN * tokens, HEAD_DIM), BF16)] * RANKS,
        ),
        (scalar(), *[anywhere()] * 4, *[whole()] * (2 * RANKS)),
        flops=LONG,
        nbytes=10 * MIB,
        scratch_shapes=[
            pltpu.VMEM((3, mod_table.shape[0], width), F32),
            *[pltpu.VMEM((frames * tokens, inner), BF16)] * 3,
            *[pltpu.VMEM((width, inner), BF16)] * 3,
            *small,
            dma((4,)),
            dma((4,)),
        ],
    )
    kvs, qs = parts[:RANKS], parts[RANKS:]
    near_kvs = [over_y(kv, d) for d, kv in enumerate(kvs)]
    far_kvs = [over_x(kv) for kv in near_kvs]
    qs = [over_y(q, d) for d, q in enumerate(qs)]
    next_latents = lax.ppermute(latents[0], "tm", back_perm)

    back = call(
        temporal_kernel,
        (column, *[in_hbm(a) for a in (scales, shifts, w_query, w_key, w_value, bias)]),
        [whole()] + [anywhere()] * 6,
        pltpu.HBM((total * share, inner + HEAD_DIM), BF16),
        anywhere(),
        flops=LONG,
        nbytes=10 * MIB,
        scratch_shapes=[
            *small[1:3],
            *[pltpu.VMEM((width, inner), BF16)] * 3,
            small[3],
            pltpu.VMEM((total * share, inner + HEAD_DIM), BF16),
            dma((6,)),
            dma((HEADS + 1,)),
        ],
    )
    back = lax.all_to_all(back.reshape(times, frames * share, inner + HEAD_DIM), "tm", 0, 0)
    back = back.reshape(times * frames * share, inner + HEAD_DIM)

    near = call(
        spatial_kernel,
        (*near_kvs, *far_kvs, *qs),
        [whole()] * (3 * RANKS),
        [sds((SPAN * tokens + STAT_ROWS, HEAD_DIM), BF16)] * RANKS,
        [whole()] * RANKS,
        flops=2 * LONG,
        nbytes=3 * MIB,
    )
    near = [over_y(part, d) for d, part in enumerate(near)]

    space = pltpu.VMEM((RANKS, SPAN * tokens + STAT_ROWS, HEAD_DIM), BF16)
    sent, first = call(
        first_kernel,
        (place, *near, back),
        [scalar()] + [whole()] * (RANKS + 1),
        (sds((tokens, inner), BF16), pltpu.VMEM((tokens, inner), BF16)),
        (whole(), whole()),
        nbytes=2 * MIB,
        scratch_shapes=[space],
    )
    next_first = lax.ppermute(sent, "tm", back_perm)
    velocity, following, wo = call(
        project_kernel,
        (place, sizes, *near, back, pinned(first), in_hbm(own), in_hbm(latents), in_hbm(w_out)),
        [scalar()] * 2 + [whole()] * (RANKS + 2) + [anywhere()] * 3,
        (
            sds((frames, tokens, width), BF16),
            sds((frames, tokens, width), BF16),
            pltpu.VMEM((inner, width), BF16),
        ),
        (whole(), whole(), whole()),
        flops=project_flops,
        nbytes=6 * MIB,
        scratch_shapes=[
            space,
            pltpu.VMEM((tokens, inner), BF16),
            small[0],
            pltpu.VMEM((frames, tokens, width), BF16),
            dma((3,)),
        ],
    )
    following = call(
        last_kernel,
        (place, sizes, next_latents, next_first, pinned(wo), in_hbm(own), in_hbm(fresh_noise), following),
        [scalar()] * 2 + [whole()] * 3 + [anywhere()] * 3,
        sds((frames, tokens, width), BF16),
        anywhere(),
        flops=project_flops // 2,
        nbytes=4 * MIB,
        scratch_shapes=[pltpu.VMEM((tokens, width), BF16), small[0], dma((3,))],
        input_output_aliases={7: 0},
    )
    return velocity, following


def solution(mesh):
    in_specs = (P("tm", "tok", None), P("tok", None), P(), P(), P(), P(), P(), P(), P(), P(), P())
    out_specs = (P("tm", "tok", None), P("tm", "tok", None))
    return jax.shard_map(body, mesh=mesh, in_specs=in_specs, out_specs=out_specs, check_vma=False)
```

time: 391 us -> 97.3 us (0.25)
  the two profiles are of different devices: /device:TPU:5 before, /device:TPU:229 now
where the time goes in v2:
time: 97.3 us; the launch traced here: 96.9 us
  starting transfers between devices  40.5 us (42%)
  Pallas kernels  38.8 us (40%)
  waiting for transfers between devices  15.1 us (16%)
  between operations  1.65 us (2%)
    pallas_call x7, Pallas kernels, call(): pl.pallas_call(kernel, out_shape=outs, in_specs=in_specs, out_specs=out_s...  38.8 us
    ppermute x9, waiting for transfers between devices, over_y(): lax.ppermute(x, 'tok', [(j, j ^ d) for j in range(ranks)])  15.1 us
    ppermute x9, starting transfers between devices, over_y(): lax.ppermute(x, 'tok', [(j, j ^ d) for j in range(ranks)])  11.8 us
    all_to_all x1, starting transfers between devices, body(): lax.all_to_all(back.reshape(times, frames * share, inner + HEAD_DIM), 'tm...  11.7 us
    all_to_all x1, starting transfers between devices, body(): lax.all_to_all(outgoing.reshape(times, frames * share, width), 'tm', 0, 0)  8.82 us
    ppermute x4, starting transfers between devices, over_x(): return lax.ppermute(x, 'tok', [(j, j ^ RANKS) for j in range(ranks)])  3.29 us
    ppermute x1, starting transfers between devices, body(): next_first = lax.ppermute(sent, 'tm', back_perm)  2.52 us
    ppermute x1, starting transfers between devices, body(): next_latents = lax.ppermute(latents[0], 'tm', back_perm)  2.29 us
  transfers between devices with their start and end apart: 17, of which 5 were waited for; matrix products, arithmetic and copies ran while one was open for 1% of the time, Pallas kernels for 24%

profile of v2, /device:TPU:229, one launch (start us, length us, event | category | flops | bytes accessed | tf_op | source)
XLA Modules:
  0.0 96.9 jit_solution(3797589899793498872)
XLA Ops:
  0.6 0.0 copy-start.2
  0.6 0.0 copy-start.3
  0.7 0.0 copy-start.4
  0.7 2.0 %shard_map.122 = (bf16[16,2,8,1536]{3,2,1,0:T(8,128)(2,1)}, bf16[2,128,1536]{2,1,0:T(8,128)(2,1)S(1)}) custom-call(bf16[2,128,1536]{2,1,0:T(8,128)(2,1)} %refs_7_.1), custom_call_target="tpu_custom_call" | custom-call | bytes 2097152 | tf_op jit(solution)/shard_map/pallas_call | solution.py:376
  2.7 8.8 %all-to-all-start = ((bf16[32,8,1536]{2,1,0:T(8,128)(2,1)}), bf16[32,8,1536]{2,1,0:T(8,128)(2,1)S(1)}, u32[]{:S(2)}, u32[]{:S(2)}) async-start(bf16[32,8,1536]{2,1,0:T(8,128)(2,1)} %bitcast.10), calls=%async_computation | async-start | bytes 1572864 | tf_op jit(solution)/shard_map/all_to_all | solution.py:426
  12.2 0.1 pad_add_fusion.place_ref
  12.3 0.0 copy-start.5
  12.3 7.2 %shard_map.123 = (f32[3]{0:T(128)S(1)}, f32[16,1536]{1,0:T(8,128)}, f32[32,2,1536]{2,1,0:T(2,128)}, f32[32,2,1536]{2,1,0:T(2,128)}, f32[256,256]{1,0:T(8,128)}, ...) custom-call(s32[64]{0:T(128)S(1)} %copy-done.2, ...), custom_call_target="tpu_custom_call" | custom-call | flops 60000002048 | bytes 10485760 | tf_op jit(solution)/shard_map/pallas_call | solution.py:376
  19.5 1.4 %collective-permute-start = (bf16[768,128]{1,0:T(8,128)(2,1)S(1)}, bf16[768,128]{1,0:T(8,128)(2,1)S(1)}, u32[]{:S(2)}, u32[]{:S(2)}) collective-permute-start(bf16[768,128]{1,0:T(8,128)(2,1)S(1)} %get-tuple-element.29), channel_id=1, source_target_pairs={{0,1},{1,0},{2,3},{3,2},{4,5},{5,4},{6,7},{7,6},{8,9},{9,8},{10,11... | collective-permute-start | bytes 589832 | tf_op jit(solution)/shard_map/ppermute | solution.py:412
  20.9 2.6 %collective-permute-start.1 = (bf16[768,128]{1,0:T(8,128)(2,1)S(1)}, bf16[768,128]{1,0:T(8,128)(2,1)S(1)}, u32[]{:S(2)}, u32[]{:S(2)}) collective-permute-start(bf16[768,128]{1,0:T(8,128)(2,1)S(1)} %get-tuple-element.30), channel_id=1, source_target_pairs={{0,2},{1,3},{2,0},{3,1},{4,6},{5,7},{6,4},{7,5},{8,10},{9,11},{10,... | collective-permute-start | bytes 589832 | tf_op jit(solution)/shard_map/ppermute | solution.py:412
  23.5 0.0 collective-permute-start.2
  23.5 0.0 collective-permute-start.7
  23.6 3.8 %collective-permute-start.8 = (bf16[384,128]{1,0:T(8,128)(2,1)S(1)}, bf16[384,128]{1,0:T(8,128)(2,1)S(1)}, u32[]{:S(2)}, u32[]{:S(2)}) collective-permute-start(bf16[384,128]{1,0:T(8,128)(2,1)S(1)} %get-tuple-element.34), channel_id=1, source_target_pairs={{0,2},{1,3},{2,0},{3,1},{4,6},{5,7},{6,4},{7,5},{8,10},{9,11},{10,... | collective-permute-start | bytes 294920 | tf_op jit(solution)/shard_map/ppermute | solution.py:412
  27.4 0.8 slice_bitcast_fusion
  28.2 3.9 %collective-permute-done.7.refs_9_ = bf16[384,128]{1,0:T(8,128)(2,1)S(1)} collective-permute-done((bf16[384,128]{1,0:T(8,128)(2,1)S(1)}, bf16[384,128]{1,0:T(8,128)(2,1)S(1)}, u32[]{:S(2)}, u32[]{:S(2)}) %collective-permute-start.7) | collective-permute-done | bytes 98336 | tf_op jit(solution)/shard_map/ppermute | solution.py:412
  32.1 0.9 collective-permute-start.3
  33.0 3.6 %collective-permute-done.8.refs_10_ = bf16[384,128]{1,0:T(8,128)(2,1)S(1)} collective-permute-done((bf16[384,128]{1,0:T(8,128)(2,1)S(1)}, bf16[384,128]{1,0:T(8,128)(2,1)S(1)}, u32[]{:S(2)}, u32[]{:S(2)}) %collective-permute-start.8) | collective-permute-done | bytes 98336 | tf_op jit(solution)/shard_map/ppermute | solution.py:412
  36.7 0.0 collective-permute-start.9
  36.7 0.0 collective-permute-done.refs_1_
  36.7 0.9 collective-permute-start.4
  37.6 0.0 collective-permute-done.1.refs_2_
  37.6 0.6 collective-permute-start.5
  38.1 0.0 collective-permute-done.2.refs_3_
  38.1 0.9 collective-permute-start.6
  39.1 0.0 all-to-all-done.x_ref
  39.1 7.2 %shard_map.125 = bf16[256,896]{1,0:T(8,128)(2,1)} custom-call(bf16[32,8,1536]{2,1,0:T(8,128)(2,1)S(1)} %all-to-all-done.x_ref, f32[32,2,1536]{2,1,0:T(2,128)} %get-tuple-element.41.refs_0_, f32[32,2,1536]{2,1,0:T(2,128)} %get-tuple-element.42.refs_1_, bf16[1536,768]{1,0:T(8,128)(2,1)} %refs_2_.1, bf16[1536,768]{1,0:T(8,128)(2,1)} %refs_3_.1, ...), custom_call_target="tpu_custom_call" | custom-call | flops 60000002048 | bytes 10485760 | tf_op jit(solution)/shard_map/pallas_call | solution.py:376
  46.2 11.7 %all-to-all-start.1 = ((bf16[32,8,896]{2,1,0:T(8,128)(2,1)}), bf16[32,8,896]{2,1,0:T(8,128)(2,1)S(1)}, u32[]{:S(2)}, u32[]{:S(2)}) async-start(bf16[32,8,896]{2,1,0:T(8,128)(2,1)} %bitcast.11), calls=%async_computation.1 | async-start | bytes 917504 | tf_op jit(solution)/shard_map/all_to_all | solution.py:496
  58.0 0.0 collective-permute-done.9.refs_11_
  58.0 2.3 %collective-permute-start.13 = (bf16[128,1536]{1,0:T(8,128)(2,1)}, bf16[128,1536]{1,0:T(8,128)(2,1)S(1)}, u32[]{:S(2)}, u32[]{:S(2)}) collective-permute-start(bf16[128,1536]{1,0:T(8,128)(2,1)} %slice_bitcast_fusion), channel_id=1, source_target_pairs={{8,0},{16,8},{24,16},{32,24},{40,32},{48,40},{56,48},{64,56},{72,6... | collective-permute-start | bytes 1179656 | tf_op jit(solution)/shard_map/ppermute | solution.py:477
  60.3 0.0 collective-permute-done.3.refs_4_
  60.3 0.0 collective-permute-done.4.refs_5_
  60.3 0.0 collective-permute-done.5.refs_6_
  60.3 0.0 collective-permute-done.6.refs_7_
  60.3 3.3 %shard_map.124 = (bf16[400,128]{1,0:T(8,128)(2,1)S(1)}, bf16[400,128]{1,0:T(8,128)(2,1)S(1)}, bf16[400,128]{1,0:T(8,128)(2,1)S(1)}, bf16[400,128]{1,0:T(8,128)(2,1)S(1)}) custom-call(bf16[768,128]{1,0:T(8,128)(2,1)S(1)} %get-tuple-element.28.refs_0_, bf16[768,128]{1,0:T(8,128)(2,1)S(1)} %collective-permute-done.refs_1_, ...), custom_call_target="tpu_custom_call" | custom-call | flops 120000004096 | bytes 3145728 | tf_op jit(solution)/shard_map/pallas_call | solution.py:376
  63.6 0.1 collective-permute-start.10
  63.7 3.9 %collective-permute-start.11 = (bf16[400,128]{1,0:T(8,128)(2,1)S(1)}, bf16[400,128]{1,0:T(8,128)(2,1)S(1)}, u32[]{:S(2)}, u32[]{:S(2)}) collective-permute-start(bf16[400,128]{1,0:T(8,128)(2,1)S(1)} %get-tuple-element.38), channel_id=1, source_target_pairs={{0,2},{1,3},{2,0},{3,1},{4,6},{5,7},{6,4},{7,5},{8,10},{9,11},{10,... | collective-permute-start | bytes 307208 | tf_op jit(solution)/shard_map/ppermute | solution.py:412
  67.6 0.0 collective-permute-start.12
  67.6 0.3 collective-permute-done.10.refs_1_
  67.9 4.6 %collective-permute-done.11.refs_2_ = bf16[400,128]{1,0:T(8,128)(2,1)S(1)} collective-permute-done((bf16[400,128]{1,0:T(8,128)(2,1)S(1)}, bf16[400,128]{1,0:T(8,128)(2,1)S(1)}, u32[]{:S(2)}, u32[]{:S(2)}) %collective-permute-start.11) | collective-permute-done | bytes 102432 | tf_op jit(solution)/shard_map/ppermute | solution.py:412
  72.5 2.6 %collective-permute-done.12.refs_3_ = bf16[400,128]{1,0:T(8,128)(2,1)S(1)} collective-permute-done((bf16[400,128]{1,0:T(8,128)(2,1)S(1)}, bf16[400,128]{1,0:T(8,128)(2,1)S(1)}, u32[]{:S(2)}, u32[]{:S(2)}) %collective-permute-start.12) | collective-permute-done | bytes 102432 | tf_op jit(solution)/shard_map/ppermute | solution.py:412
  75.1 0.0 all-to-all-done.1
  75.1 0.0 copy-done.1
  75.1 1.1 %shard_map.126 = (bf16[128,768]{1,0:T(8,128)(2,1)S(1)}, bf16[128,768]{1,0:T(8,128)(2,1)S(1)}) custom-call(s32[3]{0:T(128)S(1)} %copy-done.1, bf16[400,128]{1,0:T(8,128)(2,1)S(1)} %get-tuple-element.36.refs_0_, bf16[400,128]{1,0:T(8,128)(2,1)S(1)} %collective-permute-done.10.refs_1_, bf16[400,128]{1,0:T(8,128)(2,1)S(1)} %collective-permute-done.11.refs_2_, ...), custom_call_target="tpu_custom_call" | custom-call | bytes 2097152 | tf_op jit(solution)/shard_map/pallas_call | solution.py:376
  76.2 2.5 %collective-permute-start.14 = (bf16[128,768]{1,0:T(8,128)(2,1)S(1)}, bf16[128,768]{1,0:T(8,128)(2,1)S(1)}, u32[]{:S(2)}, u32[]{:S(2)}) collective-permute-start(bf16[128,768]{1,0:T(8,128)(2,1)S(1)} %get-tuple-element.47), channel_id=1, source_target_pairs={{8,0},{16,8},{24,16},{32,24},{40,32},{48,40},{56,48},{64,56},{72,6... | collective-permute-start | bytes 589832 | tf_op jit(solution)/shard_map/ppermute | solution.py:520
  78.7 4.4 %shard_map.127 = (bf16[2,128,1536]{2,1,0:T(8,128)(2,1)}, bf16[2,128,1536]{2,1,0:T(8,128)(2,1)}, bf16[768,1536]{1,0:T(8,128)(2,1)S(1)}) custom-call(s32[3]{0:T(128)S(1)} %copy-done.1, f32[3]{0:T(128)S(1)} %get-tuple-element.27.size_ref, bf16[400,128]{1,0:T(8,128)(2,1)S(1)} %get-tuple-element.36.refs_0_, bf16[400,128]{1,0:T(8,128)(2,1)S(1)} %collective-permute-done.10.refs_1_, ...), custom_call_target="tpu_custom_call" | custom-call | flops 603979776 | bytes 6291456 | tf_op jit(solution)/shard_map/pallas_call | solution.py:376
  83.1 0.0 collective-permute-done.13.x_ref
  83.1 0.0 collective-permute-done.14.att_ref
  83.2 13.6 %shard_map.128 = bf16[2,128,1536]{2,1,0:T(8,128)(2,1)} custom-call(s32[3]{0:T(128)S(1)} %copy-done.1, f32[3]{0:T(128)S(1)} %get-tuple-element.27.size_ref, bf16[128,1536]{1,0:T(8,128)(2,1)S(1)} %collective-permute-done.13.x_ref, bf16[128,768]{1,0:T(8,128)(2,1)S(1)} %collective-permute-done.14.att_ref, ...), custom_call_target="tpu_custom_call", output_to_operand_aliasing={{}: (7, {})} | custom-call | flops 301989888 | bytes 4194304 | tf_op jit(solution)/shard_map/pallas_call | solution.py:376
  (7 shorter events, 0.0 us)
Async XLA Ops:
  0.6 11.6 %copy-start.2 = (s32[64]{0:T(128)S(1)}, s32[64]{0:T(128)}, u32[]{:S(2)}) copy-start(s32[64]{0:T(128)} %noise_ref.1) | copy-start | bytes 772
  0.6 11.6 %copy-start.3 = (f32[32]{0:T(128)S(1)}, f32[32]{0:T(128)}, u32[]{:S(2)}) copy-start(f32[32]{0:T(128)} %step_ref.1) | copy-start | bytes 388
  0.7 11.6 %copy-start.4 = (s32[64]{0:T(128)S(1)}, s32[64]{0:T(128)}, u32[]{:S(2)}) copy-start(s32[64]{0:T(128)} %blocks_ref.1) | copy-start | bytes 772
  2.7 36.4 %all-to-all-start = ((bf16[32,8,1536]{2,1,0:T(8,128)(2,1)}), bf16[32,8,1536]{2,1,0:T(8,128)(2,1)S(1)}, u32[]{:S(2)}, u32[]{:S(2)}) async-start(bf16[32,8,1536]{2,1,0:T(8,128)(2,1)} %bitcast.10), calls=%async_computation | async-start | bytes 1572864 | tf_op jit(solution)/shard_map/all_to_all | solution.py:426
  12.3 7.3 %copy-start = (s32[3]{0:T(128)}, s32[3]{0:T(128)S(1)}, u32[]{:S(2)}) copy-start(s32[3]{0:T(128)S(1)} %pad_add_fusion.place_ref) | copy-start | bytes 40
  12.3 15.1 %copy-start.5 = (bf16[2,128,1536]{2,1,0:T(8,128)(2,1)S(1)}, bf16[2,128,1536]{2,1,0:T(8,128)(2,1)}, u32[]{:S(2)}) copy-start(bf16[2,128,1536]{2,1,0:T(8,128)(2,1)} %refs_7_.1) | copy-start | bytes 2359300
  19.5 17.1 %collective-permute-start = (bf16[768,128]{1,0:T(8,128)(2,1)S(1)}, bf16[768,128]{1,0:T(8,128)(2,1)S(1)}, u32[]{:S(2)}, u32[]{:S(2)}) collective-permute-start(bf16[768,128]{1,0:T(8,128)(2,1)S(1)} %get-tuple-element.29), channel_id=1, source_target_pairs={{0,1},{1,0},{2,3},{3,2},{4,5},{5,4},{6,7},{7,6},{8,9},{9,8},{10,11... | collective-permute-start | bytes 589832 | tf_op jit(solution)/shard_map/ppermute | solution.py:412
  20.9 16.7 %collective-permute-start.1 = (bf16[768,128]{1,0:T(8,128)(2,1)S(1)}, bf16[768,128]{1,0:T(8,128)(2,1)S(1)}, u32[]{:S(2)}, u32[]{:S(2)}) collective-permute-start(bf16[768,128]{1,0:T(8,128)(2,1)S(1)} %get-tuple-element.30), channel_id=1, source_target_pairs={{0,2},{1,3},{2,0},{3,1},{4,6},{5,7},{6,4},{7,5},{8,10},{9,11},{10,... | collective-permute-start | bytes 589832 | tf_op jit(solution)/shard_map/ppermute | solution.py:412
  23.5 14.6 %collective-permute-start.2 = (bf16[768,128]{1,0:T(8,128)(2,1)S(1)}, bf16[768,128]{1,0:T(8,128)(2,1)S(1)}, u32[]{:S(2)}, u32[]{:S(2)}) collective-permute-start(bf16[768,128]{1,0:T(8,128)(2,1)S(1)} %get-tuple-element.31), channel_id=1, source_target_pairs={{0,3},{1,2},{2,1},{3,0},{4,7},{5,6},{6,5},{7,4},{8,11},{9,10},{10,... | collective-permute-start | bytes 589832 | tf_op jit(solution)/shard_map/ppermute | solution.py:412
  23.5 8.6 %collective-permute-start.7 = (bf16[384,128]{1,0:T(8,128)(2,1)S(1)}, bf16[384,128]{1,0:T(8,128)(2,1)S(1)}, u32[]{:S(2)}, u32[]{:S(2)}) collective-permute-start(bf16[384,128]{1,0:T(8,128)(2,1)S(1)} %get-tuple-element.33), channel_id=1, source_target_pairs={{0,1},{1,0},{2,3},{3,2},{4,5},{5,4},{6,7},{7,6},{8,9},{9,8},{10,11... | collective-permute-start | bytes 294920 | tf_op jit(solution)/shard_map/ppermute | solution.py:412
  23.6 13.1 %collective-permute-start.8 = (bf16[384,128]{1,0:T(8,128)(2,1)S(1)}, bf16[384,128]{1,0:T(8,128)(2,1)S(1)}, u32[]{:S(2)}, u32[]{:S(2)}) collective-permute-start(bf16[384,128]{1,0:T(8,128)(2,1)S(1)} %get-tuple-element.34), channel_id=1, source_target_pairs={{0,2},{1,3},{2,0},{3,1},{4,6},{5,7},{6,4},{7,5},{8,10},{9,11},{10,... | collective-permute-start | bytes 294920 | tf_op jit(solution)/shard_map/ppermute | solution.py:412
  32.1 28.2 %collective-permute-start.3 = (bf16[768,128]{1,0:T(8,128)(2,1)S(1)}, bf16[768,128]{1,0:T(8,128)(2,1)S(1)}, u32[]{:S(2)}, u32[]{:S(2)}) collective-permute-start(bf16[768,128]{1,0:T(8,128)(2,1)S(1)} %get-tuple-element.28.refs_0_), channel_id=1, source_target_pairs={{0,4},{1,5},{2,6},{3,7},{4,0},{5,1},{6,2},{7,3},{8,12},{9,13},{10,... | collective-permute-start | bytes 589832 | tf_op jit(solution)/shard_map/ppermute | solution.py:415
  36.7 21.3 %collective-permute-start.9 = (bf16[384,128]{1,0:T(8,128)(2,1)S(1)}, bf16[384,128]{1,0:T(8,128)(2,1)S(1)}, u32[]{:S(2)}, u32[]{:S(2)}) collective-permute-start(bf16[384,128]{1,0:T(8,128)(2,1)S(1)} %get-tuple-element.35), channel_id=1, source_target_pairs={{0,3},{1,2},{2,1},{3,0},{4,7},{5,6},{6,5},{7,4},{8,11},{9,10},{10,... | collective-permute-start | bytes 294920 | tf_op jit(solution)/shard_map/ppermute | solution.py:412
  36.7 23.6 %collective-permute-start.4 = (bf16[768,128]{1,0:T(8,128)(2,1)S(1)}, bf16[768,128]{1,0:T(8,128)(2,1)S(1)}, u32[]{:S(2)}, u32[]{:S(2)}) collective-permute-start(bf16[768,128]{1,0:T(8,128)(2,1)S(1)} %collective-permute-done.refs_1_), channel_id=1, source_target_pairs={{0,4},{1,5},{2,6},{3,7},{4,0},{5,1},{6,2},{7,3},{8,12},{9,13},{10,... | collective-permute-start | bytes 589832 | tf_op jit(solution)/shard_map/ppermute | solution.py:415
  37.6 22.7 %collective-permute-start.5 = (bf16[768,128]{1,0:T(8,128)(2,1)S(1)}, bf16[768,128]{1,0:T(8,128)(2,1)S(1)}, u32[]{:S(2)}, u32[]{:S(2)}) collective-permute-start(bf16[768,128]{1,0:T(8,128)(2,1)S(1)} %collective-permute-done.1.refs_2_), channel_id=1, source_target_pairs={{0,4},{1,5},{2,6},{3,7},{4,0},{5,1},{6,2},{7,3},{8,12},{9,13},{10,... | collective-permute-start | bytes 589832 | tf_op jit(solution)/shard_map/ppermute | solution.py:415
  38.1 22.2 %collective-permute-start.6 = (bf16[768,128]{1,0:T(8,128)(2,1)S(1)}, bf16[768,128]{1,0:T(8,128)(2,1)S(1)}, u32[]{:S(2)}, u32[]{:S(2)}) collective-permute-start(bf16[768,128]{1,0:T(8,128)(2,1)S(1)} %collective-permute-done.2.refs_3_), channel_id=1, source_target_pairs={{0,4},{1,5},{2,6},{3,7},{4,0},{5,1},{6,2},{7,3},{8,12},{9,13},{10,... | collective-permute-start | bytes 589832 | tf_op jit(solution)/shard_map/ppermute | solution.py:415
  46.2 28.9 %all-to-all-start.1 = ((bf16[32,8,896]{2,1,0:T(8,128)(2,1)}), bf16[32,8,896]{2,1,0:T(8,128)(2,1)S(1)}, u32[]{:S(2)}, u32[]{:S(2)}) async-start(bf16[32,8,896]{2,1,0:T(8,128)(2,1)} %bitcast.11), calls=%async_computation.1 | async-start | bytes 917504 | tf_op jit(solution)/shard_map/all_to_all | solution.py:496
  58.0 25.2 %collective-permute-start.13 = (bf16[128,1536]{1,0:T(8,128)(2,1)}, bf16[128,1536]{1,0:T(8,128)(2,1)S(1)}, u32[]{:S(2)}, u32[]{:S(2)}) collective-permute-start(bf16[128,1536]{1,0:T(8,128)(2,1)} %slice_bitcast_fusion), channel_id=1, source_target_pairs={{8,0},{16,8},{24,16},{32,24},{40,32},{48,40},{56,48},{64,56},{72,6... | collective-permute-start | bytes 1179656 | tf_op jit(solution)/shard_map/ppermute | solution.py:477
  60.3 14.8 %copy-start.1 = (s32[3]{0:T(128)S(1)}, s32[3]{0:T(128)}, u32[]{:S(2)}) copy-start(s32[3]{0:T(128)} %copy-done) | copy-start | bytes 40
  63.6 4.3 %collective-permute-start.10 = (bf16[400,128]{1,0:T(8,128)(2,1)S(1)}, bf16[400,128]{1,0:T(8,128)(2,1)S(1)}, u32[]{:S(2)}, u32[]{:S(2)}) collective-permute-start(bf16[400,128]{1,0:T(8,128)(2,1)S(1)} %get-tuple-element.37), channel_id=1, source_target_pairs={{0,1},{1,0},{2,3},{3,2},{4,5},{5,4},{6,7},{7,6},{8,9},{9,8},{10,11... | collective-permute-start | bytes 307208 | tf_op jit(solution)/shard_map/ppermute | solution.py:412
  63.7 8.8 %collective-permute-start.11 = (bf16[400,128]{1,0:T(8,128)(2,1)S(1)}, bf16[400,128]{1,0:T(8,128)(2,1)S(1)}, u32[]{:S(2)}, u32[]{:S(2)}) collective-permute-start(bf16[400,128]{1,0:T(8,128)(2,1)S(1)} %get-tuple-element.38), channel_id=1, source_target_pairs={{0,2},{1,3},{2,0},{3,1},{4,6},{5,7},{6,4},{7,5},{8,10},{9,11},{10,... | collective-permute-start | bytes 307208 | tf_op jit(solution)/shard_map/ppermute | solution.py:412
  67.6 7.5 %collective-permute-start.12 = (bf16[400,128]{1,0:T(8,128)(2,1)S(1)}, bf16[400,128]{1,0:T(8,128)(2,1)S(1)}, u32[]{:S(2)}, u32[]{:S(2)}) collective-permute-start(bf16[400,128]{1,0:T(8,128)(2,1)S(1)} %get-tuple-element.39), channel_id=1, source_target_pairs={{0,3},{1,2},{2,1},{3,0},{4,7},{5,6},{6,5},{7,4},{8,11},{9,10},{10,... | collective-permute-start | bytes 307208 | tf_op jit(solution)/shard_map/ppermute | solution.py:412
  76.2 7.0 %collective-permute-start.14 = (bf16[128,768]{1,0:T(8,128)(2,1)S(1)}, bf16[128,768]{1,0:T(8,128)(2,1)S(1)}, u32[]{:S(2)}, u32[]{:S(2)}) collective-permute-start(bf16[128,768]{1,0:T(8,128)(2,1)S(1)} %get-tuple-element.47), channel_id=1, source_target_pairs={{8,0},{16,8},{24,16},{32,24},{40,32},{48,40},{56,48},{64,56},{72,6... | collective-permute-start | bytes 589832 | tf_op jit(solution)/shard_map/ppermute | solution.py:520

commit v3 on v2

v3 whole, which is shorter than its diff:
```python
import math

import jax
import jax.numpy as jnp
from jax import lax
from jax.experimental import pallas as pl
from jax.experimental.pallas import tpu as pltpu
from jax.sharding import PartitionSpec as P

HEAD_DIM = 128
HEADS = 6
SPAN = 3
RANKS = 4
BASE2 = HEAD_DIM ** (-0.5) * math.log2(math.e)
MASKED = -1e30
FLOOR = -1e29
MIB = 1 << 20
STAT_ROWS = 16
LONG = 60_000_000_000
BF16 = jnp.bfloat16
F32 = jnp.float32


def normalise(x, scale1, shift):
    values = x.astype(F32)
    center = jnp.mean(values, axis=-1, keepdims=True)
    values = values - center
    spread = jnp.mean(values * values, axis=-1, keepdims=True)
    return (values * lax.rsqrt(spread + 1e-06) * scale1 + shift).astype(BF16)


def matmul(a, b):
    return jnp.dot(a, b, preferred_element_type=F32)


def softmax_parts(q, k, bias=None):
    scores = lax.dot_general(q, k, (((1,), (1,)), ((), ())), preferred_element_type=F32)
    if bias is not None:
        scores = scores + bias
    top = jnp.max(scores, axis=-1, keepdims=True)
    if bias is not None:
        top = jnp.maximum(top, FLOOR)
    weights = jnp.exp2((scores - top) * BASE2)
    return weights.astype(BF16), jnp.sum(weights, axis=-1, keepdims=True), top


def finish(weights, total, top, v, may_be_empty):
    mixed = matmul(weights, v)
    if not may_be_empty:
        return mixed / total, top * BASE2 + jnp.log2(total)
    some = total > 0.0
    safe = jnp.where(some, total, 1.0)
    return mixed / safe, jnp.where(some, top * BASE2 + jnp.log2(safe), MASKED)


def attend(q, k, v):
    return finish(*softmax_parts(q, k), v, False)


def split3(x):
    one = x.astype(BF16).astype(F32)
    rest = x - one
    two = rest.astype(BF16).astype(F32)
    return one, two, rest - two


def swap_halves(even, odd):
    low = lax.broadcasted_iota(jnp.int32, even.shape, 1) < 4
    return jnp.where(low, even, pltpu.roll(odd, 4, 1)), jnp.where(low, pltpu.roll(even, 4, 1), odd)


def shuffle_kernel(x_hbm, out_hbm, x_ref, mixed_ref, in_sems, out_sems):
    _, tokens, width = x_ref.shape
    chunks = in_sems.shape[0]
    rows = tokens // chunks
    pairs = rows // 8
    ins, outs = [], []
    for c in range(chunks):
        r = pl.ds(c * rows, rows)
        ins.append(pltpu.make_async_copy(x_hbm.at[:, r], x_ref.at[:, r], in_sems.at[c]))
        ins[c].start()
    for c in range(chunks):
        ins[c].wait()
        first, second = [
            x_ref[f, c * rows : (c + 1) * rows].astype(F32).reshape(pairs, 8, width) for f in range(2)
        ]
        even, odd = swap_halves(first, second)
        mixed_ref[c * pairs : (c + 1) * pairs, 0] = even.astype(BF16)
        mixed_ref[c * pairs : (c + 1) * pairs, 1] = odd.astype(BF16)
        r = pl.ds(c * pairs, pairs)
        outs.append(pltpu.make_async_copy(mixed_ref.at[r], out_hbm.at[r], out_sems.at[c]))
        outs[c].start()
    for c in range(chunks):
        outs[c].wait()


def home_kernel(
    noise_ref, offset_ref, step_ref, place_ref, x_ref, table_hbm, wq_hbm, wk_hbm, wv_hbm, size_ref, own_hbm, *refs
):
    outs = refs[:RANKS]
    table_ref, q_ref, k_ref, v_ref, wq_ref, wk_ref, wv_ref, own_ref, sems, own_sem = refs[RANKS:]
    loads = []
    for n, (src, dst) in enumerate(
        ((table_hbm, table_ref), (wq_hbm, wq_ref), (wk_hbm, wk_ref), (wv_hbm, wv_ref))
    ):
        loads.append(pltpu.make_async_copy(src, dst, sems.at[n]))
        loads[n].start()
    frames, tokens, _ = x_ref.shape
    total = noise_ref.shape[0]
    loads[0].wait()
    for n in range(frames + 1):
        frame = jnp.minimum(place_ref[0] * frames + n, total - 1)
        level = noise_ref[lax.rem(frame + offset_ref[0], total)]
        size_ref[n] = step_ref[level]
        own_ref[n : n + 1, :] = table_ref[0, pl.ds(level, 1), :]
        own_ref[n + 3 : n + 4, :] = table_ref[1, pl.ds(level, 1), :] + 1.0
        own_ref[n + 6 : n + 7, :] = table_ref[2, pl.ds(level, 1), :]
    own_store = pltpu.make_async_copy(own_ref, own_hbm, own_sem)
    own_store.start()
    normed = []
    for f in range(frames):
        normed.append(normalise(x_ref[f], own_ref[f + 3 : f + 4, :], own_ref[f : f + 1, :]))
    normed = jnp.concatenate(normed, axis=0)
    for n, (ref, w) in enumerate(((q_ref, wq_ref), (k_ref, wk_ref), (v_ref, wv_ref))):
        loads[1 + n].wait()
        ref[...] = matmul(normed, w[...]).astype(BF16)
    for d in range(RANKS):
        other = place_ref[1] ^ d
        r = pl.ds(pl.multiple_of((other // 2) * tokens, tokens), tokens)
        for u in range(SPAN):
            c = pl.ds(pl.multiple_of((other % 2) * SPAN * HEAD_DIM + u * HEAD_DIM, HEAD_DIM), HEAD_DIM)
            for n, ref in enumerate((k_ref, v_ref, q_ref)):
                block = slice((n * SPAN + u) * tokens, (n * SPAN + u + 1) * tokens)
                outs[d][block] = ref[r, c]
    own_store.wait()


def column_kernel(noise_ref, offset_ref, blocks_ref, table_ref, shift_hbm, scale_hbm, bias_hbm, *refs):
    shift_ref, scale_ref, bias_ref, sems = refs
    total = noise_ref.shape[0]
    frames = shift_ref.shape[1]
    share = bias_ref.shape[0] // total
    stores = [
        pltpu.make_async_copy(src, dst, sems.at[n])
        for n, (src, dst) in enumerate(
            ((shift_ref, shift_hbm), (scale_ref, scale_hbm), (bias_ref, bias_hbm))
        )
    ]
    for f in range(total):
        level = noise_ref[lax.rem(f + offset_ref[0], total)]
        shift_ref[f // frames, f % frames : f % frames + 1, :] = table_ref[0, pl.ds(level, 1), :]
        scale_ref[f // frames, f % frames : f % frames + 1, :] = table_ref[1, pl.ds(level, 1), :] + 1.0
    stores[0].start()
    stores[1].start()
    wide = (8, total * share)
    lane = lax.broadcasted_iota(jnp.int32, wide, 1) // share
    block = jnp.zeros(wide, F32)
    for f in range(total):
        block = jnp.where(lane == f, blocks_ref[f].astype(F32), block)
    block = jnp.broadcast_to(block[0:1], bias_ref.shape)
    down = lax.broadcasted_iota(jnp.int32, bias_ref.shape, 0)
    along = lax.broadcasted_iota(jnp.int32, bias_ref.shape, 1)
    allowed = (down % share == along % share) & (down != along) & (block <= jnp.transpose(block))
    bias_ref[...] = jnp.where(allowed, 0.0, MASKED)
    stores[2].start()
    for store in stores:
        store.wait()


def spatial_kernel(*refs):
    kvs, qs, outs = refs[: 2 * RANKS], refs[:RANKS], refs[2 * RANKS :]
    tokens = HEAD_DIM
    lane = lax.broadcasted_iota(jnp.int32, (tokens, HEAD_DIM), 1)
    stats = [jnp.zeros((tokens, HEAD_DIM), F32)] * RANKS
    for u in range(SPAN):
        r = slice(u * tokens, (u + 1) * tokens)
        block = slice((2 * SPAN + u) * tokens, (2 * SPAN + u + 1) * tokens)
        keys = jnp.concatenate([ref[u * tokens : (u + 1) * tokens] for ref in kvs], axis=0)
        vals = jnp.concatenate([ref[(SPAN + u) * tokens : (SPAN + u + 1) * tokens] for ref in kvs], axis=0)
        for s in range(0, RANKS, 2):
            q = jnp.concatenate([qs[s][block], qs[s + 1][block]], axis=0)
            mixed, logs = attend(q, keys, vals)
            mixed = mixed.astype(BF16)
            for d in range(2):
                half = slice(d * tokens, (d + 1) * tokens)
                outs[s + d][r] = mixed[half]
                for n, piece in enumerate(split3(logs[half])):
                    stats[s + d] = jnp.where(lane == SPAN * u + n, piece, stats[s + d])
    for d in range(RANKS):
        turned = jnp.transpose(stats[d])[0:STAT_ROWS]
        outs[d][SPAN * tokens : SPAN * tokens + STAT_ROWS] = turned.astype(BF16)


def temporal_kernel(x_ref, *refs):
    scale_hbm, shift_hbm, wq_hbm, wk_hbm, bias_hbm, wv_hbm, out_hbm = refs[:7]
    scale_ref, shift_ref, wq_ref, wk_ref, bias_ref, wv_ref, out_ref, sems, out_sems = refs[7:]
    held = (scale_ref, shift_ref, wq_ref, wk_ref, bias_ref, wv_ref)
    loads = []
    for n, (src, dst) in enumerate(zip(refs[:6], held)):
        loads.append(pltpu.make_async_copy(src, dst, sems.at[n]))
        loads[n].start()
    groups, rows, width = x_ref.shape
    low = lax.broadcasted_iota(jnp.int32, (groups, rows, width), 1) < rows // 2

    def spread(ref):
        first = jnp.broadcast_to(ref[:, 0:1, :], low.shape)
        return jnp.where(low, first, jnp.broadcast_to(ref[:, 1:2, :], low.shape))

    loads[0].wait()
    loads[1].wait()
    normed = normalise(x_ref[...].astype(F32), spread(scale_ref), spread(shift_ref))
    normed = normed.reshape(groups * rows, width)
    loads[2].wait()
    q = matmul(normed, wq_ref[...]).astype(BF16)
    loads[3].wait()
    k = matmul(normed, wk_ref[...]).astype(BF16)
    loads[4].wait()
    lane = lax.broadcasted_iota(jnp.int32, (groups * rows, HEAD_DIM), 1)
    stats = jnp.zeros((groups * rows, HEAD_DIM), F32)
    heads = [slice(h * HEAD_DIM, (h + 1) * HEAD_DIM) for h in range(HEADS)]
    parts = [softmax_parts(q[:, own], k[:, own], bias_ref[...]) for own in heads]
    loads[5].wait()
    v = matmul(normed, wv_ref[...]).astype(BF16)
    copies = []

    def send(n):
        c = pl.ds(n * HEAD_DIM, HEAD_DIM)
        copies.append(pltpu.make_async_copy(out_ref.at[:, c], out_hbm.at[:, c], out_sems.at[n]))
        copies[n].start()

    for h, (own, (weights, total, top)) in enumerate(zip(heads, parts)):
        mixed, logs = finish(weights, total, top, v[:, own], True)
        out_ref[:, own] = mixed.astype(BF16)
        send(h)
        for m, piece in enumerate(split3(logs)):
            stats = jnp.where(lane == 8 * m + h, piece, stats)
    out_ref[:, HEADS * HEAD_DIM :] = stats.astype(BF16)
    send(HEADS)
    for copy in copies:
        copy.wait()


def merged(f, rank, near_refs, time_ref, space_ref, out_ref):
    for d, ref in enumerate(near_refs):
        space_ref[rank ^ d] = ref[...]
    tokens = out_ref.shape[0]
    width = time_ref.shape[1]
    turned = time_ref[...].astype(F32).reshape(tokens // 8, 2, 8, width)
    far_rows = swap_halves(turned[:, 0], turned[:, 1])[f].reshape(tokens, width)
    stats = far_rows[:, HEADS * HEAD_DIM :]
    time_log = stats[:, 0:8] + stats[:, 8:16] + stats[:, 16:24]
    log_rows = []
    for h in range(HEADS):
        st = space_ref[2 * f + h // SPAN, SPAN * tokens : SPAN * tokens + STAT_ROWS].astype(F32)
        b = SPAN * (h % SPAN)
        log_rows.append(st[b : b + 1] + st[b + 1 : b + 2] + st[b + 2 : b + 3])
    log_rows.append(jnp.zeros((8 - HEADS, HEAD_DIM), F32))
    space_log = jnp.transpose(jnp.concatenate(log_rows, axis=0))
    of_space = 1.0 / (1.0 + jnp.exp2(time_log - space_log))
    of_time = 1.0 / (1.0 + jnp.exp2(space_log - time_log))
    for h in range(HEADS):
        own = slice(h * HEAD_DIM, (h + 1) * HEAD_DIM)
        u = h % SPAN
        near = space_ref[2 * f + h // SPAN, u * tokens : (u + 1) * tokens].astype(F32)
        mixed = of_space[:, h : h + 1] * near + of_time[:, h : h + 1] * far_rows[:, own]
        out_ref[:, own] = mixed.astype(BF16)


def first_kernel(place_ref, *refs):
    near_refs, (time_ref, sent_ref, first_ref, space_ref) = refs[:RANKS], refs[RANKS:]
    merged(0, place_ref[1], near_refs, time_ref, space_ref, first_ref)
    sent_ref[...] = first_ref[...]


def project_kernel(place_ref, size_ref, *refs):
    near_refs = refs[:RANKS]
    time_ref, first_ref, wo_hbm, own_hbm, x_hbm, fresh_hbm, in_hbm_ref = refs[RANKS : RANKS + 7]
    vel_hbm, next_hbm, wo_ref, own_ref, base_ref = refs[RANKS + 7 : RANKS + 12]
    space_ref, second_ref, x_ref, fresh_ref, vel_ref, next_ref, sems, vel_sems, next_sems = refs[RANKS + 12 :]
    frames, tokens, _ = x_ref.shape
    loads = []
    for n, (src, dst) in enumerate(
        (
            (wo_hbm, wo_ref),
            (own_hbm, own_ref),
            (x_hbm, x_ref),
            (in_hbm_ref, base_ref),
            (fresh_hbm, fresh_ref),
        )
    ):
        loads.append(pltpu.make_async_copy(src, dst, sems.at[n]))
        loads[n].start()

    merged(1, place_ref[1], near_refs, time_ref, space_ref, second_ref)
    attended = jnp.concatenate([first_ref[...], second_ref[...]], axis=0)
    for load in loads:
        load.wait()

    @pl.when(place_ref[0] == place_ref[2])
    def _():
        base_ref[...] = fresh_ref[...]

    chunks = vel_sems.shape[0]
    width = vel_ref.shape[2] // chunks
    copies = []
    for n in range(chunks):
        c, d = slice(n * width, (n + 1) * width), pl.ds(n * width, width)
        projected = matmul(attended, wo_ref[:, c])
        for f in range(frames):
            moving = projected[f * tokens : (f + 1) * tokens] * own_ref[6 + f : 7 + f, c]
            vel_ref[f, :, c] = moving.astype(BF16)
            if f > 0:
                advanced = x_ref[f, :, c].astype(F32) + size_ref[f] * moving
                next_ref[f - 1, :, c] = advanced.astype(BF16)
        copies.append(pltpu.make_async_copy(vel_ref.at[:, :, d], vel_hbm.at[:, :, d], vel_sems.at[n]))
        copies[-1].start()
        filled = next_hbm.at[pl.ds(0, frames - 1), :, d]
        copies.append(pltpu.make_async_copy(next_ref.at[:, :, d], filled, next_sems.at[n]))
        copies[-1].start()
    for copy in copies:
        copy.wait()


def last_kernel(size_ref, att_ref, wo_ref, own_ref, base_ref, kept_ref, next_ref, out_ref, sems):
    del kept_ref
    slot = next_ref.shape[0] - 1
    chunks = sems.shape[0]
    width = out_ref.shape[1] // chunks
    copies = []
    for n in range(chunks):
        c, d = slice(n * width, (n + 1) * width), pl.ds(n * width, width)
        moving = matmul(att_ref[...], wo_ref[:, c]) * own_ref[8:9, c]
        out_ref[:, c] = (base_ref[:, c].astype(F32) + size_ref[2] * moving).astype(BF16)
        copies.append(pltpu.make_async_copy(out_ref.at[:, d], next_ref.at[slot, :, d], sems.at[n]))
        copies[n].start()
    for copy in copies:
        copy.wait()


def whole():
    return pl.BlockSpec(memory_space=pltpu.VMEM)


def scalar():
    return pl.BlockSpec(memory_space=pltpu.SMEM)


def anywhere():
    return pl.BlockSpec(memory_space=pl.ANY)


def pinned(x):
    return pltpu.with_memory_space_constraint(x, pltpu.VMEM)


def in_hbm(x):
    return pltpu.with_memory_space_constraint(x, pltpu.HBM)


def call(kernel, args, in_specs, outs, out_specs, flops=0, nbytes=0, vmem=20, **more):
    return pl.pallas_call(
        kernel,
        out_shape=outs,
        in_specs=in_specs,
        out_specs=out_specs,
        compiler_params=pltpu.CompilerParams(vmem_limit_bytes=vmem * MIB),
        cost_estimate=pl.CostEstimate(flops=flops, bytes_accessed=nbytes, transcendentals=0),
        **more,
    )(*args)


def body(
    latents,
    fresh_noise,
    noise_levels,
    offset,
    block_ids,
    mod_table,
    step_sizes,
    w_query,
    w_key,
    w_value,
    w_out,
):
    frames, tokens, width = latents.shape
    times = lax.axis_size("tm")
    ranks = lax.axis_size("tok")
    share = tokens // times
    total = frames * times
    inner = HEADS * HEAD_DIM
    sds = jax.ShapeDtypeStruct
    dma = pltpu.SemaphoreType.DMA
    back_perm = [(i, i - 1) for i in range(1, times)]
    project_flops = 2 * frames * tokens * width * inner

    def exchange(x, d):
        pairs = []
        for tm in range(times):
            for tok in range(ranks):
                side, y, core = tok // RANKS, tok % RANKS, tm % 2
                pairs.append((tm * ranks + tok, (tm - core + side) * ranks + core * RANKS + (y ^ d)))
        return lax.ppermute(x, ("tm", "tok"), pairs)

    outgoing, x = call(
        shuffle_kernel,
        (in_hbm(latents),),
        [anywhere()],
        (pltpu.HBM((tokens // 8, 2, 8, width), BF16), pltpu.VMEM((frames, tokens, width), BF16)),
        (anywhere(), whole()),
        nbytes=2 * MIB,
        scratch_shapes=[pltpu.VMEM((tokens // 8, 2, 8, width), BF16), dma((4,)), dma((4,))],
    )
    column = lax.all_to_all(outgoing.reshape(times, frames * share, width), "tm", 0, 0)

    place = lax.axis_index("tm").astype(jnp.int32)
    rank = lax.axis_index("tok").astype(jnp.int32) % RANKS
    place = jnp.stack([place, rank, jnp.int32(times - 1)])
    table = mod_table.transpose(1, 0, 2)
    sizes, own, *parts = call(
        home_kernel,
        (
            noise_levels,
            offset,
            step_sizes,
            place,
            pinned(x),
            *[in_hbm(a) for a in (table, w_query, w_key, w_value)],
        ),
        [scalar()] * 4 + [whole()] + [anywhere()] * 4,
        (
            sds((frames + 1,), F32),
            pltpu.HBM((16, width), F32),
            *[sds((3 * SPAN * tokens, HEAD_DIM), BF16)] * RANKS,
        ),
        (scalar(), anywhere(), *[whole()] * RANKS),
        flops=LONG,
        nbytes=10 * MIB,
        scratch_shapes=[
            pltpu.VMEM(table.shape, F32),
            *[pltpu.VMEM((frames * tokens, inner), BF16)] * 3,
            *[pltpu.VMEM((width, inner), BF16)] * 3,
            pltpu.VMEM((16, width), F32),
            dma((4,)),
            dma,
        ],
    )
    units = [exchange(part, d) for d, part in enumerate(parts)]

    small = (
        pltpu.VMEM((16, width), F32),
        pltpu.VMEM((times, frames, width), F32),
        pltpu.VMEM((times, frames, width), F32),
        pltpu.VMEM((total * share, total * share), F32),
    )
    table, noise_levels, sizes = lax.optimization_barrier((table, noise_levels, sizes))
    shifts, scales, bias = call(
        column_kernel,
        (noise_levels, offset, block_ids, table),
        [scalar()] * 3 + [whole()],
        tuple(pltpu.HBM(a.inner_aval.shape, F32) for a in small[1:]),
        (anywhere(),) * 3,
        nbytes=MIB // 4,
        scratch_shapes=[*small[1:], dma((3,))],
    )
    incoming, sizes = lax.optimization_barrier((latents[0], sizes))
    next_latents = lax.ppermute(incoming, "tm", back_perm)

    back = call(
        temporal_kernel,
        (column, *[in_hbm(a) for a in (scales, shifts, w_query, w_key, bias, w_value)]),
        [whole()] + [anywhere()] * 6,
        pltpu.HBM((total * share, inner + HEAD_DIM), BF16),
        anywhere(),
        flops=LONG,
        nbytes=10 * MIB,
        scratch_shapes=[
            *small[1:3],
            *[pltpu.VMEM((width, inner), BF16)] * 2,
            small[3],
            pltpu.VMEM((width, inner), BF16),
            pltpu.VMEM((total * share, inner + HEAD_DIM), BF16),
            dma((6,)),
            dma((HEADS + 1,)),
        ],
    )
    back, next_latents, *units = lax.optimization_barrier((back, next_latents, *units))
    sibling = [lax.ppermute(part, "tm", [(i, i ^ 1) for i in range(times)]) for part in units]
    back = lax.all_to_all(back.reshape(times, frames * share, inner + HEAD_DIM), "tm", 0, 0)
    back = back.reshape(times * frames * share, inner + HEAD_DIM)

    near = call(
        spatial_kernel,
        (*units, *sibling),
        [whole()] * (2 * RANKS),
        [sds((SPAN * tokens + STAT_ROWS, HEAD_DIM), BF16)] * RANKS,
        [whole()] * RANKS,
        flops=2 * LONG,
        nbytes=3 * MIB,
    )
    near = [exchange(part, d) for d, part in enumerate(near)]

    space = pltpu.VMEM((RANKS, SPAN * tokens + STAT_ROWS, HEAD_DIM), BF16)
    sent, first = call(
        first_kernel,
        (place, *near, back),
        [scalar()] + [whole()] * (RANKS + 1),
        (sds((tokens, inner), BF16), pltpu.VMEM((tokens, inner), BF16)),
        (whole(), whole()),
        nbytes=2 * MIB,
        scratch_shapes=[space],
    )
    next_first = lax.ppermute(sent, "tm", back_perm)
    velocity, following, wo, own, base = call(
        project_kernel,
        (
            place,
            sizes,
            *near,
            back,
            pinned(first),
            *[in_hbm(a) for a in (w_out, own, latents, fresh_noise, next_latents)],
        ),
        [scalar()] * 2 + [whole()] * (RANKS + 2) + [anywhere()] * 5,
        (
            pltpu.HBM((frames, tokens, width), BF16),
            pltpu.HBM((frames, tokens, width), BF16),
            pltpu.VMEM((inner, width), BF16),
            pltpu.VMEM((16, width), F32),
            pltpu.VMEM((tokens, width), BF16),
        ),
        (anywhere(), anywhere(), whole(), whole(), whole()),
        flops=project_flops,
        nbytes=6 * MIB,
        scratch_shapes=[
            space,
            pltpu.VMEM((tokens, inner), BF16),
            pltpu.VMEM((frames, tokens, width), BF16),
            pltpu.VMEM((tokens, width), BF16),
            pltpu.VMEM((frames, tokens, width), BF16),
            pltpu.VMEM((frames - 1, tokens, width), BF16),
            dma((5,)),
            *[dma((3,))] * 2,
        ],
    )
    following = call(
        last_kernel,
        (sizes, next_first, pinned(wo), pinned(own), pinned(base), following),
        [scalar()] + [whole()] * 4 + [anywhere()],
        sds((frames, tokens, width), BF16),
        anywhere(),
        flops=project_flops // 2,
        nbytes=4 * MIB,
        scratch_shapes=[pltpu.VMEM((tokens, width), BF16), dma((3,))],
        input_output_aliases={5: 0},
    )
    return velocity, following


def solution(mesh):
    in_specs = (P("tm", "tok", None), P("tok", None), P(), P(), P(), P(), P(), P(), P(), P(), P())
    out_specs = (P("tm", "tok", None), P("tm", "tok", None))
    return jax.shard_map(body, mesh=mesh, in_specs=in_specs, out_specs=out_specs, check_vma=False)
```

time: 97.3 us -> 88.5 us (0.910)
  the two profiles are of different devices: /device:TPU:229 before, /device:TPU:5 now
where the time goes in v3:
time: 88.5 us; the launch traced here: 88.1 us
  starting transfers between devices  45.4 us (51%)
  Pallas kernels  26.9 us (30%)
  waiting for transfers between devices  14 us (16%)
  between operations  1.7 us (2%)
    pallas_call x8, Pallas kernels, call(): pl.pallas_call(kernel, out_shape=outs, in_specs=in_specs, out_specs=out_s...  26.9 us
    ppermute x8, starting transfers between devices, exchange(): return lax.ppermute(x, ('tm', 'tok'), pairs)  19.6 us
    all_to_all x1, starting transfers between devices, body(): lax.all_to_all(outgoing.reshape(times, frames * share, width), 'tm', 0, 0)  11.9 us
    all_to_all x1, starting transfers between devices, body(): lax.all_to_all(back.reshape(times, frames * share, inner + HEAD_DIM), 'tm...  9.07 us
    ppermute x8, waiting for transfers between devices, exchange(): return lax.ppermute(x, ('tm', 'tok'), pairs)  7.07 us
    all_to_all x1, waiting for transfers between devices, body(): lax.all_to_all(outgoing.reshape(times, frames * share, width), 'tm', 0, 0)  3.79 us
    ppermute x1, waiting for transfers between devices, body(): next_first = lax.ppermute(sent, 'tm', back_perm)  3.14 us
    ppermute x1, starting transfers between devices, body(): next_latents = lax.ppermute(incoming, 'tm', back_perm)  1.92 us
  transfers between devices with their start and end apart: 16, of which 6 were waited for; matrix products, arithmetic and copies ran while one was open for 0% of the time, Pallas kernels for 25%

profile of v3, /device:TPU:5, one launch (start us, length us, event | category | flops | bytes accessed | tf_op | source)
XLA Modules:
  0.0 88.1 jit_solution(13997075652179206449)
XLA Ops:
  0.6 0.0 copy-start.3
  0.6 0.0 copy-start.5
  0.6 2.0 %shard_map.122 = (bf16[16,2,8,1536]{3,2,1,0:T(8,128)(2,1)}, bf16[2,128,1536]{2,1,0:T(8,128)(2,1)S(1)}) custom-call(bf16[2,128,1536]{2,1,0:T(8,128)(2,1)} %refs_8_.1), custom_call_target="tpu_custom_call" | custom-call | bytes 2097152 | tf_op jit(solution)/shard_map/pallas_call | solution.py:361
  2.7 11.9 %all-to-all-start = ((bf16[32,8,1536]{2,1,0:T(8,128)(2,1)}), bf16[32,8,1536]{2,1,0:T(8,128)(2,1)S(1)}, u32[]{:S(2)}, u32[]{:S(2)}) async-start(bf16[32,8,1536]{2,1,0:T(8,128)(2,1)} %bitcast.12), calls=%async_computation | async-start | bytes 1572864 | tf_op jit(solution)/shard_map/all_to_all | solution.py:413
  15.3 0.1 pad_add_fusion.place_ref
  15.4 0.0 copy-start.6
  15.4 0.0 copy-start
  15.4 0.0 copy-start.4
  15.4 5.9 %shard_map.123 = (f32[3]{0:T(128)S(1)}, f32[16,1536]{1,0:T(8,128)}, bf16[1152,128]{1,0:T(8,128)(2,1)S(1)}, bf16[1152,128]{1,0:T(8,128)(2,1)S(1)}, bf16[1152,128]...) custom-call(s32[64]{0:T(128)S(1)} %copy-done.3, s32[1]{0:T(128)S(6)} %copy.15.offset_ref, f32[32]{0:T(128)S(1)} %copy-done.5, ...), custom_call_target="tpu_custom_call" | custom-call | flops 60000002048 | bytes 10485760 | tf_op jit(solution)/shard_map/pallas_call | solution.py:361
  21.3 3.1 %collective-permute-start.1 = (bf16[1152,128]{1,0:T(8,128)(2,1)S(1)}, bf16[1152,128]{1,0:T(8,128)(2,1)S(1)}, u32[]{:S(2)}, u32[]{:S(2)}) collective-permute-start(bf16[1152,128]{1,0:T(8,128)(2,1)S(1)} %get-tuple-element.46), channel_id=1, source_target_pairs={{0,0},{1,1},{2,2},{3,3},{4,8},{5,9},{6,10},{7,11},{8,4},{9,5},{10,... | collective-permute-start | bytes 884744 | tf_op jit(solution)/shard_map/ppermute | solution.py:402
  24.4 1.7 %collective-permute-start.2 = (bf16[1152,128]{1,0:T(8,128)(2,1)S(1)}, bf16[1152,128]{1,0:T(8,128)(2,1)S(1)}, u32[]{:S(2)}, u32[]{:S(2)}) collective-permute-start(bf16[1152,128]{1,0:T(8,128)(2,1)S(1)} %get-tuple-element.47), channel_id=1, source_target_pairs={{0,1},{1,0},{2,3},{3,2},{4,9},{5,8},{6,11},{7,10},{8,5},{9,4},{10,... | collective-permute-start | bytes 884744 | tf_op jit(solution)/shard_map/ppermute | solution.py:402
  26.1 3.5 %collective-permute-start.3 = (bf16[1152,128]{1,0:T(8,128)(2,1)S(1)}, bf16[1152,128]{1,0:T(8,128)(2,1)S(1)}, u32[]{:S(2)}, u32[]{:S(2)}) collective-permute-start(bf16[1152,128]{1,0:T(8,128)(2,1)S(1)} %get-tuple-element.48), channel_id=1, source_target_pairs={{0,2},{1,3},{2,0},{3,1},{4,10},{5,11},{6,8},{7,9},{8,6},{9,7},{10,... | collective-permute-start | bytes 884744 | tf_op jit(solution)/shard_map/ppermute | solution.py:402
  29.6 0.2 collective-permute-start.4
  29.8 0.0 copy-done.6
  29.9 1.9 %collective-permute-start = (bf16[128,1536]{1,0:T(8,128)(2,1)S(1)}, bf16[128,1536]{1,0:T(8,128)(2,1)}, u32[]{:S(2)}, u32[]{:S(2)}) collective-permute-start(bf16[128,1536]{1,0:T(8,128)(2,1)S(1)} %slice_bitcast_fusion), channel_id=1, source_target_pairs={{8,0},{16,8},{24,16},{32,24},{40,32},{48,40},{56,48},{64,56},{72,6... | collective-permute-start | bytes 1179656 | tf_op jit(solution)/shard_map/ppermute | solution.py:466
  31.8 1.9 %shard_map.124 = (f32[32,2,1536]{2,1,0:T(2,128)}, f32[32,2,1536]{2,1,0:T(2,128)}, f32[256,256]{1,0:T(8,128)}) custom-call(s32[64]{0:T(128)S(1)} %copy-done.3, s32[1]{0:T(128)S(6)} %copy.15.offset_ref, s32[64]{0:T(128)S(1)} %copy-done.4, f32[3,32,1536]{2,1,0:T(8,128)S(1)} %bitcast.11), custom_call_target="tpu_custom_call" | custom-call | bytes 262144 | tf_op jit(solution)/shard_map/pallas_call | solution.py:361
  33.7 3.8 %all-to-all-done.x_ref = bf16[32,8,1536]{2,1,0:T(8,128)(2,1)S(1)} async-done(((bf16[32,8,1536]{2,1,0:T(8,128)(2,1)}), bf16[32,8,1536]{2,1,0:T(8,128)(2,1)S(1)}, u32[]{:S(2)}, u32[]{:S(2)}) %all-to-all-start) | async-done | bytes 786464 | tf_op jit(solution)/shard_map/all_to_all | solution.py:413
  37.5 6.6 %shard_map.125 = bf16[256,896]{1,0:T(8,128)(2,1)} custom-call(bf16[32,8,1536]{2,1,0:T(8,128)(2,1)S(1)} %all-to-all-done.x_ref, f32[32,2,1536]{2,1,0:T(2,128)} %get-tuple-element.42.refs_0_, f32[32,2,1536]{2,1,0:T(2,128)} %get-tuple-element.43.refs_1_, bf16[1536,768]{1,0:T(8,128)(2,1)} %refs_2_.1, bf16[1536,768]{1,0:T(8,128)(2,1)} %refs_3_.1, ...), custom_call_target="tpu_custom_call" | custom-call | flops 60000002048 | bytes 10485760 | tf_op jit(solution)/shard_map/pallas_call | solution.py:361
  44.1 0.0 collective-permute-done.1.refs_0_
  44.1 0.0 collective-permute-done.2.refs_1_
  44.1 0.0 collective-permute-done.3.refs_2_
  44.1 2.5 %collective-permute-done.4.refs_3_ = bf16[1152,128]{1,0:T(8,128)(2,1)S(1)} collective-permute-done((bf16[1152,128]{1,0:T(8,128)(2,1)S(1)}, bf16[1152,128]{1,0:T(8,128)(2,1)S(1)}, u32[]{:S(2)}, u32[]{:S(2)}) %collective-permute-start.4) | collective-permute-done | bytes 294944 | tf_op jit(solution)/shard_map/ppermute | solution.py:402
  46.6 0.0 collective-permute-done.refs_10_
  46.6 0.0 collective-permute-start.5
  46.7 0.5 collective-permute-start.6
  47.2 0.0 collective-permute-start.7
  47.2 0.5 collective-permute-start.8
  47.7 9.1 %all-to-all-start.1 = ((bf16[32,8,896]{2,1,0:T(8,128)(2,1)}), bf16[32,8,896]{2,1,0:T(8,128)(2,1)S(1)}, u32[]{:S(2)}, u32[]{:S(2)}) async-start(bf16[32,8,896]{2,1,0:T(8,128)(2,1)} %bitcast.13), calls=%async_computation.1 | async-start | bytes 917504 | tf_op jit(solution)/shard_map/all_to_all | solution.py:488
  56.8 0.0 collective-permute-done.5.refs_4_
  56.8 0.0 collective-permute-done.6.refs_5_
  56.8 0.0 collective-permute-done.7.refs_6_
  56.8 0.0 collective-permute-done.8.refs_7_
  56.8 3.3 %shard_map.126 = (bf16[400,128]{1,0:T(8,128)(2,1)S(1)}, bf16[400,128]{1,0:T(8,128)(2,1)S(1)}, bf16[400,128]{1,0:T(8,128)(2,1)S(1)}, bf16[400,128]{1,0:T(8,128)(2,1)S(1)}) custom-call(bf16[1152,128]{1,0:T(8,128)(2,1)S(1)} %collective-permute-done.1.refs_0_, bf16[1152,128]{1,0:T(8,128)(2,1)S(1)} %collective-permute-done.2.refs_1_, ...), custom_call_target="tpu_custom_call" | custom-call | flops 120000004096 | bytes 3145728 | tf_op jit(solution)/shard_map/pallas_call | solution.py:361
  60.1 6.2 %collective-permute-start.9 = (bf16[400,128]{1,0:T(8,128)(2,1)S(1)}, bf16[400,128]{1,0:T(8,128)(2,1)S(1)}, u32[]{:S(2)}, u32[]{:S(2)}) collective-permute-start(bf16[400,128]{1,0:T(8,128)(2,1)S(1)} %get-tuple-element.54), channel_id=1, source_target_pairs={{0,0},{1,1},{2,2},{3,3},{4,8},{5,9},{6,10},{7,11},{8,4},{9,5},{10,... | collective-permute-start | bytes 307208 | tf_op jit(solution)/shard_map/ppermute | solution.py:402
  66.3 0.1 collective-permute-start.10
  66.4 3.1 %collective-permute-start.11 = (bf16[400,128]{1,0:T(8,128)(2,1)S(1)}, bf16[400,128]{1,0:T(8,128)(2,1)S(1)}, u32[]{:S(2)}, u32[]{:S(2)}) collective-permute-start(bf16[400,128]{1,0:T(8,128)(2,1)S(1)} %get-tuple-element.56), channel_id=1, source_target_pairs={{0,2},{1,3},{2,0},{3,1},{4,10},{5,11},{6,8},{7,9},{8,6},{9,7},{10,... | collective-permute-start | bytes 307208 | tf_op jit(solution)/shard_map/ppermute | solution.py:402
  69.6 1.6 %collective-permute-start.12 = (bf16[400,128]{1,0:T(8,128)(2,1)S(1)}, bf16[400,128]{1,0:T(8,128)(2,1)S(1)}, u32[]{:S(2)}, u32[]{:S(2)}) collective-permute-start(bf16[400,128]{1,0:T(8,128)(2,1)S(1)} %get-tuple-element.57), channel_id=1, source_target_pairs={{0,3},{1,2},{2,1},{3,0},{4,11},{5,10},{6,9},{7,8},{8,7},{9,6},{10,... | collective-permute-start | bytes 307208 | tf_op jit(solution)/shard_map/ppermute | solution.py:402
  71.2 0.0 collective-permute-done.9.refs_0_
  71.2 1.4 %collective-permute-done.10.refs_1_ = bf16[400,128]{1,0:T(8,128)(2,1)S(1)} collective-permute-done((bf16[400,128]{1,0:T(8,128)(2,1)S(1)}, bf16[400,128]{1,0:T(8,128)(2,1)S(1)}, u32[]{:S(2)}, u32[]{:S(2)}) %collective-permute-start.10) | collective-permute-done | bytes 102432 | tf_op jit(solution)/shard_map/ppermute | solution.py:402
  72.6 1.3 %collective-permute-done.11.refs_2_ = bf16[400,128]{1,0:T(8,128)(2,1)S(1)} collective-permute-done((bf16[400,128]{1,0:T(8,128)(2,1)S(1)}, bf16[400,128]{1,0:T(8,128)(2,1)S(1)}, u32[]{:S(2)}, u32[]{:S(2)}) %collective-permute-start.11) | collective-permute-done | bytes 102432 | tf_op jit(solution)/shard_map/ppermute | solution.py:402
  73.9 1.8 %collective-permute-done.12.refs_3_ = bf16[400,128]{1,0:T(8,128)(2,1)S(1)} collective-permute-done((bf16[400,128]{1,0:T(8,128)(2,1)S(1)}, bf16[400,128]{1,0:T(8,128)(2,1)S(1)}, u32[]{:S(2)}, u32[]{:S(2)}) %collective-permute-start.12) | collective-permute-done | bytes 102432 | tf_op jit(solution)/shard_map/ppermute | solution.py:402
  75.8 0.0 all-to-all-done.1
  75.8 0.0 copy-done.2
  75.8 1.1 %shard_map.127 = (bf16[128,768]{1,0:T(8,128)(2,1)S(1)}, bf16[128,768]{1,0:T(8,128)(2,1)S(1)}) custom-call(s32[3]{0:T(128)S(1)} %copy-done.2, bf16[400,128]{1,0:T(8,128)(2,1)S(1)} %collective-permute-done.9.refs_0_, bf16[400,128]{1,0:T(8,128)(2,1)S(1)} %collective-permute-done.10.refs_1_, bf16[400,128]{1,0:T(8,128)(2,1)S(1)} %collective-permute-done.11.refs_2_, ...), custom_call_target="tpu_custom_call" | custom-call | bytes 2097152 | tf_op jit(solution)/shard_map/pallas_call | solution.py:361
  76.9 1.9 %collective-permute-start.13 = (bf16[128,768]{1,0:T(8,128)(2,1)S(1)}, bf16[128,768]{1,0:T(8,128)(2,1)S(1)}, u32[]{:S(2)}, u32[]{:S(2)}) collective-permute-start(bf16[128,768]{1,0:T(8,128)(2,1)S(1)} %get-tuple-element.63), channel_id=1, source_target_pairs={{8,0},{16,8},{24,16},{32,24},{40,32},{48,40},{56,48},{64,56},{72,6... | collective-permute-start | bytes 589832 | tf_op jit(solution)/shard_map/ppermute | solution.py:512
  78.8 4.3 %shard_map.128 = (bf16[2,128,1536]{2,1,0:T(8,128)(2,1)}, bf16[2,128,1536]{2,1,0:T(8,128)(2,1)}, bf16[768,1536]{1,0:T(8,128)(2,1)S(1)}, f32[16,1536]{1,0:T(8,128)S(1)}, bf16[128,1536]{1,0:T(8,128)(2,1)S(1)}) custom-call(s32[3]{0:T(128)S(1)} %copy-done.2, f32[3]{0:T(128)S(1)} %get-tuple-element.38.size_ref, ...), custom_call_target="tpu_custom_call" | custom-call | flops 603979776 | bytes 6291456 | tf_op jit(solution)/shard_map/pallas_call | solution.py:361
  83.1 3.1 %collective-permute-done.13.att_ref = bf16[128,768]{1,0:T(8,128)(2,1)S(1)} collective-permute-done((bf16[128,768]{1,0:T(8,128)(2,1)S(1)}, bf16[128,768]{1,0:T(8,128)(2,1)S(1)}, u32[]{:S(2)}, u32[]{:S(2)}) %collective-permute-start.13) | collective-permute-done | bytes 196640 | tf_op jit(solution)/shard_map/ppermute | solution.py:512
  86.3 1.7 %shard_map.129 = bf16[2,128,1536]{2,1,0:T(8,128)(2,1)} custom-call(f32[3]{0:T(128)S(1)} %get-tuple-element.38.size_ref, bf16[128,768]{1,0:T(8,128)(2,1)S(1)} %collective-permute-done.13.att_ref, bf16[768,1536]{1,0:T(8,128)(2,1)S(1)} %get-tuple-element.64.wo_ref, f32[16,1536]{1,0:T(8,128)S(1)} %get-tuple-element.65.own_ref, ...), custom_call_target="tpu_custom_call", output_to_operand_aliasing={{}: (5, {})} | custom-call | flops 301989888 | bytes 4194304 | tf_op jit(solution)/shard_map/pallas_call | solution.py:361
  (8 shorter events, 0.0 us)
Async XLA Ops:
  0.6 14.7 %copy-start.3 = (s32[64]{0:T(128)S(1)}, s32[64]{0:T(128)}, u32[]{:S(2)}) copy-start(s32[64]{0:T(128)} %noise_ref.2) | copy-start | bytes 772
  0.6 14.7 %copy-start.5 = (f32[32]{0:T(128)S(1)}, f32[32]{0:T(128)}, u32[]{:S(2)}) copy-start(f32[32]{0:T(128)} %step_ref.1) | copy-start | bytes 388
  2.7 34.8 %all-to-all-start = ((bf16[32,8,1536]{2,1,0:T(8,128)(2,1)}), bf16[32,8,1536]{2,1,0:T(8,128)(2,1)S(1)}, u32[]{:S(2)}, u32[]{:S(2)}) async-start(bf16[32,8,1536]{2,1,0:T(8,128)(2,1)} %bitcast.12), calls=%async_computation | async-start | bytes 1572864 | tf_op jit(solution)/shard_map/all_to_all | solution.py:413
  15.3 6.0 %copy-start.1 = (s32[3]{0:T(128)}, s32[3]{0:T(128)S(1)}, u32[]{:S(2)}) copy-start(s32[3]{0:T(128)S(1)} %pad_add_fusion.place_ref) | copy-start | bytes 40
  15.4 14.5 %copy-start.6 = (bf16[2,128,1536]{2,1,0:T(8,128)(2,1)S(1)}, bf16[2,128,1536]{2,1,0:T(8,128)(2,1)}, u32[]{:S(2)}) copy-start(bf16[2,128,1536]{2,1,0:T(8,128)(2,1)} %refs_8_.1) | copy-start | bytes 2359300
  15.4 16.4 %copy-start = (f32[32,3,1536]{2,0,1:T(8,128)S(1)}, f32[32,3,1536]{2,0,1:T(8,128)}, u32[]{:S(2)}) copy-start(f32[32,3,1536]{2,0,1:T(8,128)} %param.16) | copy-start | bytes 1769476
  15.4 16.4 %copy-start.4 = (s32[64]{0:T(128)S(1)}, s32[64]{0:T(128)}, u32[]{:S(2)}) copy-start(s32[64]{0:T(128)} %blocks_ref.1) | copy-start | bytes 772
  21.3 22.8 %collective-permute-start.1 = (bf16[1152,128]{1,0:T(8,128)(2,1)S(1)}, bf16[1152,128]{1,0:T(8,128)(2,1)S(1)}, u32[]{:S(2)}, u32[]{:S(2)}) collective-permute-start(bf16[1152,128]{1,0:T(8,128)(2,1)S(1)} %get-tuple-element.46), channel_id=1, source_target_pairs={{0,0},{1,1},{2,2},{3,3},{4,8},{5,9},{6,10},{7,11},{8,4},{9,5},{10,... | collective-permute-start | bytes 884744 | tf_op jit(solution)/shard_map/ppermute | solution.py:402
  24.4 19.7 %collective-permute-start.2 = (bf16[1152,128]{1,0:T(8,128)(2,1)S(1)}, bf16[1152,128]{1,0:T(8,128)(2,1)S(1)}, u32[]{:S(2)}, u32[]{:S(2)}) collective-permute-start(bf16[1152,128]{1,0:T(8,128)(2,1)S(1)} %get-tuple-element.47), channel_id=1, source_target_pairs={{0,1},{1,0},{2,3},{3,2},{4,9},{5,8},{6,11},{7,10},{8,5},{9,4},{10,... | collective-permute-start | bytes 884744 | tf_op jit(solution)/shard_map/ppermute | solution.py:402
  26.1 18.1 %collective-permute-start.3 = (bf16[1152,128]{1,0:T(8,128)(2,1)S(1)}, bf16[1152,128]{1,0:T(8,128)(2,1)S(1)}, u32[]{:S(2)}, u32[]{:S(2)}) collective-permute-start(bf16[1152,128]{1,0:T(8,128)(2,1)S(1)} %get-tuple-element.48), channel_id=1, source_target_pairs={{0,2},{1,3},{2,0},{3,1},{4,10},{5,11},{6,8},{7,9},{8,6},{9,7},{10,... | collective-permute-start | bytes 884744 | tf_op jit(solution)/shard_map/ppermute | solution.py:402
  29.6 17.1 %collective-permute-start.4 = (bf16[1152,128]{1,0:T(8,128)(2,1)S(1)}, bf16[1152,128]{1,0:T(8,128)(2,1)S(1)}, u32[]{:S(2)}, u32[]{:S(2)}) collective-permute-start(bf16[1152,128]{1,0:T(8,128)(2,1)S(1)} %get-tuple-element.49), channel_id=1, source_target_pairs={{0,3},{1,2},{2,1},{3,0},{4,11},{5,10},{6,9},{7,8},{8,7},{9,6},{10,... | collective-permute-start | bytes 884744 | tf_op jit(solution)/shard_map/ppermute | solution.py:402
  29.9 16.8 %collective-permute-start = (bf16[128,1536]{1,0:T(8,128)(2,1)S(1)}, bf16[128,1536]{1,0:T(8,128)(2,1)}, u32[]{:S(2)}, u32[]{:S(2)}) collective-permute-start(bf16[128,1536]{1,0:T(8,128)(2,1)S(1)} %slice_bitcast_fusion), channel_id=1, source_target_pairs={{8,0},{16,8},{24,16},{32,24},{40,32},{48,40},{56,48},{64,56},{72,6... | collective-permute-start | bytes 1179656 | tf_op jit(solution)/shard_map/ppermute | solution.py:466
  46.6 10.1 %collective-permute-start.5 = (bf16[1152,128]{1,0:T(8,128)(2,1)S(1)}, bf16[1152,128]{1,0:T(8,128)(2,1)S(1)}, u32[]{:S(2)}, u32[]{:S(2)}) collective-permute-start(bf16[1152,128]{1,0:T(8,128)(2,1)S(1)} %collective-permute-done.1.refs_0_), channel_id=1, source_target_pairs={{0,8},{8,0},{16,24},{24,16},{32,40},{40,32},{48,56},{56,48},{64,72... | collective-permute-start | bytes 884744 | tf_op jit(solution)/shard_map/ppermute | solution.py:487
  46.7 10.1 %collective-permute-start.6 = (bf16[1152,128]{1,0:T(8,128)(2,1)S(1)}, bf16[1152,128]{1,0:T(8,128)(2,1)S(1)}, u32[]{:S(2)}, u32[]{:S(2)}) collective-permute-start(bf16[1152,128]{1,0:T(8,128)(2,1)S(1)} %collective-permute-done.2.refs_1_), channel_id=1, source_target_pairs={{0,8},{8,0},{16,24},{24,16},{32,40},{40,32},{48,56},{56,48},{64,72... | collective-permute-start | bytes 884744 | tf_op jit(solution)/shard_map/ppermute | solution.py:487
  47.2 9.6 %collective-permute-start.7 = (bf16[1152,128]{1,0:T(8,128)(2,1)S(1)}, bf16[1152,128]{1,0:T(8,128)(2,1)S(1)}, u32[]{:S(2)}, u32[]{:S(2)}) collective-permute-start(bf16[1152,128]{1,0:T(8,128)(2,1)S(1)} %collective-permute-done.3.refs_2_), channel_id=1, source_target_pairs={{0,8},{8,0},{16,24},{24,16},{32,40},{40,32},{48,56},{56,48},{64,72... | collective-permute-start | bytes 884744 | tf_op jit(solution)/shard_map/ppermute | solution.py:487
  47.2 9.6 %collective-permute-start.8 = (bf16[1152,128]{1,0:T(8,128)(2,1)S(1)}, bf16[1152,128]{1,0:T(8,128)(2,1)S(1)}, u32[]{:S(2)}, u32[]{:S(2)}) collective-permute-start(bf16[1152,128]{1,0:T(8,128)(2,1)S(1)} %collective-permute-done.4.refs_3_), channel_id=1, source_target_pairs={{0,8},{8,0},{16,24},{24,16},{32,40},{40,32},{48,56},{56,48},{64,72... | collective-permute-start | bytes 884744 | tf_op jit(solution)/shard_map/ppermute | solution.py:487
  47.7 28.1 %all-to-all-start.1 = ((bf16[32,8,896]{2,1,0:T(8,128)(2,1)}), bf16[32,8,896]{2,1,0:T(8,128)(2,1)S(1)}, u32[]{:S(2)}, u32[]{:S(2)}) async-start(bf16[32,8,896]{2,1,0:T(8,128)(2,1)} %bitcast.13), calls=%async_computation.1 | async-start | bytes 917504 | tf_op jit(solution)/shard_map/all_to_all | solution.py:488
  56.7 19.0 %copy-start.2 = (s32[3]{0:T(128)S(1)}, s32[3]{0:T(128)}, u32[]{:S(2)}) copy-start(s32[3]{0:T(128)} %copy-done.1) | copy-start | bytes 40
  60.1 11.1 %collective-permute-start.9 = (bf16[400,128]{1,0:T(8,128)(2,1)S(1)}, bf16[400,128]{1,0:T(8,128)(2,1)S(1)}, u32[]{:S(2)}, u32[]{:S(2)}) collective-permute-start(bf16[400,128]{1,0:T(8,128)(2,1)S(1)} %get-tuple-element.54), channel_id=1, source_target_pairs={{0,0},{1,1},{2,2},{3,3},{4,8},{5,9},{6,10},{7,11},{8,4},{9,5},{10,... | collective-permute-start | bytes 307208 | tf_op jit(solution)/shard_map/ppermute | solution.py:402
  66.3 6.2 %collective-permute-start.10 = (bf16[400,128]{1,0:T(8,128)(2,1)S(1)}, bf16[400,128]{1,0:T(8,128)(2,1)S(1)}, u32[]{:S(2)}, u32[]{:S(2)}) collective-permute-start(bf16[400,128]{1,0:T(8,128)(2,1)S(1)} %get-tuple-element.55), channel_id=1, source_target_pairs={{0,1},{1,0},{2,3},{3,2},{4,9},{5,8},{6,11},{7,10},{8,5},{9,4},{10,... | collective-permute-start | bytes 307208 | tf_op jit(solution)/shard_map/ppermute | solution.py:402
  66.4 7.5 %collective-permute-start.11 = (bf16[400,128]{1,0:T(8,128)(2,1)S(1)}, bf16[400,128]{1,0:T(8,128)(2,1)S(1)}, u32[]{:S(2)}, u32[]{:S(2)}) collective-permute-start(bf16[400,128]{1,0:T(8,128)(2,1)S(1)} %get-tuple-element.56), channel_id=1, source_target_pairs={{0,2},{1,3},{2,0},{3,1},{4,10},{5,11},{6,8},{7,9},{8,6},{9,7},{10,... | collective-permute-start | bytes 307208 | tf_op jit(solution)/shard_map/ppermute | solution.py:402
  69.6 6.2 %collective-permute-start.12 = (bf16[400,128]{1,0:T(8,128)(2,1)S(1)}, bf16[400,128]{1,0:T(8,128)(2,1)S(1)}, u32[]{:S(2)}, u32[]{:S(2)}) collective-permute-start(bf16[400,128]{1,0:T(8,128)(2,1)S(1)} %get-tuple-element.57), channel_id=1, source_target_pairs={{0,3},{1,2},{2,1},{3,0},{4,11},{5,10},{6,9},{7,8},{8,7},{9,6},{10,... | collective-permute-start | bytes 307208 | tf_op jit(solution)/shard_map/ppermute | solution.py:402
  76.9 9.4 %collective-permute-start.13 = (bf16[128,768]{1,0:T(8,128)(2,1)S(1)}, bf16[128,768]{1,0:T(8,128)(2,1)S(1)}, u32[]{:S(2)}, u32[]{:S(2)}) collective-permute-start(bf16[128,768]{1,0:T(8,128)(2,1)S(1)} %get-tuple-element.63), channel_id=1, source_target_pairs={{8,0},{16,8},{24,16},{32,24},{40,32},{48,40},{56,48},{64,56},{72,6... | collective-permute-start | bytes 589832 | tf_op jit(solution)/shard_map/ppermute | solution.py:512

commit v4 on v3

--- a/solution.py
+++ b/solution.py
@@ -16,6 +16,7 @@
 FLOOR = -1e29
 MIB = 1 << 20
 STAT_ROWS = 16
+PAUSE = 3_500_000_000
 LONG = 60_000_000_000
 BF16 = jnp.bfloat16
 F32 = jnp.float32
@@ -167,6 +168,10 @@
         store.wait()
 
 
+def pass_kernel(in_ref, out_ref):
+    out_ref[...] = in_ref[...]
+
+
 def spatial_kernel(*refs):
     kvs, qs, outs = refs[: 2 * RANKS], refs[:RANKS], refs[2 * RANKS :]
     tokens = HEAD_DIM
@@ -240,15 +245,22 @@
         copy.wait()
 
 
-def merged(f, rank, near_refs, time_ref, space_ref, out_ref):
+def reorder_kernel(time_ref, far_ref, logs_ref):
+    frames, tokens, inner = far_ref.shape
+    width = time_ref.shape[1]
+    turned = time_ref[...].astype(F32).reshape(tokens // 8, 2, 8, width)
+    for f, rows in enumerate(swap_halves(turned[:, 0], turned[:, 1])):
+        rows = rows.reshape(tokens, width)
+        far_ref[f] = rows[:, :inner].astype(BF16)
+        stats = rows[:, inner:]
+        logs_ref[f, :, 0:8] = stats[:, 0:8] + stats[:, 8:16] + stats[:, 16:24]
+
+
+def merged(f, rank, near_refs, far_ref, logs_ref, space_ref, out_ref):
     for d, ref in enumerate(near_refs):
         space_ref[rank ^ d] = ref[...]
     tokens = out_ref.shape[0]
-    width = time_ref.shape[1]
-    turned = time_ref[...].astype(F32).reshape(tokens // 8, 2, 8, width)
-    far_rows = swap_halves(turned[:, 0], turned[:, 1])[f].reshape(tokens, width)
-    stats = far_rows[:, HEADS * HEAD_DIM :]
-    time_log = stats[:, 0:8] + stats[:, 8:16] + stats[:, 16:24]
+    time_log = logs_ref[f, :, 0:8]
     log_rows = []
     for h in range(HEADS):
         st = space_ref[2 * f + h // SPAN, SPAN * tokens : SPAN * tokens + STAT_ROWS].astype(F32)
@@ -262,21 +274,23 @@
         own = slice(h * HEAD_DIM, (h + 1) * HEAD_DIM)
         u = h % SPAN
         near = space_ref[2 * f + h // SPAN, u * tokens : (u + 1) * tokens].astype(F32)
-        mixed = of_space[:, h : h + 1] * near + of_time[:, h : h + 1] * far_rows[:, own]
+        far = far_ref[f, :, own].astype(F32)
+        mixed = of_space[:, h : h + 1] * near + of_time[:, h : h + 1] * far
         out_ref[:, own] = mixed.astype(BF16)
 
 
-def first_kernel(place_ref, *refs):
-    near_refs, (time_ref, sent_ref, first_ref, space_ref) = refs[:RANKS], refs[RANKS:]
-    merged(0, place_ref[1], near_refs, time_ref, space_ref, first_ref)
+def first_kernel(place_ref, mark_ref, *refs):
+    del mark_ref
+    near_refs, (far_ref, logs_ref, sent_ref, first_ref, space_ref) = refs[:RANKS], refs[RANKS:]
+    merged(0, place_ref[1], near_refs, far_ref, logs_ref, space_ref, first_ref)
     sent_ref[...] = first_ref[...]
 
 
 def project_kernel(place_ref, size_ref, *refs):
     near_refs = refs[:RANKS]
-    time_ref, first_ref, wo_hbm, own_hbm, x_hbm, fresh_hbm, in_hbm_ref = refs[RANKS : RANKS + 7]
-    vel_hbm, next_hbm, wo_ref, own_ref, base_ref = refs[RANKS + 7 : RANKS + 12]
-    space_ref, second_ref, x_ref, fresh_ref, vel_ref, next_ref, sems, vel_sems, next_sems = refs[RANKS + 12 :]
+    far_ref, logs_ref, first_ref, wo_hbm, own_hbm, x_hbm, fresh_hbm, in_hbm_ref = refs[RANKS : RANKS + 8]
+    vel_hbm, next_hbm, wo_ref, own_ref, base_ref = refs[RANKS + 8 : RANKS + 13]
+    space_ref, second_ref, x_ref, fresh_ref, vel_ref, next_ref, sems, vel_sems, next_sems = refs[RANKS + 13 :]
     frames, tokens, _ = x_ref.shape
     loads = []
     for n, (src, dst) in enumerate(
@@ -291,7 +305,7 @@
         loads.append(pltpu.make_async_copy(src, dst, sems.at[n]))
         loads[n].start()
 
-    merged(1, place_ref[1], near_refs, time_ref, space_ref, second_ref)
+    merged(1, place_ref[1], near_refs, far_ref, logs_ref, space_ref, second_ref)
     attended = jnp.concatenate([first_ref[...], second_ref[...]], axis=0)
     for load in loads:
         load.wait()
@@ -483,7 +497,10 @@
             dma((HEADS + 1,)),
         ],
     )
-    back, next_latents, *units = lax.optimization_barrier((back, next_latents, *units))
+    mark = step_sizes.reshape(1, -1)
+    _, next_latents, mark, *units = lax.optimization_barrier((back, next_latents, mark, *units))
+    mark = call(pass_kernel, (mark,), [whole()], sds(mark.shape, F32), whole(), flops=PAUSE)
+    mark, *units = lax.optimization_barrier((mark, *units))
     sibling = [lax.ppermute(part, "tm", [(i, i ^ 1) for i in range(times)]) for part in units]
     back = lax.all_to_all(back.reshape(times, frames * share, inner + HEAD_DIM), "tm", 0, 0)
     back = back.reshape(times * frames * share, inner + HEAD_DIM)
@@ -494,16 +511,25 @@
         [whole()] * (2 * RANKS),
         [sds((SPAN * tokens + STAT_ROWS, HEAD_DIM), BF16)] * RANKS,
         [whole()] * RANKS,
-        flops=2 * LONG,
+        flops=4 * SPAN * RANKS * ranks * tokens * tokens * HEAD_DIM,
         nbytes=3 * MIB,
     )
     near = [exchange(part, d) for d, part in enumerate(near)]
 
     space = pltpu.VMEM((RANKS, SPAN * tokens + STAT_ROWS, HEAD_DIM), BF16)
+    far, logs = call(
+        reorder_kernel,
+        (back,),
+        [whole()],
+        (pltpu.VMEM((frames, tokens, inner), BF16), pltpu.VMEM((frames, tokens, HEAD_DIM), F32)),
+        (whole(), whole()),
+        flops=LONG,
+        nbytes=MIB,
+    )
     sent, first = call(
         first_kernel,
-        (place, *near, back),
-        [scalar()] + [whole()] * (RANKS + 1),
+        (place, mark, *near, pinned(far), pinned(logs)),
+        [scalar()] + [whole()] * (RANKS + 3),
         (sds((tokens, inner), BF16), pltpu.VMEM((tokens, inner), BF16)),
         (whole(), whole()),
         nbytes=2 * MIB,
@@ -516,11 +542,12 @@
             place,
             sizes,
             *near,
-            back,
+            pinned(far),
+            pinned(logs),
             pinned(first),
             *[in_hbm(a) for a in (w_out, own, latents, fresh_noise, next_latents)],
         ),
-        [scalar()] * 2 + [whole()] * (RANKS + 2) + [anywhere()] * 5,
+        [scalar()] * 2 + [whole()] * (RANKS + 3) + [anywhere()] * 5,
         (
             pltpu.HBM((frames, tokens, width), BF16),
             pltpu.HBM((frames, tokens, width), BF16),

time: 88.5 us -> 85 us (0.960)
  starting transfers between devices: 45.4 us -> 40.8 us
  local copies, waits for them, and re-layouts: 0.06 us -> 1.55 us
    ppermute x8, starting transfers between devices: 19.6 us -> 17 us  [exchange(): return lax.ppermute(x, ('tm', 'tok'), pairs)]
    all_to_all x1, starting transfers between devices: 9.07 us -> 7.03 us  [body(): lax.all_to_all(back.reshape(times, frames * share, inner + HEAD_DIM), 'tm...]
    ppermute x4, waiting for transfers between devices: 0.01 us -> 1.82 us  [body(): lax.ppermute(part, 'tm', [(i, i ^ 1) for i in range(times)])]
    ppermute x8, waiting for transfers between devices: 7.07 us -> 5.51 us  [exchange(): return lax.ppermute(x, ('tm', 'tok'), pairs)]
    pallas_call x8 -> x10, Pallas kernels: 26.9 us -> 27 us  [call(): pl.pallas_call(kernel, out_shape=outs, in_specs=in_specs, out_specs=out_s...]
  transfers between devices with their start and end apart: 16 -> 16, of which waited for: 6 -> 8; matrix products, arithmetic and copies ran while one was open for 0% -> 1% of each run, Pallas kernels for 25% -> 26%
where the time goes in v4:
time: 85 us; the launch traced here: 84.6 us
  starting transfers between devices  40.8 us (48%)
  Pallas kernels  27 us (32%)
  waiting for transfers between devices  13.5 us (16%)
  between operations  1.68 us (2%)
  local copies, waits for them, and re-layouts  1.55 us (2%)
    pallas_call x10, Pallas kernels, call(): pl.pallas_call(kernel, out_shape=outs, in_specs=in_specs, out_specs=out_s...  27 us
    ppermute x8, starting transfers between devices, exchange(): return lax.ppermute(x, ('tm', 'tok'), pairs)  17 us
    all_to_all x1, starting transfers between devices, body(): lax.all_to_all(outgoing.reshape(times, frames * share, width), 'tm', 0, 0)  11.9 us
    all_to_all x1, starting transfers between devices, body(): lax.all_to_all(back.reshape(times, frames * share, inner + HEAD_DIM), 'tm...  7.03 us
    ppermute x8, waiting for transfers between devices, exchange(): return lax.ppermute(x, ('tm', 'tok'), pairs)  5.51 us
    ppermute x1, waiting for transfers between devices, body(): next_first = lax.ppermute(sent, 'tm', back_perm)  3.13 us
    all_to_all x1, waiting for transfers between devices, body(): lax.all_to_all(outgoing.reshape(times, frames * share, width), 'tm', 0, 0)  3.07 us
    ppermute x1, starting transfers between devices, body(): next_first = lax.ppermute(sent, 'tm', back_perm)  1.92 us
  transfers between devices with their start and end apart: 16, of which 8 were waited for; matrix products, arithmetic and copies ran while one was open for 1% of the time, Pallas kernels for 26%

profile of v4, /device:TPU:5, one launch (start us, length us, event | category | flops | bytes accessed | tf_op | source)
XLA Modules:
  0.0 84.6 jit_solution(6583033582153450412)
XLA Ops:
  0.6 0.0 copy-start.3
  0.6 2.0 %shard_map.122 = (bf16[16,2,8,1536]{3,2,1,0:T(8,128)(2,1)}, bf16[2,128,1536]{2,1,0:T(8,128)(2,1)S(1)}) custom-call(bf16[2,128,1536]{2,1,0:T(8,128)(2,1)} %refs_9_.1), custom_call_target="tpu_custom_call" | custom-call | bytes 2097152 | tf_op jit(solution)/shard_map/pallas_call | solution.py:375
  2.7 11.9 %all-to-all-start = ((bf16[32,8,1536]{2,1,0:T(8,128)(2,1)}), bf16[32,8,1536]{2,1,0:T(8,128)(2,1)S(1)}, u32[]{:S(2)}, u32[]{:S(2)}) async-start(bf16[32,8,1536]{2,1,0:T(8,128)(2,1)} %bitcast.13), calls=%async_computation | async-start | bytes 1572864 | tf_op jit(solution)/shard_map/all_to_all | solution.py:427
  15.3 0.1 pad_add_fusion.place_ref
  15.4 0.0 copy-start
  15.4 0.0 copy-start.2
  15.4 5.9 %shard_map.123 = (f32[3]{0:T(128)S(1)}, f32[16,1536]{1,0:T(8,128)}, bf16[1152,128]{1,0:T(8,128)(2,1)S(1)}, bf16[1152,128]{1,0:T(8,128)(2,1)S(1)}, bf16[1152,128]...) custom-call(s32[64]{0:T(128)S(1)} %copy-done.1, s32[1]{0:T(128)S(6)} %copy.15.offset_ref, f32[32]{0:T(128)S(1)} %copy-done.3, ...), custom_call_target="tpu_custom_call" | custom-call | flops 60000002048 | bytes 10485760 | tf_op jit(solution)/shard_map/pallas_call | solution.py:375
  21.3 3.1 %collective-permute-start.1 = (bf16[1152,128]{1,0:T(8,128)(2,1)S(1)}, bf16[1152,128]{1,0:T(8,128)(2,1)S(1)}, u32[]{:S(2)}, u32[]{:S(2)}) collective-permute-start(bf16[1152,128]{1,0:T(8,128)(2,1)S(1)} %get-tuple-element.53), channel_id=1, source_target_pairs={{0,0},{1,1},{2,2},{3,3},{4,8},{5,9},{6,10},{7,11},{8,4},{9,5},{10,... | collective-permute-start | bytes 884744 | tf_op jit(solution)/shard_map/ppermute | solution.py:416
  24.4 1.7 %collective-permute-start.2 = (bf16[1152,128]{1,0:T(8,128)(2,1)S(1)}, bf16[1152,128]{1,0:T(8,128)(2,1)S(1)}, u32[]{:S(2)}, u32[]{:S(2)}) collective-permute-start(bf16[1152,128]{1,0:T(8,128)(2,1)S(1)} %get-tuple-element.54), channel_id=1, source_target_pairs={{0,1},{1,0},{2,3},{3,2},{4,9},{5,8},{6,11},{7,10},{8,5},{9,4},{10,... | collective-permute-start | bytes 884744 | tf_op jit(solution)/shard_map/ppermute | solution.py:416
  26.1 3.5 %collective-permute-start.3 = (bf16[1152,128]{1,0:T(8,128)(2,1)S(1)}, bf16[1152,128]{1,0:T(8,128)(2,1)S(1)}, u32[]{:S(2)}, u32[]{:S(2)}) collective-permute-start(bf16[1152,128]{1,0:T(8,128)(2,1)S(1)} %get-tuple-element.55), channel_id=1, source_target_pairs={{0,2},{1,3},{2,0},{3,1},{4,10},{5,11},{6,8},{7,9},{8,6},{9,7},{10,... | collective-permute-start | bytes 884744 | tf_op jit(solution)/shard_map/ppermute | solution.py:416
  29.6 0.2 collective-permute-start.4
  29.8 0.8 slice_bitcast_fusion
  30.6 1.9 %collective-permute-start = (bf16[128,1536]{1,0:T(8,128)(2,1)}, bf16[128,1536]{1,0:T(8,128)(2,1)S(1)}, u32[]{:S(2)}, u32[]{:S(2)}) collective-permute-start(bf16[128,1536]{1,0:T(8,128)(2,1)} %slice_bitcast_fusion), channel_id=1, source_target_pairs={{8,0},{16,8},{24,16},{32,24},{40,32},{48,40},{56,48},{64,56},{72,6... | collective-permute-start | bytes 1179656 | tf_op jit(solution)/shard_map/ppermute | solution.py:480
  32.5 1.9 %shard_map.124 = (f32[32,2,1536]{2,1,0:T(2,128)}, f32[32,2,1536]{2,1,0:T(2,128)}, f32[256,256]{1,0:T(8,128)}) custom-call(s32[64]{0:T(128)S(1)} %copy-done.1, s32[1]{0:T(128)S(6)} %copy.15.offset_ref, s32[64]{0:T(128)S(1)} %copy-done.2, f32[3,32,1536]{2,1,0:T(8,128)S(1)} %bitcast.10), custom_call_target="tpu_custom_call" | custom-call | bytes 262144 | tf_op jit(solution)/shard_map/pallas_call | solution.py:375
  34.4 3.1 %all-to-all-done.x_ref = bf16[32,8,1536]{2,1,0:T(8,128)(2,1)S(1)} async-done(((bf16[32,8,1536]{2,1,0:T(8,128)(2,1)}), bf16[32,8,1536]{2,1,0:T(8,128)(2,1)S(1)}, u32[]{:S(2)}, u32[]{:S(2)}) %all-to-all-start) | async-done | bytes 786464 | tf_op jit(solution)/shard_map/all_to_all | solution.py:427
  37.5 6.6 %shard_map.125 = bf16[256,896]{1,0:T(8,128)(2,1)} custom-call(bf16[32,8,1536]{2,1,0:T(8,128)(2,1)S(1)} %all-to-all-done.x_ref, f32[32,2,1536]{2,1,0:T(2,128)} %get-tuple-element.49.refs_0_, f32[32,2,1536]{2,1,0:T(2,128)} %get-tuple-element.50.refs_1_, bf16[1536,768]{1,0:T(8,128)(2,1)} %refs_2_.1, bf16[1536,768]{1,0:T(8,128)(2,1)} %refs_3_.1, ...), custom_call_target="tpu_custom_call" | custom-call | flops 60000002048 | bytes 10485760 | tf_op jit(solution)/shard_map/pallas_call | solution.py:375
  44.1 7.0 %all-to-all-start.1 = ((bf16[32,8,896]{2,1,0:T(8,128)(2,1)}), bf16[32,8,896]{2,1,0:T(8,128)(2,1)S(1)}, u32[]{:S(2)}, u32[]{:S(2)}) async-start(bf16[32,8,896]{2,1,0:T(8,128)(2,1)} %bitcast.14), calls=%async_computation.1 | async-start | bytes 917504 | tf_op jit(solution)/shard_map/all_to_all | solution.py:505
  51.2 0.0 collective-permute-done.1.refs_0_
  51.2 0.0 collective-permute-done.2.refs_1_
  51.2 0.0 collective-permute-done.3.refs_2_
  51.2 0.0 collective-permute-done.4.refs_3_
  51.2 0.0 collective-permute-done.refs_11_
  51.2 0.0 copy-start.5
  51.2 0.7 copy-done.5
  52.0 0.4 collective-permute-start.5
  52.3 0.1 collective-permute-start.6
  52.5 0.4 collective-permute-start.7
  52.8 0.1 collective-permute-start.8
  53.0 0.6 collective-permute-done.5.refs_4_
  53.5 0.4 collective-permute-done.6.refs_5_
  54.0 0.4 collective-permute-done.7.refs_6_
  54.4 0.4 collective-permute-done.8.refs_7_
  54.8 3.3 %shard_map.127 = (bf16[400,128]{1,0:T(8,128)(2,1)S(1)}, bf16[400,128]{1,0:T(8,128)(2,1)S(1)}, bf16[400,128]{1,0:T(8,128)(2,1)S(1)}, bf16[400,128]{1,0:T(8,128)(2,1)S(1)}) custom-call(bf16[1152,128]{1,0:T(8,128)(2,1)S(1)} %collective-permute-done.1.refs_0_, bf16[1152,128]{1,0:T(8,128)(2,1)S(1)} %collective-permute-done.2.refs_1_, ...), custom_call_target="tpu_custom_call" | custom-call | flops 805306368 | bytes 3145728 | tf_op jit(solution)/shard_map/pallas_call | solution.py:375
  58.1 2.9 %collective-permute-start.9 = (bf16[400,128]{1,0:T(8,128)(2,1)S(1)}, bf16[400,128]{1,0:T(8,128)(2,1)S(1)}, u32[]{:S(2)}, u32[]{:S(2)}) collective-permute-start(bf16[400,128]{1,0:T(8,128)(2,1)S(1)} %get-tuple-element.66), channel_id=1, source_target_pairs={{0,0},{1,1},{2,2},{3,3},{4,8},{5,9},{6,10},{7,11},{8,4},{9,5},{10,... | collective-permute-start | bytes 307208 | tf_op jit(solution)/shard_map/ppermute | solution.py:416
  60.9 0.7 collective-permute-start.10
  61.6 4.5 %collective-permute-start.11 = (bf16[400,128]{1,0:T(8,128)(2,1)S(1)}, bf16[400,128]{1,0:T(8,128)(2,1)S(1)}, u32[]{:S(2)}, u32[]{:S(2)}) collective-permute-start(bf16[400,128]{1,0:T(8,128)(2,1)S(1)} %get-tuple-element.68), channel_id=1, source_target_pairs={{0,2},{1,3},{2,0},{3,1},{4,10},{5,11},{6,8},{7,9},{8,6},{9,7},{10,... | collective-permute-start | bytes 307208 | tf_op jit(solution)/shard_map/ppermute | solution.py:416
  66.1 0.4 collective-permute-start.12
  66.6 0.0 all-to-all-done.1
  66.6 0.2 shard_map.128
  66.8 0.0 collective-permute-done.9.refs_0_
  66.8 0.0 collective-permute-done.10.refs_1_
  66.8 2.8 %collective-permute-done.11.refs_2_ = bf16[400,128]{1,0:T(8,128)(2,1)S(1)} collective-permute-done((bf16[400,128]{1,0:T(8,128)(2,1)S(1)}, bf16[400,128]{1,0:T(8,128)(2,1)S(1)}, u32[]{:S(2)}, u32[]{:S(2)}) %collective-permute-start.11) | collective-permute-done | bytes 102432 | tf_op jit(solution)/shard_map/ppermute | solution.py:416
  69.7 2.6 %collective-permute-done.12.refs_3_ = bf16[400,128]{1,0:T(8,128)(2,1)S(1)} collective-permute-done((bf16[400,128]{1,0:T(8,128)(2,1)S(1)}, bf16[400,128]{1,0:T(8,128)(2,1)S(1)}, u32[]{:S(2)}, u32[]{:S(2)}) %collective-permute-start.12) | collective-permute-done | bytes 102432 | tf_op jit(solution)/shard_map/ppermute | solution.py:416
  72.3 1.0 %shard_map.129 = (bf16[128,768]{1,0:T(8,128)(2,1)S(1)}, bf16[128,768]{1,0:T(8,128)(2,1)S(1)}) custom-call(s32[3]{0:T(128)S(1)} %pad_add_fusion.place_ref, f32[1,32]{1,0:T(1,128)S(1)} %shard_map.126.mark_ref, bf16[400,128]{1,0:T(8,128)(2,1)S(1)} %collective-permute-done.9.refs_0_, bf16[400,128]{1,0:T(8,128)(2,1)S(1)} %collective-permute-done.10.refs_1_, ...), custom_call_target="tpu_custom_call" | custom-call | bytes 2097152 | tf_op jit(solution)/shard_map/pallas_call | solution.py:375
  73.4 1.9 %collective-permute-start.13 = (bf16[128,768]{1,0:T(8,128)(2,1)S(1)}, bf16[128,768]{1,0:T(8,128)(2,1)S(1)}, u32[]{:S(2)}, u32[]{:S(2)}) collective-permute-start(bf16[128,768]{1,0:T(8,128)(2,1)S(1)} %get-tuple-element.77), channel_id=1, source_target_pairs={{8,0},{16,8},{24,16},{32,24},{40,32},{48,40},{56,48},{64,56},{72,6... | collective-permute-start | bytes 589832 | tf_op jit(solution)/shard_map/ppermute | solution.py:538
  75.3 4.3 %shard_map.130 = (bf16[2,128,1536]{2,1,0:T(8,128)(2,1)}, bf16[2,128,1536]{2,1,0:T(8,128)(2,1)}, bf16[768,1536]{1,0:T(8,128)(2,1)S(1)}, f32[16,1536]{1,0:T(8,128)S(1)}, bf16[128,1536]{1,0:T(8,128)(2,1)S(1)}) custom-call(s32[3]{0:T(128)S(1)} %pad_add_fusion.place_ref, f32[3]{0:T(128)S(1)} %get-tuple-element.45.size_ref, ...), custom_call_target="tpu_custom_call" | custom-call | flops 603979776 | bytes 6291456 | tf_op jit(solution)/shard_map/pallas_call | solution.py:375
  79.6 3.1 %collective-permute-done.13.att_ref = bf16[128,768]{1,0:T(8,128)(2,1)S(1)} collective-permute-done((bf16[128,768]{1,0:T(8,128)(2,1)S(1)}, bf16[128,768]{1,0:T(8,128)(2,1)S(1)}, u32[]{:S(2)}, u32[]{:S(2)}) %collective-permute-start.13) | collective-permute-done | bytes 196640 | tf_op jit(solution)/shard_map/ppermute | solution.py:538
  82.7 1.7 %shard_map.131 = bf16[2,128,1536]{2,1,0:T(8,128)(2,1)} custom-call(f32[3]{0:T(128)S(1)} %get-tuple-element.45.size_ref, bf16[128,768]{1,0:T(8,128)(2,1)S(1)} %collective-permute-done.13.att_ref, bf16[768,1536]{1,0:T(8,128)(2,1)S(1)} %get-tuple-element.78.wo_ref, f32[16,1536]{1,0:T(8,128)S(1)} %get-tuple-element.79.own_ref, ...), custom_call_target="tpu_custom_call", output_to_operand_aliasing={{}: (5, {})} | custom-call | flops 301989888 | bytes 4194304 | tf_op jit(solution)/shard_map/pallas_call | solution.py:375
  (8 shorter events, 0.0 us)
Async XLA Ops:
  0.6 14.7 %copy-start.3 = (f32[32]{0:T(128)S(1)}, f32[32]{0:T(128)}, u32[]{:S(2)}) copy-start(f32[32]{0:T(128)} %step_ref.1) | copy-start | bytes 388
  0.6 14.7 %copy-start.1 = (s32[64]{0:T(128)S(1)}, s32[64]{0:T(128)}, u32[]{:S(2)}) copy-start(s32[64]{0:T(128)} %noise_ref.2) | copy-start | bytes 772
  2.7 34.8 %all-to-all-start = ((bf16[32,8,1536]{2,1,0:T(8,128)(2,1)}), bf16[32,8,1536]{2,1,0:T(8,128)(2,1)S(1)}, u32[]{:S(2)}, u32[]{:S(2)}) async-start(bf16[32,8,1536]{2,1,0:T(8,128)(2,1)} %bitcast.13), calls=%async_computation | async-start | bytes 1572864 | tf_op jit(solution)/shard_map/all_to_all | solution.py:427
  15.4 14.5 %copy-start.4 = (bf16[2,128,1536]{2,1,0:T(8,128)(2,1)S(1)}, bf16[2,128,1536]{2,1,0:T(8,128)(2,1)}, u32[]{:S(2)}) copy-start(bf16[2,128,1536]{2,1,0:T(8,128)(2,1)} %refs_9_.1) | copy-start | bytes 2359300
  15.4 17.1 %copy-start = (f32[32,3,1536]{2,0,1:T(8,128)S(1)}, f32[32,3,1536]{2,0,1:T(8,128)}, u32[]{:S(2)}) copy-start(f32[32,3,1536]{2,0,1:T(8,128)} %param.16) | copy-start | bytes 1769476
  15.4 17.1 %copy-start.2 = (s32[64]{0:T(128)S(1)}, s32[64]{0:T(128)}, u32[]{:S(2)}) copy-start(s32[64]{0:T(128)} %blocks_ref.1) | copy-start | bytes 772
  21.3 29.9 %collective-permute-start.1 = (bf16[1152,128]{1,0:T(8,128)(2,1)S(1)}, bf16[1152,128]{1,0:T(8,128)(2,1)S(1)}, u32[]{:S(2)}, u32[]{:S(2)}) collective-permute-start(bf16[1152,128]{1,0:T(8,128)(2,1)S(1)} %get-tuple-element.53), channel_id=1, source_target_pairs={{0,0},{1,1},{2,2},{3,3},{4,8},{5,9},{6,10},{7,11},{8,4},{9,5},{10,... | collective-permute-start | bytes 884744 | tf_op jit(solution)/shard_map/ppermute | solution.py:416
  24.4 26.8 %collective-permute-start.2 = (bf16[1152,128]{1,0:T(8,128)(2,1)S(1)}, bf16[1152,128]{1,0:T(8,128)(2,1)S(1)}, u32[]{:S(2)}, u32[]{:S(2)}) collective-permute-start(bf16[1152,128]{1,0:T(8,128)(2,1)S(1)} %get-tuple-element.54), channel_id=1, source_target_pairs={{0,1},{1,0},{2,3},{3,2},{4,9},{5,8},{6,11},{7,10},{8,5},{9,4},{10,... | collective-permute-start | bytes 884744 | tf_op jit(solution)/shard_map/ppermute | solution.py:416
  26.1 25.1 %collective-permute-start.3 = (bf16[1152,128]{1,0:T(8,128)(2,1)S(1)}, bf16[1152,128]{1,0:T(8,128)(2,1)S(1)}, u32[]{:S(2)}, u32[]{:S(2)}) collective-permute-start(bf16[1152,128]{1,0:T(8,128)(2,1)S(1)} %get-tuple-element.55), channel_id=1, source_target_pairs={{0,2},{1,3},{2,0},{3,1},{4,10},{5,11},{6,8},{7,9},{8,6},{9,7},{10,... | collective-permute-start | bytes 884744 | tf_op jit(solution)/shard_map/ppermute | solution.py:416
  29.6 21.6 %collective-permute-start.4 = (bf16[1152,128]{1,0:T(8,128)(2,1)S(1)}, bf16[1152,128]{1,0:T(8,128)(2,1)S(1)}, u32[]{:S(2)}, u32[]{:S(2)}) collective-permute-start(bf16[1152,128]{1,0:T(8,128)(2,1)S(1)} %get-tuple-element.56), channel_id=1, source_target_pairs={{0,3},{1,2},{2,1},{3,0},{4,11},{5,10},{6,9},{7,8},{8,7},{9,6},{10,... | collective-permute-start | bytes 884744 | tf_op jit(solution)/shard_map/ppermute | solution.py:416
  30.6 20.6 %collective-permute-start = (bf16[128,1536]{1,0:T(8,128)(2,1)}, bf16[128,1536]{1,0:T(8,128)(2,1)S(1)}, u32[]{:S(2)}, u32[]{:S(2)}) collective-permute-start(bf16[128,1536]{1,0:T(8,128)(2,1)} %slice_bitcast_fusion), channel_id=1, source_target_pairs={{8,0},{16,8},{24,16},{32,24},{40,32},{48,40},{56,48},{64,56},{72,6... | collective-permute-start | bytes 1179656 | tf_op jit(solution)/shard_map/ppermute | solution.py:480
  44.1 22.5 %all-to-all-start.1 = ((bf16[32,8,896]{2,1,0:T(8,128)(2,1)}), bf16[32,8,896]{2,1,0:T(8,128)(2,1)S(1)}, u32[]{:S(2)}, u32[]{:S(2)}) async-start(bf16[32,8,896]{2,1,0:T(8,128)(2,1)} %bitcast.14), calls=%async_computation.1 | async-start | bytes 917504 | tf_op jit(solution)/shard_map/all_to_all | solution.py:505
  51.2 0.8 copy-start.5
  52.0 1.6 %collective-permute-start.5 = (bf16[1152,128]{1,0:T(8,128)(2,1)S(1)}, bf16[1152,128]{1,0:T(8,128)(2,1)S(1)}, u32[]{:S(2)}, u32[]{:S(2)}) collective-permute-start(bf16[1152,128]{1,0:T(8,128)(2,1)S(1)} %collective-permute-done.1.refs_0_), channel_id=1, source_target_pairs={{0,8},{8,0},{16,24},{24,16},{32,40},{40,32},{48,56},{56,48},{64,72... | collective-permute-start | bytes 884744 | tf_op jit(solution)/shard_map/ppermute | solution.py:504
  52.3 1.6 %collective-permute-start.6 = (bf16[1152,128]{1,0:T(8,128)(2,1)S(1)}, bf16[1152,128]{1,0:T(8,128)(2,1)S(1)}, u32[]{:S(2)}, u32[]{:S(2)}) collective-permute-start(bf16[1152,128]{1,0:T(8,128)(2,1)S(1)} %collective-permute-done.2.refs_1_), channel_id=1, source_target_pairs={{0,8},{8,0},{16,24},{24,16},{32,40},{40,32},{48,56},{56,48},{64,72... | collective-permute-start | bytes 884744 | tf_op jit(solution)/shard_map/ppermute | solution.py:504
  52.5 1.9 %collective-permute-start.7 = (bf16[1152,128]{1,0:T(8,128)(2,1)S(1)}, bf16[1152,128]{1,0:T(8,128)(2,1)S(1)}, u32[]{:S(2)}, u32[]{:S(2)}) collective-permute-start(bf16[1152,128]{1,0:T(8,128)(2,1)S(1)} %collective-permute-done.3.refs_2_), channel_id=1, source_target_pairs={{0,8},{8,0},{16,24},{24,16},{32,40},{40,32},{48,56},{56,48},{64,72... | collective-permute-start | bytes 884744 | tf_op jit(solution)/shard_map/ppermute | solution.py:504
  52.8 2.0 %collective-permute-start.8 = (bf16[1152,128]{1,0:T(8,128)(2,1)S(1)}, bf16[1152,128]{1,0:T(8,128)(2,1)S(1)}, u32[]{:S(2)}, u32[]{:S(2)}) collective-permute-start(bf16[1152,128]{1,0:T(8,128)(2,1)S(1)} %collective-permute-done.4.refs_3_), channel_id=1, source_target_pairs={{0,8},{8,0},{16,24},{24,16},{32,40},{40,32},{48,56},{56,48},{64,72... | collective-permute-start | bytes 884744 | tf_op jit(solution)/shard_map/ppermute | solution.py:504
  58.1 8.7 %collective-permute-start.9 = (bf16[400,128]{1,0:T(8,128)(2,1)S(1)}, bf16[400,128]{1,0:T(8,128)(2,1)S(1)}, u32[]{:S(2)}, u32[]{:S(2)}) collective-permute-start(bf16[400,128]{1,0:T(8,128)(2,1)S(1)} %get-tuple-element.66), channel_id=1, source_target_pairs={{0,0},{1,1},{2,2},{3,3},{4,8},{5,9},{6,10},{7,11},{8,4},{9,5},{10,... | collective-permute-start | bytes 307208 | tf_op jit(solution)/shard_map/ppermute | solution.py:416
  60.9 5.9 %collective-permute-start.10 = (bf16[400,128]{1,0:T(8,128)(2,1)S(1)}, bf16[400,128]{1,0:T(8,128)(2,1)S(1)}, u32[]{:S(2)}, u32[]{:S(2)}) collective-permute-start(bf16[400,128]{1,0:T(8,128)(2,1)S(1)} %get-tuple-element.67), channel_id=1, source_target_pairs={{0,1},{1,0},{2,3},{3,2},{4,9},{5,8},{6,11},{7,10},{8,5},{9,4},{10,... | collective-permute-start | bytes 307208 | tf_op jit(solution)/shard_map/ppermute | solution.py:416
  61.6 8.0 %collective-permute-start.11 = (bf16[400,128]{1,0:T(8,128)(2,1)S(1)}, bf16[400,128]{1,0:T(8,128)(2,1)S(1)}, u32[]{:S(2)}, u32[]{:S(2)}) collective-permute-start(bf16[400,128]{1,0:T(8,128)(2,1)S(1)} %get-tuple-element.68), channel_id=1, source_target_pairs={{0,2},{1,3},{2,0},{3,1},{4,10},{5,11},{6,8},{7,9},{8,6},{9,7},{10,... | collective-permute-start | bytes 307208 | tf_op jit(solution)/shard_map/ppermute | solution.py:416
  66.1 6.2 %collective-permute-start.12 = (bf16[400,128]{1,0:T(8,128)(2,1)S(1)}, bf16[400,128]{1,0:T(8,128)(2,1)S(1)}, u32[]{:S(2)}, u32[]{:S(2)}) collective-permute-start(bf16[400,128]{1,0:T(8,128)(2,1)S(1)} %get-tuple-element.69), channel_id=1, source_target_pairs={{0,3},{1,2},{2,1},{3,0},{4,11},{5,10},{6,9},{7,8},{8,7},{9,6},{10,... | collective-permute-start | bytes 307208 | tf_op jit(solution)/shard_map/ppermute | solution.py:416
  73.4 9.4 %collective-permute-start.13 = (bf16[128,768]{1,0:T(8,128)(2,1)S(1)}, bf16[128,768]{1,0:T(8,128)(2,1)S(1)}, u32[]{:S(2)}, u32[]{:S(2)}) collective-permute-start(bf16[128,768]{1,0:T(8,128)(2,1)S(1)} %get-tuple-element.77), channel_id=1, source_target_pairs={{8,0},{16,8},{24,16},{32,24},{40,32},{48,40},{56,48},{64,56},{72,6... | collective-permute-start | bytes 589832 | tf_op jit(solution)/shard_map/ppermute | solution.py:538

commit v5 on v4

--- a/solution.py
+++ b/solution.py
@@ -136,8 +136,14 @@
     own_store.wait()
 
 
-def column_kernel(noise_ref, offset_ref, blocks_ref, table_ref, shift_hbm, scale_hbm, bias_hbm, *refs):
-    shift_ref, scale_ref, bias_ref, sems = refs
+def column_kernel(noise_ref, offset_ref, blocks_ref, table_ref, *refs):
+    count = 1
+    sources, (shift_hbm, scale_hbm, bias_hbm), refs = refs[:count], refs[count : count + 3], refs[count + 3 :]
+    held, (shift_ref, scale_ref, bias_ref, sems, load_sems) = refs[:count], refs[count:]
+    loads = []
+    for n, (src, dst) in enumerate(zip(sources, held)):
+        loads.append(pltpu.make_async_copy(src, dst, load_sems.at[n]))
+        loads[n].start()
     total = noise_ref.shape[0]
     frames = shift_ref.shape[1]
     share = bias_ref.shape[0] // total
@@ -164,8 +170,8 @@
     allowed = (down % share == along % share) & (down != along) & (block <= jnp.transpose(block))
     bias_ref[...] = jnp.where(allowed, 0.0, MASKED)
     stores[2].start()
-    for store in stores:
-        store.wait()
+    for copy in stores + loads:
+        copy.wait()
 
 
 def pass_kernel(in_ref, out_ref):
@@ -196,14 +202,15 @@
         outs[d][SPAN * tokens : SPAN * tokens + STAT_ROWS] = turned.astype(BF16)
 
 
-def temporal_kernel(x_ref, *refs):
-    scale_hbm, shift_hbm, wq_hbm, wk_hbm, bias_hbm, wv_hbm, out_hbm = refs[:7]
-    scale_ref, shift_ref, wq_ref, wk_ref, bias_ref, wv_ref, out_ref, sems, out_sems = refs[7:]
-    held = (scale_ref, shift_ref, wq_ref, wk_ref, bias_ref, wv_ref)
-    loads = []
-    for n, (src, dst) in enumerate(zip(refs[:6], held)):
-        loads.append(pltpu.make_async_copy(src, dst, sems.at[n]))
-        loads[n].start()
+def temporal_kernel(x_ref, wq_ref, *refs):
+    scale_hbm, shift_hbm, wk_hbm, bias_hbm, wv_hbm, out_hbm = refs[:6]
+    scale_ref, shift_ref, wk_ref, bias_ref, wv_ref, out_ref, sems, out_sems = refs[6:]
+    loads = {}
+    for n, (name, src, dst) in enumerate((
+        ("scale", scale_hbm, scale_ref), ("shift", shift_hbm, shift_ref), ("wk", wk_hbm, wk_ref), ("bias", bias_hbm, bias_ref), ("wv", wv_hbm, wv_ref),
+    )):
+        loads[name] = pltpu.make_async_copy(src, dst, sems.at[n])
+        loads[name].start()
     groups, rows, width = x_ref.shape
     low = lax.broadcasted_iota(jnp.int32, (groups, rows, width), 1) < rows // 2
 
@@ -211,20 +218,19 @@
         first = jnp.broadcast_to(ref[:, 0:1, :], low.shape)
         return jnp.where(low, first, jnp.broadcast_to(ref[:, 1:2, :], low.shape))
 
-    loads[0].wait()
-    loads[1].wait()
+    loads["scale"].wait()
+    loads["shift"].wait()
     normed = normalise(x_ref[...].astype(F32), spread(scale_ref), spread(shift_ref))
     normed = normed.reshape(groups * rows, width)
-    loads[2].wait()
     q = matmul(normed, wq_ref[...]).astype(BF16)
-    loads[3].wait()
+    loads["wk"].wait()
     k = matmul(normed, wk_ref[...]).astype(BF16)
-    loads[4].wait()
+    loads["bias"].wait()
     lane = lax.broadcasted_iota(jnp.int32, (groups * rows, HEAD_DIM), 1)
     stats = jnp.zeros((groups * rows, HEAD_DIM), F32)
     heads = [slice(h * HEAD_DIM, (h + 1) * HEAD_DIM) for h in range(HEADS)]
     parts = [softmax_parts(q[:, own], k[:, own], bias_ref[...]) for own in heads]
-    loads[5].wait()
+    loads["wv"].wait()
     v = matmul(normed, wv_ref[...]).astype(BF16)
     copies = []
 
@@ -245,7 +251,11 @@
         copy.wait()
 
 
-def reorder_kernel(time_ref, far_ref, logs_ref):
+def reorder_kernel(time_ref, wo_hbm, own_hbm, far_ref, logs_ref, wo_ref, own_ref, sems):
+    loads = []
+    for n, (src, dst) in enumerate(((wo_hbm, wo_ref), (own_hbm, own_ref))):
+        loads.append(pltpu.make_async_copy(src, dst, sems.at[n]))
+        loads[n].start()
     frames, tokens, inner = far_ref.shape
     width = time_ref.shape[1]
     turned = time_ref[...].astype(F32).reshape(tokens // 8, 2, 8, width)
@@ -254,6 +264,8 @@
         far_ref[f] = rows[:, :inner].astype(BF16)
         stats = rows[:, inner:]
         logs_ref[f, :, 0:8] = stats[:, 0:8] + stats[:, 8:16] + stats[:, 16:24]
+    for load in loads:
+        load.wait()
 
 
 def merged(f, rank, near_refs, far_ref, logs_ref, space_ref, out_ref):
@@ -288,15 +300,13 @@
 
 def project_kernel(place_ref, size_ref, *refs):
     near_refs = refs[:RANKS]
-    far_ref, logs_ref, first_ref, wo_hbm, own_hbm, x_hbm, fresh_hbm, in_hbm_ref = refs[RANKS : RANKS + 8]
-    vel_hbm, next_hbm, wo_ref, own_ref, base_ref = refs[RANKS + 8 : RANKS + 13]
-    space_ref, second_ref, x_ref, fresh_ref, vel_ref, next_ref, sems, vel_sems, next_sems = refs[RANKS + 13 :]
+    far_ref, logs_ref, first_ref, wo_ref, own_ref, x_hbm, fresh_hbm, in_hbm_ref = refs[RANKS : RANKS + 8]
+    vel_hbm, next_hbm, base_ref = refs[RANKS + 8 : RANKS + 11]
+    space_ref, second_ref, x_ref, fresh_ref, vel_ref, next_ref, sems, vel_sems, next_sems = refs[RANKS + 11 :]
     frames, tokens, _ = x_ref.shape
     loads = []
     for n, (src, dst) in enumerate(
         (
-            (wo_hbm, wo_ref),
-            (own_hbm, own_ref),
             (x_hbm, x_ref),
             (in_hbm_ref, base_ref),
             (fresh_hbm, fresh_ref),
@@ -467,33 +477,36 @@
         pltpu.VMEM((total * share, total * share), F32),
     )
     table, noise_levels, sizes = lax.optimization_barrier((table, noise_levels, sizes))
-    shifts, scales, bias = call(
+    shifts, scales, bias, *fetched = call(
         column_kernel,
-        (noise_levels, offset, block_ids, table),
-        [scalar()] * 3 + [whole()],
-        tuple(pltpu.HBM(a.inner_aval.shape, F32) for a in small[1:]),
-        (anywhere(),) * 3,
+        (noise_levels, offset, block_ids, table, *[in_hbm(a) for a in (w_query, w_key, w_value)[:1]]),
+        [scalar()] * 3 + [whole()] + [anywhere()] * 1,
+        (
+            *[pltpu.HBM(a.inner_aval.shape, F32) for a in small[1:]],
+            *[pltpu.VMEM((width, inner), BF16)] * 1,
+        ),
+        (*[anywhere()] * 3, *[whole()] * 1),
         nbytes=MIB // 4,
-        scratch_shapes=[*small[1:], dma((3,))],
+        scratch_shapes=[*small[1:], dma((3,)), dma((1,))],
     )
     incoming, sizes = lax.optimization_barrier((latents[0], sizes))
     next_latents = lax.ppermute(incoming, "tm", back_perm)
 
     back = call(
         temporal_kernel,
-        (column, *[in_hbm(a) for a in (scales, shifts, w_query, w_key, bias, w_value)]),
-        [whole()] + [anywhere()] * 6,
+        (column, *[pinned(a) for a in fetched], *[in_hbm(a) for a in (scales, shifts, w_key, bias, w_value)]),
+        [whole()] * 2 + [anywhere()] * 5,
         pltpu.HBM((total * share, inner + HEAD_DIM), BF16),
         anywhere(),
         flops=LONG,
         nbytes=10 * MIB,
         scratch_shapes=[
             *small[1:3],
-            *[pltpu.VMEM((width, inner), BF16)] * 2,
+            *[pltpu.VMEM((width, inner), BF16)] * 1,
             small[3],
-            pltpu.VMEM((width, inner), BF16),
+            *[pltpu.VMEM((width, inner), BF16)] * 1,
             pltpu.VMEM((total * share, inner + HEAD_DIM), BF16),
-            dma((6,)),
+            dma((5,)),
             dma((HEADS + 1,)),
         ],
     )
@@ -517,12 +530,18 @@
     near = [exchange(part, d) for d, part in enumerate(near)]
 
     space = pltpu.VMEM((RANKS, SPAN * tokens + STAT_ROWS, HEAD_DIM), BF16)
-    far, logs = call(
+    far, logs, wo, own = call(
         reorder_kernel,
-        (back,),
-        [whole()],
-        (pltpu.VMEM((frames, tokens, inner), BF16), pltpu.VMEM((frames, tokens, HEAD_DIM), F32)),
-        (whole(), whole()),
+        (back, in_hbm(w_out), in_hbm(own)),
+        [whole()] + [anywhere()] * 2,
+        (
+            pltpu.VMEM((frames, tokens, inner), BF16),
+            pltpu.VMEM((frames, tokens, HEAD_DIM), F32),
+            pltpu.VMEM((inner, width), BF16),
+            pltpu.VMEM((16, width), F32),
+        ),
+        (whole(),) * 4,
+        scratch_shapes=[dma((2,))],
         flops=LONG,
         nbytes=MIB,
     )
@@ -536,7 +555,7 @@
         scratch_shapes=[space],
     )
     next_first = lax.ppermute(sent, "tm", back_perm)
-    velocity, following, wo, own, base = call(
+    velocity, following, base = call(
         project_kernel,
         (
             place,
@@ -545,17 +564,17 @@
             pinned(far),
             pinned(logs),
             pinned(first),
-            *[in_hbm(a) for a in (w_out, own, latents, fresh_noise, next_latents)],
+            pinned(wo),
+            pinned(own),
+            *[in_hbm(a) for a in (latents, fresh_noise, next_latents)],
         ),
-        [scalar()] * 2 + [whole()] * (RANKS + 3) + [anywhere()] * 5,
+        [scalar()] * 2 + [whole()] * (RANKS + 5) + [anywhere()] * 3,
         (
             pltpu.HBM((frames, tokens, width), BF16),
             pltpu.HBM((frames, tokens, width), BF16),
-            pltpu.VMEM((inner, width), BF16),
-            pltpu.VMEM((16, width), F32),
             pltpu.VMEM((tokens, width), BF16),
         ),
-        (anywhere(), anywhere(), whole(), whole(), whole()),
+        (anywhere(), anywhere(), whole()),
         flops=project_flops,
         nbytes=6 * MIB,
         scratch_shapes=[
@@ -565,7 +584,7 @@
             pltpu.VMEM((tokens, width), BF16),
             pltpu.VMEM((frames, tokens, width), BF16),
             pltpu.VMEM((frames - 1, tokens, width), BF16),
-            dma((5,)),
+            dma((3,)),
             *[dma((3,))] * 2,
         ],
     )

time: 85 us -> 84.9 us (level)
  waiting for transfers between devices: 13.5 us -> 8.87 us
  Pallas kernels: 27 us -> 29.9 us
  starting transfers between devices: 40.8 us -> 43 us
    ppermute x8, waiting for transfers between devices: 5.51 us -> 2.27 us  [exchange(): return lax.ppermute(x, ('tm', 'tok'), pairs)]
    pallas_call x10, Pallas kernels: 27 us -> 29.9 us  [call(): pl.pallas_call(kernel, out_shape=outs, in_specs=in_specs, out_specs=out_s...]
    all_to_all x1, waiting for transfers between devices: 3.07 us -> 1.24 us  [body(): lax.all_to_all(outgoing.reshape(times, frames * share, width), 'tm', 0, 0)]
    all_to_all x1, starting transfers between devices: 7.03 us -> 8.31 us  [body(): lax.all_to_all(back.reshape(times, frames * share, inner + HEAD_DIM), 'tm...]
  transfers between devices with their start and end apart: 16 -> 16, of which waited for: 8 -> 8; matrix products, arithmetic and copies ran while one was open for 1% -> 1% of each run, Pallas kernels for 26% -> 30%
where the time goes in v5:
time: 84.9 us; the launch traced here: 84.4 us
  starting transfers between devices  43 us (51%)
  Pallas kernels  29.9 us (35%)
  waiting for transfers between devices  8.87 us (10%)
  between operations  1.68 us (2%)
    pallas_call x10, Pallas kernels, call(): pl.pallas_call(kernel, out_shape=outs, in_specs=in_specs, out_specs=out_s...  29.9 us
    ppermute x8, starting transfers between devices, exchange(): return lax.ppermute(x, ('tm', 'tok'), pairs)  17 us
    all_to_all x1, starting transfers between devices, body(): lax.all_to_all(outgoing.reshape(times, frames * share, width), 'tm', 0, 0)  11.9 us
    all_to_all x1, starting transfers between devices, body(): lax.all_to_all(back.reshape(times, frames * share, inner + HEAD_DIM), 'tm...  8.31 us
    ppermute x1, waiting for transfers between devices, body(): next_first = lax.ppermute(sent, 'tm', back_perm)  3.33 us
    ppermute x1, starting transfers between devices, body(): next_first = lax.ppermute(sent, 'tm', back_perm)  2.49 us
    ppermute x8, waiting for transfers between devices, exchange(): return lax.ppermute(x, ('tm', 'tok'), pairs)  2.27 us
    ppermute x1, starting transfers between devices, body(): next_latents = lax.ppermute(incoming, 'tm', back_perm)  2.26 us
  transfers between devices with their start and end apart: 16, of which 8 were waited for; matrix products, arithmetic and copies ran while one was open for 1% of the time, Pallas kernels for 30%

profile of v5, /device:TPU:5, one launch (start us, length us, event | category | flops | bytes accessed | tf_op | source)
XLA Modules:
  0.0 84.4 jit_solution(13190082591170747564)
XLA Ops:
  0.6 0.0 copy-start.1
  0.6 0.0 copy-start.3
  0.6 2.0 %shard_map.122 = (bf16[16,2,8,1536]{3,2,1,0:T(8,128)(2,1)}, bf16[2,128,1536]{2,1,0:T(8,128)(2,1)S(1)}) custom-call(bf16[2,128,1536]{2,1,0:T(8,128)(2,1)} %refs_9_.1), custom_call_target="tpu_custom_call" | custom-call | bytes 2097152 | tf_op jit(solution)/shard_map/pallas_call | solution.py:385
  2.7 11.9 %all-to-all-start = ((bf16[32,8,1536]{2,1,0:T(8,128)(2,1)}), bf16[32,8,1536]{2,1,0:T(8,128)(2,1)S(1)}, u32[]{:S(2)}, u32[]{:S(2)}) async-start(bf16[32,8,1536]{2,1,0:T(8,128)(2,1)} %bitcast.13), calls=%async_computation | async-start | bytes 1572864 | tf_op jit(solution)/shard_map/all_to_all | solution.py:437
  15.3 0.1 pad_add_fusion.place_ref
  15.4 0.0 copy-start
  15.4 0.0 copy-start.2
  15.4 6.3 %shard_map.123 = (f32[3]{0:T(128)S(1)}, f32[16,1536]{1,0:T(8,128)}, bf16[1152,128]{1,0:T(8,128)(2,1)}, bf16[1152,128]{1,0:T(8,128)(2,1)}, bf16[1152,128]{1,0:T(8,128)(2,1)}, /*index=5*/bf16[1152,128]{1,0:T(8,128)(2,1)}) custom-call(s32[64]{0:T(128)S(1)} %copy-done.1, s32[1]{0:T(128)S(6)} %copy.15.offset_ref, f32[32]{0:T(128)S(1)} %copy-done.3, ...), custom_call_target="tpu_custom_call" | custom-call | flops 60000002048 | bytes 10485760 | tf_op jit(solution)/shard_map/pallas_call | solution.py:385
  21.7 0.0 copy-done.4
  21.7 0.8 slice_bitcast_fusion
  22.5 2.3 %collective-permute-start = (bf16[128,1536]{1,0:T(8,128)(2,1)}, bf16[128,1536]{1,0:T(8,128)(2,1)}, u32[]{:S(2)}, u32[]{:S(2)}) collective-permute-start(bf16[128,1536]{1,0:T(8,128)(2,1)} %slice_bitcast_fusion), channel_id=1, source_target_pairs={{8,0},{16,8},{24,16},{32,24},{40,32},{48,40},{56,48},{64,56},{72,6... | collective-permute-start | bytes 1179656 | tf_op jit(solution)/shard_map/ppermute | solution.py:493
  24.8 2.8 %collective-permute-start.1 = (bf16[1152,128]{1,0:T(8,128)(2,1)}, bf16[1152,128]{1,0:T(8,128)(2,1)S(1)}, u32[]{:S(2)}, u32[]{:S(2)}) collective-permute-start(bf16[1152,128]{1,0:T(8,128)(2,1)} %get-tuple-element.55), channel_id=1, source_target_pairs={{0,0},{1,1},{2,2},{3,3},{4,8},{5,9},{6,10},{7,11},{8,4},{9,5},{10,... | collective-permute-start | bytes 884744 | tf_op jit(solution)/shard_map/ppermute | solution.py:426
  27.6 1.9 %collective-permute-start.2 = (bf16[1152,128]{1,0:T(8,128)(2,1)}, bf16[1152,128]{1,0:T(8,128)(2,1)}, u32[]{:S(2)}, u32[]{:S(2)}) collective-permute-start(bf16[1152,128]{1,0:T(8,128)(2,1)} %get-tuple-element.56), channel_id=1, source_target_pairs={{0,1},{1,0},{2,3},{3,2},{4,9},{5,8},{6,11},{7,10},{8,5},{9,4},{10,... | collective-permute-start | bytes 884744 | tf_op jit(solution)/shard_map/ppermute | solution.py:426
  29.5 3.3 %collective-permute-start.3 = (bf16[1152,128]{1,0:T(8,128)(2,1)}, bf16[1152,128]{1,0:T(8,128)(2,1)}, u32[]{:S(2)}, u32[]{:S(2)}) collective-permute-start(bf16[1152,128]{1,0:T(8,128)(2,1)} %get-tuple-element.57), channel_id=1, source_target_pairs={{0,2},{1,3},{2,0},{3,1},{4,10},{5,11},{6,8},{7,9},{8,6},{9,7},{10,... | collective-permute-start | bytes 884744 | tf_op jit(solution)/shard_map/ppermute | solution.py:426
  32.8 0.5 collective-permute-start.4
  33.3 3.0 %shard_map.124 = (f32[32,2,1536]{2,1,0:T(2,128)}, f32[32,2,1536]{2,1,0:T(2,128)}, f32[256,256]{1,0:T(8,128)}, bf16[1536,768]{1,0:T(8,128)(2,1)S(1)}) custom-call(s32[64]{0:T(128)S(1)} %copy-done.1, s32[1]{0:T(128)S(6)} %copy.15.offset_ref, s32[64]{0:T(128)S(1)} %copy-done.2, f32[3,32,1536]{2,1,0:T(8,128)S(1)} %bitcast.10, bf16[1536,768]{1,0:T(8,128)(2,1)} %refs_0_.1), custom_call_target="tpu_custom_call" | custom-call | bytes 262144 | tf_op jit(solution)/shard_map/pallas_call | solution.py:385
  36.3 1.2 %all-to-all-done.x_ref = bf16[32,8,1536]{2,1,0:T(8,128)(2,1)S(1)} async-done(((bf16[32,8,1536]{2,1,0:T(8,128)(2,1)}), bf16[32,8,1536]{2,1,0:T(8,128)(2,1)S(1)}, u32[]{:S(2)}, u32[]{:S(2)}) %all-to-all-start) | async-done | bytes 786464 | tf_op jit(solution)/shard_map/all_to_all | solution.py:437
  37.5 6.2 %shard_map.125 = bf16[256,896]{1,0:T(8,128)(2,1)} custom-call(bf16[32,8,1536]{2,1,0:T(8,128)(2,1)S(1)} %all-to-all-done.x_ref, bf16[1536,768]{1,0:T(8,128)(2,1)S(1)} %get-tuple-element.50.wq_ref, f32[32,2,1536]{2,1,0:T(2,128)} %get-tuple-element.51.refs_0_, f32[32,2,1536]{2,1,0:T(2,128)} %get-tuple-element.52.refs_1_, bf16[1536,768]{1,0:T(8,128)(2,1)} %refs_2_.1, ...), custom_call_target="tpu_custom_call" | custom-call | flops 60000002048 | bytes 10485760 | tf_op jit(solution)/shard_map/pallas_call | solution.py:385
  43.7 8.3 %all-to-all-start.1 = ((bf16[32,8,896]{2,1,0:T(8,128)(2,1)}), bf16[32,8,896]{2,1,0:T(8,128)(2,1)S(1)}, u32[]{:S(2)}, u32[]{:S(2)}) async-start(bf16[32,8,896]{2,1,0:T(8,128)(2,1)} %bitcast.14), calls=%async_computation.1 | async-start | bytes 917504 | tf_op jit(solution)/shard_map/all_to_all | solution.py:518
  52.0 0.0 collective-permute-done.1.refs_0_
  52.0 0.0 collective-permute-done.2.refs_1_
  52.1 0.0 collective-permute-done.3.refs_2_
  52.1 0.0 collective-permute-done.4.refs_3_
  52.1 0.0 collective-permute-done.refs_11_
  52.1 0.4 collective-permute-start.5
  52.5 0.1 collective-permute-start.6
  52.7 0.4 collective-permute-start.7
  53.1 0.1 collective-permute-start.8
  53.2 0.6 collective-permute-done.5.refs_4_
  53.8 0.6 collective-permute-done.6.refs_5_
  54.4 0.4 collective-permute-done.7.refs_6_
  54.8 0.4 collective-permute-done.8.refs_7_
  55.2 4.4 %shard_map.127 = (bf16[400,128]{1,0:T(8,128)(2,1)S(1)}, bf16[400,128]{1,0:T(8,128)(2,1)S(1)}, bf16[400,128]{1,0:T(8,128)(2,1)S(1)}, bf16[400,128]{1,0:T(8,128)(2,1)S(1)}) custom-call(bf16[1152,128]{1,0:T(8,128)(2,1)S(1)} %collective-permute-done.1.refs_0_, bf16[1152,128]{1,0:T(8,128)(2,1)} %collective-permute-done.2.refs_1_, ...), custom_call_target="tpu_custom_call" | custom-call | flops 805306368 | bytes 3145728 | tf_op jit(solution)/shard_map/pallas_call | solution.py:385
  59.6 1.2 %collective-permute-start.10 = (bf16[400,128]{1,0:T(8,128)(2,1)S(1)}, bf16[400,128]{1,0:T(8,128)(2,1)S(1)}, u32[]{:S(2)}, u32[]{:S(2)}) collective-permute-start(bf16[400,128]{1,0:T(8,128)(2,1)S(1)} %get-tuple-element.69), channel_id=1, source_target_pairs={{0,1},{1,0},{2,3},{3,2},{4,9},{5,8},{6,11},{7,10},{8,5},{9,4},{10,... | collective-permute-start | bytes 307208 | tf_op jit(solution)/shard_map/ppermute | solution.py:426
  60.9 3.9 %collective-permute-start.11 = (bf16[400,128]{1,0:T(8,128)(2,1)S(1)}, bf16[400,128]{1,0:T(8,128)(2,1)S(1)}, u32[]{:S(2)}, u32[]{:S(2)}) collective-permute-start(bf16[400,128]{1,0:T(8,128)(2,1)S(1)} %get-tuple-element.70), channel_id=1, source_target_pairs={{0,2},{1,3},{2,0},{3,1},{4,10},{5,11},{6,8},{7,9},{8,6},{9,7},{10,... | collective-permute-start | bytes 307208 | tf_op jit(solution)/shard_map/ppermute | solution.py:426
  64.8 1.0 %collective-permute-start.12 = (bf16[400,128]{1,0:T(8,128)(2,1)S(1)}, bf16[400,128]{1,0:T(8,128)(2,1)S(1)}, u32[]{:S(2)}, u32[]{:S(2)}) collective-permute-start(bf16[400,128]{1,0:T(8,128)(2,1)S(1)} %get-tuple-element.71), channel_id=1, source_target_pairs={{0,3},{1,2},{2,1},{3,0},{4,11},{5,10},{6,9},{7,8},{8,7},{9,6},{10,... | collective-permute-start | bytes 307208 | tf_op jit(solution)/shard_map/ppermute | solution.py:426
  65.8 2.3 %collective-permute-start.9 = (bf16[400,128]{1,0:T(8,128)(2,1)S(1)}, bf16[400,128]{1,0:T(8,128)(2,1)S(1)}, u32[]{:S(2)}, u32[]{:S(2)}) collective-permute-start(bf16[400,128]{1,0:T(8,128)(2,1)S(1)} %get-tuple-element.68), channel_id=1, source_target_pairs={{0,0},{1,1},{2,2},{3,3},{4,8},{5,9},{6,10},{7,11},{8,4},{9,5},{10,... | collective-permute-start | bytes 307208 | tf_op jit(solution)/shard_map/ppermute | solution.py:426
  68.1 0.0 all-to-all-done.1
  68.1 1.7 %shard_map.128 = (bf16[2,128,768]{2,1,0:T(8,128)(2,1)S(1)}, f32[2,128,128]{2,1,0:T(8,128)S(1)}, bf16[768,1536]{1,0:T(8,128)(2,1)S(1)}, f32[16,1536]{1,0:T(8,128)S(1)}) custom-call(bf16[256,896]{1,0:T(8,128)(2,1)S(1)} %bitcast.11, bf16[768,1536]{1,0:T(8,128)(2,1)} %wo_hbm.1, f32[16,1536]{1,0:T(8,128)} %get-tuple-element.72.own_hbm), custom_call_target="tpu_custom_call" | custom-call | flops 60000002048 | bytes 1048576 | tf_op jit(solution)/shard_map/pallas_call | solution.py:385
  69.8 0.0 collective-permute-done.10.refs_1_
  69.8 0.0 collective-permute-done.11.refs_2_
  69.8 1.2 %collective-permute-done.12.refs_3_ = bf16[400,128]{1,0:T(8,128)(2,1)S(1)} collective-permute-done((bf16[400,128]{1,0:T(8,128)(2,1)S(1)}, bf16[400,128]{1,0:T(8,128)(2,1)S(1)}, u32[]{:S(2)}, u32[]{:S(2)}) %collective-permute-start.12) | collective-permute-done | bytes 102432 | tf_op jit(solution)/shard_map/ppermute | solution.py:426
  71.0 1.0 %collective-permute-done.9.refs_0_ = bf16[400,128]{1,0:T(8,128)(2,1)S(1)} collective-permute-done((bf16[400,128]{1,0:T(8,128)(2,1)S(1)}, bf16[400,128]{1,0:T(8,128)(2,1)S(1)}, u32[]{:S(2)}, u32[]{:S(2)}) %collective-permute-start.9) | collective-permute-done | bytes 102432 | tf_op jit(solution)/shard_map/ppermute | solution.py:426
  72.1 1.0 %shard_map.129 = (bf16[128,768]{1,0:T(8,128)(2,1)S(1)}, bf16[128,768]{1,0:T(8,128)(2,1)S(1)}) custom-call(s32[3]{0:T(128)S(1)} %pad_add_fusion.place_ref, f32[1,32]{1,0:T(1,128)S(1)} %shard_map.126.mark_ref, bf16[400,128]{1,0:T(8,128)(2,1)S(1)} %collective-permute-done.9.refs_0_, bf16[400,128]{1,0:T(8,128)(2,1)S(1)} %collective-permute-done.10.refs_1_, ...), custom_call_target="tpu_custom_call" | custom-call | bytes 2097152 | tf_op jit(solution)/shard_map/pallas_call | solution.py:385
  73.1 2.5 %collective-permute-start.13 = (bf16[128,768]{1,0:T(8,128)(2,1)S(1)}, bf16[128,768]{1,0:T(8,128)(2,1)S(1)}, u32[]{:S(2)}, u32[]{:S(2)}) collective-permute-start(bf16[128,768]{1,0:T(8,128)(2,1)S(1)} %get-tuple-element.81), channel_id=1, source_target_pairs={{8,0},{16,8},{24,16},{32,24},{40,32},{48,40},{56,48},{64,56},{72,6... | collective-permute-start | bytes 589832 | tf_op jit(solution)/shard_map/ppermute | solution.py:557
  75.6 3.6 %shard_map.130 = (bf16[2,128,1536]{2,1,0:T(8,128)(2,1)}, bf16[2,128,1536]{2,1,0:T(8,128)(2,1)}, bf16[128,1536]{1,0:T(8,128)(2,1)S(1)}) custom-call(s32[3]{0:T(128)S(1)} %pad_add_fusion.place_ref, f32[3]{0:T(128)S(1)} %get-tuple-element.46.size_ref, bf16[400,128]{1,0:T(8,128)(2,1)S(1)} %collective-permute-done.9.refs_0_, ...), custom_call_target="tpu_custom_call" | custom-call | flops 603979776 | bytes 6291456 | tf_op jit(solution)/shard_map/pallas_call | solution.py:385
  79.2 3.3 %collective-permute-done.13.att_ref = bf16[128,768]{1,0:T(8,128)(2,1)S(1)} collective-permute-done((bf16[128,768]{1,0:T(8,128)(2,1)S(1)}, bf16[128,768]{1,0:T(8,128)(2,1)S(1)}, u32[]{:S(2)}, u32[]{:S(2)}) %collective-permute-start.13) | collective-permute-done | bytes 196640 | tf_op jit(solution)/shard_map/ppermute | solution.py:557
  82.5 1.7 %shard_map.131 = bf16[2,128,1536]{2,1,0:T(8,128)(2,1)} custom-call(f32[3]{0:T(128)S(1)} %get-tuple-element.46.size_ref, bf16[128,768]{1,0:T(8,128)(2,1)S(1)} %collective-permute-done.13.att_ref, bf16[768,1536]{1,0:T(8,128)(2,1)S(1)} %get-tuple-element.77.refs_7_.wo_ref, ...), custom_call_target="tpu_custom_call", output_to_operand_aliasing={{}: (5, {})} | custom-call | flops 301989888 | bytes 4194304 | tf_op jit(solution)/shard_map/pallas_call | solution.py:385
  (6 shorter events, 0.0 us)
Async XLA Ops:
  0.6 14.7 %copy-start.1 = (s32[64]{0:T(128)S(1)}, s32[64]{0:T(128)}, u32[]{:S(2)}) copy-start(s32[64]{0:T(128)} %noise_ref.2) | copy-start | bytes 772
  0.6 14.7 %copy-start.3 = (f32[32]{0:T(128)S(1)}, f32[32]{0:T(128)}, u32[]{:S(2)}) copy-start(f32[32]{0:T(128)} %step_ref.1) | copy-start | bytes 388
  2.7 34.8 %all-to-all-start = ((bf16[32,8,1536]{2,1,0:T(8,128)(2,1)}), bf16[32,8,1536]{2,1,0:T(8,128)(2,1)S(1)}, u32[]{:S(2)}, u32[]{:S(2)}) async-start(bf16[32,8,1536]{2,1,0:T(8,128)(2,1)} %bitcast.13), calls=%async_computation | async-start | bytes 1572864 | tf_op jit(solution)/shard_map/all_to_all | solution.py:437
  15.4 6.4 %copy-start.4 = (bf16[2,128,1536]{2,1,0:T(8,128)(2,1)S(1)}, bf16[2,128,1536]{2,1,0:T(8,128)(2,1)}, u32[]{:S(2)}) copy-start(bf16[2,128,1536]{2,1,0:T(8,128)(2,1)} %refs_9_.1) | copy-start | bytes 2359300
  15.4 17.9 %copy-start = (f32[32,3,1536]{2,0,1:T(8,128)S(1)}, f32[32,3,1536]{2,0,1:T(8,128)}, u32[]{:S(2)}) copy-start(f32[32,3,1536]{2,0,1:T(8,128)} %param.16) | copy-start | bytes 1769476
  15.4 17.9 %copy-start.2 = (s32[64]{0:T(128)S(1)}, s32[64]{0:T(128)}, u32[]{:S(2)}) copy-start(s32[64]{0:T(128)} %blocks_ref.1) | copy-start | bytes 772
  22.5 29.6 %collective-permute-start = (bf16[128,1536]{1,0:T(8,128)(2,1)}, bf16[128,1536]{1,0:T(8,128)(2,1)}, u32[]{:S(2)}, u32[]{:S(2)}) collective-permute-start(bf16[128,1536]{1,0:T(8,128)(2,1)} %slice_bitcast_fusion), channel_id=1, source_target_pairs={{8,0},{16,8},{24,16},{32,24},{40,32},{48,40},{56,48},{64,56},{72,6... | collective-permute-start | bytes 1179656 | tf_op jit(solution)/shard_map/ppermute | solution.py:493
  24.8 27.3 %collective-permute-start.1 = (bf16[1152,128]{1,0:T(8,128)(2,1)}, bf16[1152,128]{1,0:T(8,128)(2,1)S(1)}, u32[]{:S(2)}, u32[]{:S(2)}) collective-permute-start(bf16[1152,128]{1,0:T(8,128)(2,1)} %get-tuple-element.55), channel_id=1, source_target_pairs={{0,0},{1,1},{2,2},{3,3},{4,8},{5,9},{6,10},{7,11},{8,4},{9,5},{10,... | collective-permute-start | bytes 884744 | tf_op jit(solution)/shard_map/ppermute | solution.py:426
  27.6 24.4 %collective-permute-start.2 = (bf16[1152,128]{1,0:T(8,128)(2,1)}, bf16[1152,128]{1,0:T(8,128)(2,1)}, u32[]{:S(2)}, u32[]{:S(2)}) collective-permute-start(bf16[1152,128]{1,0:T(8,128)(2,1)} %get-tuple-element.56), channel_id=1, source_target_pairs={{0,1},{1,0},{2,3},{3,2},{4,9},{5,8},{6,11},{7,10},{8,5},{9,4},{10,... | collective-permute-start | bytes 884744 | tf_op jit(solution)/shard_map/ppermute | solution.py:426
  29.5 22.5 %collective-permute-start.3 = (bf16[1152,128]{1,0:T(8,128)(2,1)}, bf16[1152,128]{1,0:T(8,128)(2,1)}, u32[]{:S(2)}, u32[]{:S(2)}) collective-permute-start(bf16[1152,128]{1,0:T(8,128)(2,1)} %get-tuple-element.57), channel_id=1, source_target_pairs={{0,2},{1,3},{2,0},{3,1},{4,10},{5,11},{6,8},{7,9},{8,6},{9,7},{10,... | collective-permute-start | bytes 884744 | tf_op jit(solution)/shard_map/ppermute | solution.py:426
  32.8 19.3 %collective-permute-start.4 = (bf16[1152,128]{1,0:T(8,128)(2,1)}, bf16[1152,128]{1,0:T(8,128)(2,1)}, u32[]{:S(2)}, u32[]{:S(2)}) collective-permute-start(bf16[1152,128]{1,0:T(8,128)(2,1)} %get-tuple-element.58), channel_id=1, source_target_pairs={{0,3},{1,2},{2,1},{3,0},{4,11},{5,10},{6,9},{7,8},{8,7},{9,6},{10,... | collective-permute-start | bytes 884744 | tf_op jit(solution)/shard_map/ppermute | solution.py:426
  43.7 24.4 %all-to-all-start.1 = ((bf16[32,8,896]{2,1,0:T(8,128)(2,1)}), bf16[32,8,896]{2,1,0:T(8,128)(2,1)S(1)}, u32[]{:S(2)}, u32[]{:S(2)}) async-start(bf16[32,8,896]{2,1,0:T(8,128)(2,1)} %bitcast.14), calls=%async_computation.1 | async-start | bytes 917504 | tf_op jit(solution)/shard_map/all_to_all | solution.py:518
  52.1 1.7 %collective-permute-start.5 = (bf16[1152,128]{1,0:T(8,128)(2,1)S(1)}, bf16[1152,128]{1,0:T(8,128)(2,1)S(1)}, u32[]{:S(2)}, u32[]{:S(2)}) collective-permute-start(bf16[1152,128]{1,0:T(8,128)(2,1)S(1)} %collective-permute-done.1.refs_0_), channel_id=1, source_target_pairs={{0,8},{8,0},{16,24},{24,16},{32,40},{40,32},{48,56},{56,48},{64,72... | collective-permute-start | bytes 884744 | tf_op jit(solution)/shard_map/ppermute | solution.py:517
  52.5 1.9 %collective-permute-start.6 = (bf16[1152,128]{1,0:T(8,128)(2,1)}, bf16[1152,128]{1,0:T(8,128)(2,1)S(1)}, u32[]{:S(2)}, u32[]{:S(2)}) collective-permute-start(bf16[1152,128]{1,0:T(8,128)(2,1)} %collective-permute-done.2.refs_1_), channel_id=1, source_target_pairs={{0,8},{8,0},{16,24},{24,16},{32,40},{40,32},{48,56},{56,48},{64,72... | collective-permute-start | bytes 884744 | tf_op jit(solution)/shard_map/ppermute | solution.py:517
  52.7 2.1 %collective-permute-start.7 = (bf16[1152,128]{1,0:T(8,128)(2,1)}, bf16[1152,128]{1,0:T(8,128)(2,1)S(1)}, u32[]{:S(2)}, u32[]{:S(2)}) collective-permute-start(bf16[1152,128]{1,0:T(8,128)(2,1)} %collective-permute-done.3.refs_2_), channel_id=1, source_target_pairs={{0,8},{8,0},{16,24},{24,16},{32,40},{40,32},{48,56},{56,48},{64,72... | collective-permute-start | bytes 884744 | tf_op jit(solution)/shard_map/ppermute | solution.py:517
  53.1 2.2 %collective-permute-start.8 = (bf16[1152,128]{1,0:T(8,128)(2,1)}, bf16[1152,128]{1,0:T(8,128)(2,1)S(1)}, u32[]{:S(2)}, u32[]{:S(2)}) collective-permute-start(bf16[1152,128]{1,0:T(8,128)(2,1)} %collective-permute-done.4.refs_3_), channel_id=1, source_target_pairs={{0,8},{8,0},{16,24},{24,16},{32,40},{40,32},{48,56},{56,48},{64,72... | collective-permute-start | bytes 884744 | tf_op jit(solution)/shard_map/ppermute | solution.py:517
  59.6 10.2 %collective-permute-start.10 = (bf16[400,128]{1,0:T(8,128)(2,1)S(1)}, bf16[400,128]{1,0:T(8,128)(2,1)S(1)}, u32[]{:S(2)}, u32[]{:S(2)}) collective-permute-start(bf16[400,128]{1,0:T(8,128)(2,1)S(1)} %get-tuple-element.69), channel_id=1, source_target_pairs={{0,1},{1,0},{2,3},{3,2},{4,9},{5,8},{6,11},{7,10},{8,5},{9,4},{10,... | collective-permute-start | bytes 307208 | tf_op jit(solution)/shard_map/ppermute | solution.py:426
  60.9 9.0 %collective-permute-start.11 = (bf16[400,128]{1,0:T(8,128)(2,1)S(1)}, bf16[400,128]{1,0:T(8,128)(2,1)S(1)}, u32[]{:S(2)}, u32[]{:S(2)}) collective-permute-start(bf16[400,128]{1,0:T(8,128)(2,1)S(1)} %get-tuple-element.70), channel_id=1, source_target_pairs={{0,2},{1,3},{2,0},{3,1},{4,10},{5,11},{6,8},{7,9},{8,6},{9,7},{10,... | collective-permute-start | bytes 307208 | tf_op jit(solution)/shard_map/ppermute | solution.py:426
  64.8 6.3 %collective-permute-start.12 = (bf16[400,128]{1,0:T(8,128)(2,1)S(1)}, bf16[400,128]{1,0:T(8,128)(2,1)S(1)}, u32[]{:S(2)}, u32[]{:S(2)}) collective-permute-start(bf16[400,128]{1,0:T(8,128)(2,1)S(1)} %get-tuple-element.71), channel_id=1, source_target_pairs={{0,3},{1,2},{2,1},{3,0},{4,11},{5,10},{6,9},{7,8},{8,7},{9,6},{10,... | collective-permute-start | bytes 307208 | tf_op jit(solution)/shard_map/ppermute | solution.py:426
  65.8 6.3 %collective-permute-start.9 = (bf16[400,128]{1,0:T(8,128)(2,1)S(1)}, bf16[400,128]{1,0:T(8,128)(2,1)S(1)}, u32[]{:S(2)}, u32[]{:S(2)}) collective-permute-start(bf16[400,128]{1,0:T(8,128)(2,1)S(1)} %get-tuple-element.68), channel_id=1, source_target_pairs={{0,0},{1,1},{2,2},{3,3},{4,8},{5,9},{6,10},{7,11},{8,4},{9,5},{10,... | collective-permute-start | bytes 307208 | tf_op jit(solution)/shard_map/ppermute | solution.py:426
  73.1 9.4 %collective-permute-start.13 = (bf16[128,768]{1,0:T(8,128)(2,1)S(1)}, bf16[128,768]{1,0:T(8,128)(2,1)S(1)}, u32[]{:S(2)}, u32[]{:S(2)}) collective-permute-start(bf16[128,768]{1,0:T(8,128)(2,1)S(1)} %get-tuple-element.81), channel_id=1, source_target_pairs={{8,0},{16,8},{24,16},{32,24},{40,32},{48,40},{56,48},{64,56},{72,6... | collective-permute-start | bytes 589832 | tf_op jit(solution)/shard_map/ppermute | solution.py:557

commit v6 on v4

--- a/solution.py
+++ b/solution.py
@@ -70,7 +70,7 @@
     return jnp.where(low, even, pltpu.roll(odd, 4, 1)), jnp.where(low, pltpu.roll(even, 4, 1), odd)
 
 
-def shuffle_kernel(x_hbm, out_hbm, x_ref, mixed_ref, in_sems, out_sems):
+def shuffle_kernel(x_hbm, out_hbm, first_hbm, x_ref, mixed_ref, in_sems, out_sems, first_sem):
     _, tokens, width = x_ref.shape
     chunks = in_sems.shape[0]
     rows = tokens // chunks
@@ -91,15 +91,33 @@
         r = pl.ds(c * pairs, pairs)
         outs.append(pltpu.make_async_copy(mixed_ref.at[r], out_hbm.at[r], out_sems.at[c]))
         outs[c].start()
-    for c in range(chunks):
-        outs[c].wait()
+    outs.append(pltpu.make_async_copy(x_ref.at[0], first_hbm, first_sem))
+    outs[-1].start()
+    for copy in outs:
+        copy.wait()
 
 
 def home_kernel(
-    noise_ref, offset_ref, step_ref, place_ref, x_ref, table_hbm, wq_hbm, wk_hbm, wv_hbm, size_ref, own_hbm, *refs
+    noise_ref,
+    offset_ref,
+    step_ref,
+    blocks_ref,
+    place_ref,
+    x_ref,
+    table_hbm,
+    wq_hbm,
+    wk_hbm,
+    wv_hbm,
+    size_ref,
+    own_hbm,
+    shift_hbm,
+    scale_hbm,
+    bias_hbm,
+    *refs,
 ):
     outs = refs[:RANKS]
-    table_ref, q_ref, k_ref, v_ref, wq_ref, wk_ref, wv_ref, own_ref, sems, own_sem = refs[RANKS:]
+    table_ref, q_ref, k_ref, v_ref, wq_ref, wk_ref, wv_ref, *refs = refs[RANKS:]
+    own_ref, shift_ref, scale_ref, bias_ref, sems, store_sems = refs
     loads = []
     for n, (src, dst) in enumerate(
         ((table_hbm, table_ref), (wq_hbm, wq_ref), (wk_hbm, wk_ref), (wv_hbm, wv_ref))
@@ -116,8 +134,31 @@
         own_ref[n : n + 1, :] = table_ref[0, pl.ds(level, 1), :]
         own_ref[n + 3 : n + 4, :] = table_ref[1, pl.ds(level, 1), :] + 1.0
         own_ref[n + 6 : n + 7, :] = table_ref[2, pl.ds(level, 1), :]
-    own_store = pltpu.make_async_copy(own_ref, own_hbm, own_sem)
-    own_store.start()
+    stores = [
+        pltpu.make_async_copy(src, dst, store_sems.at[n])
+        for n, (src, dst) in enumerate(
+            ((own_ref, own_hbm), (shift_ref, shift_hbm), (scale_ref, scale_hbm), (bias_ref, bias_hbm))
+        )
+    ]
+    stores[0].start()
+    share = bias_ref.shape[0] // total
+    for f in range(total):
+        level = noise_ref[lax.rem(f + offset_ref[0], total)]
+        shift_ref[f // frames, f % frames : f % frames + 1, :] = table_ref[0, pl.ds(level, 1), :]
+        scale_ref[f // frames, f % frames : f % frames + 1, :] = table_ref[1, pl.ds(level, 1), :] + 1.0
+    stores[1].start()
+    stores[2].start()
+    wide = (8, total * share)
+    lane = lax.broadcasted_iota(jnp.int32, wide, 1) // share
+    block = jnp.zeros(wide, F32)
+    for f in range(total):
+        block = jnp.where(lane == f, blocks_ref[f].astype(F32), block)
+    block = jnp.broadcast_to(block[0:1], bias_ref.shape)
+    down = lax.broadcasted_iota(jnp.int32, bias_ref.shape, 0)
+    along = lax.broadcasted_iota(jnp.int32, bias_ref.shape, 1)
+    allowed = (down % share == along % share) & (down != along) & (block <= jnp.transpose(block))
+    bias_ref[...] = jnp.where(allowed, 0.0, MASKED)
+    stores[3].start()
     normed = []
     for f in range(frames):
         normed.append(normalise(x_ref[f], own_ref[f + 3 : f + 4, :], own_ref[f : f + 1, :]))
@@ -133,37 +174,6 @@
             for n, ref in enumerate((k_ref, v_ref, q_ref)):
                 block = slice((n * SPAN + u) * tokens, (n * SPAN + u + 1) * tokens)
                 outs[d][block] = ref[r, c]
-    own_store.wait()
-
-
-def column_kernel(noise_ref, offset_ref, blocks_ref, table_ref, shift_hbm, scale_hbm, bias_hbm, *refs):
-    shift_ref, scale_ref, bias_ref, sems = refs
-    total = noise_ref.shape[0]
-    frames = shift_ref.shape[1]
-    share = bias_ref.shape[0] // total
-    stores = [
-        pltpu.make_async_copy(src, dst, sems.at[n])
-        for n, (src, dst) in enumerate(
-            ((shift_ref, shift_hbm), (scale_ref, scale_hbm), (bias_ref, bias_hbm))
-        )
-    ]
-    for f in range(total):
-        level = noise_ref[lax.rem(f + offset_ref[0], total)]
-        shift_ref[f // frames, f % frames : f % frames + 1, :] = table_ref[0, pl.ds(level, 1), :]
-        scale_ref[f // frames, f % frames : f % frames + 1, :] = table_ref[1, pl.ds(level, 1), :] + 1.0
-    stores[0].start()
-    stores[1].start()
-    wide = (8, total * share)
-    lane = lax.broadcasted_iota(jnp.int32, wide, 1) // share
-    block = jnp.zeros(wide, F32)
-    for f in range(total):
-        block = jnp.where(lane == f, blocks_ref[f].astype(F32), block)
-    block = jnp.broadcast_to(block[0:1], bias_ref.shape)
-    down = lax.broadcasted_iota(jnp.int32, bias_ref.shape, 0)
-    along = lax.broadcasted_iota(jnp.int32, bias_ref.shape, 1)
-    allowed = (down % share == along % share) & (down != along) & (block <= jnp.transpose(block))
-    bias_ref[...] = jnp.where(allowed, 0.0, MASKED)
-    stores[2].start()
     for store in stores:
         store.wait()
 
@@ -245,7 +255,11 @@
         copy.wait()
 
 
-def reorder_kernel(time_ref, far_ref, logs_ref):
+def reorder_kernel(time_ref, wo_hbm, own_hbm, far_ref, logs_ref, wo_ref, own_ref, sems):
+    loads = []
+    for n, (src, dst) in enumerate(((wo_hbm, wo_ref), (own_hbm, own_ref))):
+        loads.append(pltpu.make_async_copy(src, dst, sems.at[n]))
+        loads[n].start()
     frames, tokens, inner = far_ref.shape
     width = time_ref.shape[1]
     turned = time_ref[...].astype(F32).reshape(tokens // 8, 2, 8, width)
@@ -254,6 +268,8 @@
         far_ref[f] = rows[:, :inner].astype(BF16)
         stats = rows[:, inner:]
         logs_ref[f, :, 0:8] = stats[:, 0:8] + stats[:, 8:16] + stats[:, 16:24]
+    for load in loads:
+        load.wait()
 
 
 def merged(f, rank, near_refs, far_ref, logs_ref, space_ref, out_ref):
@@ -288,17 +304,14 @@
 
 def project_kernel(place_ref, size_ref, *refs):
     near_refs = refs[:RANKS]
-    far_ref, logs_ref, first_ref, wo_hbm, own_hbm, x_hbm, fresh_hbm, in_hbm_ref = refs[RANKS : RANKS + 8]
-    vel_hbm, next_hbm, wo_ref, own_ref, base_ref = refs[RANKS + 8 : RANKS + 13]
-    space_ref, second_ref, x_ref, fresh_ref, vel_ref, next_ref, sems, vel_sems, next_sems = refs[RANKS + 13 :]
+    far_ref, logs_ref, first_ref, wo_ref, own_ref, in_ref, x_hbm, fresh_hbm = refs[RANKS : RANKS + 8]
+    vel_hbm, next_hbm, base_ref = refs[RANKS + 8 : RANKS + 11]
+    space_ref, second_ref, x_ref, fresh_ref, vel_ref, next_ref, sems, vel_sems, next_sems = refs[RANKS + 11 :]
     frames, tokens, _ = x_ref.shape
     loads = []
     for n, (src, dst) in enumerate(
         (
-            (wo_hbm, wo_ref),
-            (own_hbm, own_ref),
             (x_hbm, x_ref),
-            (in_hbm_ref, base_ref),
             (fresh_hbm, fresh_ref),
         )
     ):
@@ -310,10 +323,7 @@
     for load in loads:
         load.wait()
 
-    @pl.when(place_ref[0] == place_ref[2])
-    def _():
-        base_ref[...] = fresh_ref[...]
-
+    base_ref[...] = jnp.where(place_ref[0] == place_ref[2], fresh_ref[...], in_ref[...])
     chunks = vel_sems.shape[0]
     width = vel_ref.shape[2] // chunks
     copies = []
@@ -415,14 +425,18 @@
                 pairs.append((tm * ranks + tok, (tm - core + side) * ranks + core * RANKS + (y ^ d)))
         return lax.ppermute(x, ("tm", "tok"), pairs)
 
-    outgoing, x = call(
+    outgoing, incoming, x = call(
         shuffle_kernel,
         (in_hbm(latents),),
         [anywhere()],
-        (pltpu.HBM((tokens // 8, 2, 8, width), BF16), pltpu.VMEM((frames, tokens, width), BF16)),
-        (anywhere(), whole()),
+        (
+            pltpu.HBM((tokens // 8, 2, 8, width), BF16),
+            pltpu.HBM((tokens, width), BF16),
+            pltpu.VMEM((frames, tokens, width), BF16),
+        ),
+        (anywhere(), anywhere(), whole()),
         nbytes=2 * MIB,
-        scratch_shapes=[pltpu.VMEM((tokens // 8, 2, 8, width), BF16), dma((4,)), dma((4,))],
+        scratch_shapes=[pltpu.VMEM((tokens // 8, 2, 8, width), BF16), dma((4,)), dma((4,)), dma],
     )
     column = lax.all_to_all(outgoing.reshape(times, frames * share, width), "tm", 0, 0)
 
@@ -430,53 +444,44 @@
     rank = lax.axis_index("tok").astype(jnp.int32) % RANKS
     place = jnp.stack([place, rank, jnp.int32(times - 1)])
     table = mod_table.transpose(1, 0, 2)
-    sizes, own, *parts = call(
+    small = (
+        pltpu.VMEM((16, width), F32),
+        pltpu.VMEM((times, frames, width), F32),
+        pltpu.VMEM((times, frames, width), F32),
+        pltpu.VMEM((total * share, total * share), F32),
+    )
+    sizes, own, shifts, scales, bias, *parts = call(
         home_kernel,
         (
             noise_levels,
             offset,
             step_sizes,
+            block_ids,
             place,
             pinned(x),
             *[in_hbm(a) for a in (table, w_query, w_key, w_value)],
         ),
-        [scalar()] * 4 + [whole()] + [anywhere()] * 4,
+        [scalar()] * 5 + [whole()] + [anywhere()] * 4,
         (
             sds((frames + 1,), F32),
-            pltpu.HBM((16, width), F32),
+            *[pltpu.HBM(a.inner_aval.shape, F32) for a in small],
             *[sds((3 * SPAN * tokens, HEAD_DIM), BF16)] * RANKS,
         ),
-        (scalar(), anywhere(), *[whole()] * RANKS),
+        (scalar(), *[anywhere()] * 4, *[whole()] * RANKS),
         flops=LONG,
         nbytes=10 * MIB,
         scratch_shapes=[
             pltpu.VMEM(table.shape, F32),
             *[pltpu.VMEM((frames * tokens, inner), BF16)] * 3,
             *[pltpu.VMEM((width, inner), BF16)] * 3,
-            pltpu.VMEM((16, width), F32),
+            *small,
             dma((4,)),
-            dma,
+            dma((4,)),
         ],
     )
     units = [exchange(part, d) for d, part in enumerate(parts)]
 
-    small = (
-        pltpu.VMEM((16, width), F32),
-        pltpu.VMEM((times, frames, width), F32),
-        pltpu.VMEM((times, frames, width), F32),
-        pltpu.VMEM((total * share, total * share), F32),
-    )
-    table, noise_levels, sizes = lax.optimization_barrier((table, noise_levels, sizes))
-    shifts, scales, bias = call(
-        column_kernel,
-        (noise_levels, offset, block_ids, table),
-        [scalar()] * 3 + [whole()],
-        tuple(pltpu.HBM(a.inner_aval.shape, F32) for a in small[1:]),
-        (anywhere(),) * 3,
-        nbytes=MIB // 4,
-        scratch_shapes=[*small[1:], dma((3,))],
-    )
-    incoming, sizes = lax.optimization_barrier((latents[0], sizes))
+    incoming, sizes = lax.optimization_barrier((incoming, sizes))
     next_latents = lax.ppermute(incoming, "tm", back_perm)
 
     back = call(
@@ -517,12 +522,18 @@
     near = [exchange(part, d) for d, part in enumerate(near)]
 
     space = pltpu.VMEM((RANKS, SPAN * tokens + STAT_ROWS, HEAD_DIM), BF16)
-    far, logs = call(
+    far, logs, wo, own = call(
         reorder_kernel,
-        (back,),
-        [whole()],
-        (pltpu.VMEM((frames, tokens, inner), BF16), pltpu.VMEM((frames, tokens, HEAD_DIM), F32)),
-        (whole(), whole()),
+        (back, in_hbm(w_out), in_hbm(own)),
+        [whole()] + [anywhere()] * 2,
+        (
+            pltpu.VMEM((frames, tokens, inner), BF16),
+            pltpu.VMEM((frames, tokens, HEAD_DIM), F32),
+            pltpu.VMEM((inner, width), BF16),
+            pltpu.VMEM((16, width), F32),
+        ),
+        (whole(),) * 4,
+        scratch_shapes=[dma((2,))],
         flops=LONG,
         nbytes=MIB,
     )
@@ -536,7 +547,7 @@
         scratch_shapes=[space],
     )
     next_first = lax.ppermute(sent, "tm", back_perm)
-    velocity, following, wo, own, base = call(
+    velocity, following, base = call(
         project_kernel,
         (
             place,
@@ -545,17 +556,19 @@
             pinned(far),
             pinned(logs),
             pinned(first),
-            *[in_hbm(a) for a in (w_out, own, latents, fresh_noise, next_latents)],
+            pinned(wo),
+            pinned(own),
+            next_latents,
+            in_hbm(latents),
+            in_hbm(fresh_noise),
         ),
-        [scalar()] * 2 + [whole()] * (RANKS + 3) + [anywhere()] * 5,
+        [scalar()] * 2 + [whole()] * (RANKS + 6) + [anywhere()] * 2,
         (
             pltpu.HBM((frames, tokens, width), BF16),
             pltpu.HBM((frames, tokens, width), BF16),
-            pltpu.VMEM((inner, width), BF16),
-            pltpu.VMEM((16, width), F32),
             pltpu.VMEM((tokens, width), BF16),
         ),
-        (anywhere(), anywhere(), whole(), whole(), whole()),
+        (anywhere(), anywhere(), whole()),
         flops=project_flops,
         nbytes=6 * MIB,
         scratch_shapes=[
@@ -565,7 +578,7 @@
             pltpu.VMEM((tokens, width), BF16),
             pltpu.VMEM((frames, tokens, width), BF16),
             pltpu.VMEM((frames - 1, tokens, width), BF16),
-            dma((5,)),
+            dma((2,)),
             *[dma((3,))] * 2,
         ],
     )

time: 85 us -> 83.2 us (0.979)
  waiting for transfers between devices: 13.5 us -> 15.4 us
  starting transfers between devices: 40.8 us -> 39.2 us
  local copies, waits for them, and re-layouts: 1.55 us -> 0.01 us
    all_to_all x1, waiting for transfers between devices: 3.07 us -> 5.29 us  [body(): lax.all_to_all(outgoing.reshape(times, frames * share, width), 'tm', 0, 0)]
    ppermute x8, waiting for transfers between devices: 5.51 us -> 3.65 us  [exchange(): return lax.ppermute(x, ('tm', 'tok'), pairs)]
    all_to_all x1, starting transfers between devices: 7.03 us -> 5.42 us  [body(): lax.all_to_all(back.reshape(times, frames * share, inner + HEAD_DIM), 'tm...]
    ppermute x1, waiting for transfers between devices: 3.13 us -> 4.01 us  [body(): next_first = lax.ppermute(sent, 'tm', back_perm)]
    pallas_call x10 -> x9, Pallas kernels: 27 us -> 26.3 us  [call(): pl.pallas_call(kernel, out_shape=outs, in_specs=in_specs, out_specs=out_s...]
  transfers between devices with their start and end apart: 16 -> 16, of which waited for: 8 -> 9; matrix products, arithmetic and copies ran while one was open for 1% -> 0% of each run, Pallas kernels for 26% -> 26%
where the time goes in v6:
time: 83.2 us; the launch traced here: 82.7 us
  starting transfers between devices  39.2 us (47%)
  Pallas kernels  26.3 us (32%)
  waiting for transfers between devices  15.4 us (19%)
  between operations  1.64 us (2%)
    pallas_call x9, Pallas kernels, call(): pl.pallas_call(kernel, out_shape=outs, in_specs=in_specs, out_specs=out_s...  26.3 us
    ppermute x8, starting transfers between devices, exchange(): return lax.ppermute(x, ('tm', 'tok'), pairs)  17 us
    all_to_all x1, starting transfers between devices, body(): lax.all_to_all(outgoing.reshape(times, frames * share, width), 'tm', 0, 0)  11.9 us
    all_to_all x1, starting transfers between devices, body(): lax.all_to_all(back.reshape(times, frames * share, inner + HEAD_DIM), 'tm...  5.42 us
    all_to_all x1, waiting for transfers between devices, body(): lax.all_to_all(outgoing.reshape(times, frames * share, width), 'tm', 0, 0)  5.29 us
    ppermute x1, waiting for transfers between devices, body(): next_first = lax.ppermute(sent, 'tm', back_perm)  4.01 us
    ppermute x8, waiting for transfers between devices, exchange(): return lax.ppermute(x, ('tm', 'tok'), pairs)  3.65 us
    ppermute x1, starting transfers between devices, body(): next_first = lax.ppermute(sent, 'tm', back_perm)  1.92 us
  transfers between devices with their start and end apart: 16, of which 9 were waited for; matrix products, arithmetic and copies ran while one was open for 0% of the time, Pallas kernels for 26%

profile of v6, /device:TPU:5, one launch (start us, length us, event | category | flops | bytes accessed | tf_op | source)
XLA Modules:
  0.0 82.7 jit_solution(7053141793808269665)
XLA Ops:
  0.6 0.0 copy-start.2
  0.6 0.0 copy-start.1
  0.7 0.0 copy-start
  0.7 2.1 %shard_map.122 = (bf16[16,2,8,1536]{3,2,1,0:T(8,128)(2,1)}, bf16[128,1536]{1,0:T(8,128)(2,1)}, bf16[2,128,1536]{2,1,0:T(8,128)(2,1)S(1)}) custom-call(bf16[2,128,1536]{2,1,0:T(8,128)(2,1)} %refs_10_.1), custom_call_target="tpu_custom_call" | custom-call | bytes 2097152 | tf_op jit(solution)/shard_map/pallas_call | solution.py:385
  2.8 11.9 %all-to-all-start = ((bf16[32,8,1536]{2,1,0:T(8,128)(2,1)}), bf16[32,8,1536]{2,1,0:T(8,128)(2,1)S(1)}, u32[]{:S(2)}, u32[]{:S(2)}) async-start(bf16[32,8,1536]{2,1,0:T(8,128)(2,1)} %bitcast.9), calls=%async_computation | async-start | bytes 1572864 | tf_op jit(solution)/shard_map/all_to_all | solution.py:441
  15.4 0.1 pad_add_fusion.place_ref
  15.5 0.0 copy-done.2
  15.5 0.0 copy-done.1
  15.5 0.0 copy-done
  15.5 6.4 %shard_map.123 = (f32[3]{0:T(128)S(1)}, f32[16,1536]{1,0:T(8,128)}, f32[32,2,1536]{2,1,0:T(2,128)}, f32[32,2,1536]{2,1,0:T(2,128)}, f32[256,256]{1,0:T(8,128)}, ...) custom-call(s32[64]{0:T(128)S(1)} %copy-done, ...), custom_call_target="tpu_custom_call" | custom-call | flops 60000002048 | bytes 10485760 | tf_op jit(solution)/shard_map/pallas_call | solution.py:385
  21.9 3.1 %collective-permute-start.1 = (bf16[1152,128]{1,0:T(8,128)(2,1)}, bf16[1152,128]{1,0:T(8,128)(2,1)S(1)}, u32[]{:S(2)}, u32[]{:S(2)}) collective-permute-start(bf16[1152,128]{1,0:T(8,128)(2,1)} %get-tuple-element.49), channel_id=1, source_target_pairs={{0,0},{1,1},{2,2},{3,3},{4,8},{5,9},{6,10},{7,11},{8,4},{9,5},{10,... | collective-permute-start | bytes 884744 | tf_op jit(solution)/shard_map/ppermute | solution.py:426
  25.0 1.7 %collective-permute-start.2 = (bf16[1152,128]{1,0:T(8,128)(2,1)S(1)}, bf16[1152,128]{1,0:T(8,128)(2,1)S(1)}, u32[]{:S(2)}, u32[]{:S(2)}) collective-permute-start(bf16[1152,128]{1,0:T(8,128)(2,1)S(1)} %get-tuple-element.50), channel_id=1, source_target_pairs={{0,1},{1,0},{2,3},{3,2},{4,9},{5,8},{6,11},{7,10},{8,5},{9,4},{10,... | collective-permute-start | bytes 884744 | tf_op jit(solution)/shard_map/ppermute | solution.py:426
  26.7 3.5 %collective-permute-start.3 = (bf16[1152,128]{1,0:T(8,128)(2,1)S(1)}, bf16[1152,128]{1,0:T(8,128)(2,1)S(1)}, u32[]{:S(2)}, u32[]{:S(2)}) collective-permute-start(bf16[1152,128]{1,0:T(8,128)(2,1)S(1)} %get-tuple-element.51), channel_id=1, source_target_pairs={{0,2},{1,3},{2,0},{3,1},{4,10},{5,11},{6,8},{7,9},{8,6},{9,7},{10,... | collective-permute-start | bytes 884744 | tf_op jit(solution)/shard_map/ppermute | solution.py:426
  30.2 0.2 collective-permute-start.4
  30.4 1.9 %collective-permute-start = (bf16[128,1536]{1,0:T(8,128)(2,1)}, bf16[128,1536]{1,0:T(8,128)(2,1)S(1)}, u32[]{:S(2)}, u32[]{:S(2)}) collective-permute-start(bf16[128,1536]{1,0:T(8,128)(2,1)} %get-tuple-element.48), channel_id=1, source_target_pairs={{8,0},{16,8},{24,16},{32,24},{40,32},{48,40},{56,48},{64,56},{72,6... | collective-permute-start | bytes 1179656 | tf_op jit(solution)/shard_map/ppermute | solution.py:485
  32.3 5.3 %all-to-all-done.x_ref = bf16[32,8,1536]{2,1,0:T(8,128)(2,1)S(1)} async-done(((bf16[32,8,1536]{2,1,0:T(8,128)(2,1)}), bf16[32,8,1536]{2,1,0:T(8,128)(2,1)S(1)}, u32[]{:S(2)}, u32[]{:S(2)}) %all-to-all-start) | async-done | bytes 786464 | tf_op jit(solution)/shard_map/all_to_all | solution.py:441
  37.6 6.6 %shard_map.124 = bf16[256,896]{1,0:T(8,128)(2,1)} custom-call(bf16[32,8,1536]{2,1,0:T(8,128)(2,1)S(1)} %all-to-all-done.x_ref, f32[32,2,1536]{2,1,0:T(2,128)} %get-tuple-element.45.refs_0_, f32[32,2,1536]{2,1,0:T(2,128)} %get-tuple-element.46.refs_1_, bf16[1536,768]{1,0:T(8,128)(2,1)} %refs_2_.1, bf16[1536,768]{1,0:T(8,128)(2,1)} %refs_3_.1, ...), custom_call_target="tpu_custom_call" | custom-call | flops 60000002048 | bytes 10485760 | tf_op jit(solution)/shard_map/pallas_call | solution.py:385
  44.2 5.4 %all-to-all-start.1 = ((bf16[32,8,896]{2,1,0:T(8,128)(2,1)}), bf16[32,8,896]{2,1,0:T(8,128)(2,1)S(1)}, u32[]{:S(2)}, u32[]{:S(2)}) async-start(bf16[32,8,896]{2,1,0:T(8,128)(2,1)} %bitcast.10), calls=%async_computation.1 | async-start | bytes 917504 | tf_op jit(solution)/shard_map/all_to_all | solution.py:510
  49.6 0.0 collective-permute-done.1.refs_0_
  49.7 0.0 collective-permute-done.2.refs_1_
  49.7 0.0 collective-permute-done.3.refs_2_
  49.7 0.0 collective-permute-done.4.refs_3_
  49.7 0.0 collective-permute-done.refs_9_
  49.7 0.4 collective-permute-start.5
  50.2 0.1 collective-permute-start.6
  50.3 0.4 collective-permute-start.7
  50.7 0.1 collective-permute-start.8
  50.8 0.6 collective-permute-done.5.refs_4_
  51.4 0.4 collective-permute-done.6.refs_5_
  51.8 0.4 collective-permute-done.7.refs_6_
  52.2 0.4 collective-permute-done.8.refs_7_
  52.6 3.3 %shard_map.126 = (bf16[400,128]{1,0:T(8,128)(2,1)S(1)}, bf16[400,128]{1,0:T(8,128)(2,1)S(1)}, bf16[400,128]{1,0:T(8,128)(2,1)S(1)}, bf16[400,128]{1,0:T(8,128)(2,1)S(1)}) custom-call(bf16[1152,128]{1,0:T(8,128)(2,1)S(1)} %collective-permute-done.1.refs_0_, bf16[1152,128]{1,0:T(8,128)(2,1)S(1)} %collective-permute-done.2.refs_1_, ...), custom_call_target="tpu_custom_call" | custom-call | flops 805306368 | bytes 3145728 | tf_op jit(solution)/shard_map/pallas_call | solution.py:385
  56.0 3.6 %collective-permute-start.9 = (bf16[400,128]{1,0:T(8,128)(2,1)S(1)}, bf16[400,128]{1,0:T(8,128)(2,1)S(1)}, u32[]{:S(2)}, u32[]{:S(2)}) collective-permute-start(bf16[400,128]{1,0:T(8,128)(2,1)S(1)} %get-tuple-element.62), channel_id=1, source_target_pairs={{0,0},{1,1},{2,2},{3,3},{4,8},{5,9},{6,10},{7,11},{8,4},{9,5},{10,... | collective-permute-start | bytes 307208 | tf_op jit(solution)/shard_map/ppermute | solution.py:426
  59.6 1.1 %collective-permute-start.10 = (bf16[400,128]{1,0:T(8,128)(2,1)S(1)}, bf16[400,128]{1,0:T(8,128)(2,1)S(1)}, u32[]{:S(2)}, u32[]{:S(2)}) collective-permute-start(bf16[400,128]{1,0:T(8,128)(2,1)S(1)} %get-tuple-element.63), channel_id=1, source_target_pairs={{0,1},{1,0},{2,3},{3,2},{4,9},{5,8},{6,11},{7,10},{8,5},{9,4},{10,... | collective-permute-start | bytes 307208 | tf_op jit(solution)/shard_map/ppermute | solution.py:426
  60.7 3.5 %collective-permute-start.11 = (bf16[400,128]{1,0:T(8,128)(2,1)S(1)}, bf16[400,128]{1,0:T(8,128)(2,1)S(1)}, u32[]{:S(2)}, u32[]{:S(2)}) collective-permute-start(bf16[400,128]{1,0:T(8,128)(2,1)S(1)} %get-tuple-element.64), channel_id=1, source_target_pairs={{0,2},{1,3},{2,0},{3,1},{4,10},{5,11},{6,8},{7,9},{8,6},{9,7},{10,... | collective-permute-start | bytes 307208 | tf_op jit(solution)/shard_map/ppermute | solution.py:426
  64.2 0.2 collective-permute-start.12
  64.4 0.6 all-to-all-done.1
  65.1 1.7 %shard_map.127 = (bf16[2,128,768]{2,1,0:T(8,128)(2,1)S(1)}, f32[2,128,128]{2,1,0:T(8,128)S(1)}, bf16[768,1536]{1,0:T(8,128)(2,1)S(1)}, f32[16,1536]{1,0:T(8,128)S(1)}) custom-call(bf16[256,896]{1,0:T(8,128)(2,1)S(1)} %bitcast.7, bf16[768,1536]{1,0:T(8,128)(2,1)} %wo_hbm.1, f32[16,1536]{1,0:T(8,128)} %get-tuple-element.66.own_hbm), custom_call_target="tpu_custom_call" | custom-call | flops 60000002048 | bytes 1048576 | tf_op jit(solution)/shard_map/pallas_call | solution.py:385
  66.7 0.0 collective-permute-done.9.refs_0_
  66.8 0.0 collective-permute-done.10.refs_1_
  66.8 1.1 %collective-permute-done.11.refs_2_ = bf16[400,128]{1,0:T(8,128)(2,1)S(1)} collective-permute-done((bf16[400,128]{1,0:T(8,128)(2,1)S(1)}, bf16[400,128]{1,0:T(8,128)(2,1)S(1)}, u32[]{:S(2)}, u32[]{:S(2)}) %collective-permute-start.11) | collective-permute-done | bytes 102432 | tf_op jit(solution)/shard_map/ppermute | solution.py:426
  67.8 2.6 %collective-permute-done.12.refs_3_ = bf16[400,128]{1,0:T(8,128)(2,1)S(1)} collective-permute-done((bf16[400,128]{1,0:T(8,128)(2,1)S(1)}, bf16[400,128]{1,0:T(8,128)(2,1)S(1)}, u32[]{:S(2)}, u32[]{:S(2)}) %collective-permute-start.12) | collective-permute-done | bytes 102432 | tf_op jit(solution)/shard_map/ppermute | solution.py:426
  70.4 1.0 %shard_map.128 = (bf16[128,768]{1,0:T(8,128)(2,1)S(1)}, bf16[128,768]{1,0:T(8,128)(2,1)S(1)}) custom-call(s32[3]{0:T(128)S(1)} %pad_add_fusion.place_ref, f32[1,32]{1,0:T(1,128)S(1)} %shard_map.125.mark_ref, bf16[400,128]{1,0:T(8,128)(2,1)S(1)} %collective-permute-done.9.refs_0_, bf16[400,128]{1,0:T(8,128)(2,1)S(1)} %collective-permute-done.10.refs_1_, ...), custom_call_target="tpu_custom_call" | custom-call | bytes 2097152 | tf_op jit(solution)/shard_map/pallas_call | solution.py:385
  71.4 1.9 %collective-permute-start.13 = (bf16[128,768]{1,0:T(8,128)(2,1)S(1)}, bf16[128,768]{1,0:T(8,128)(2,1)S(1)}, u32[]{:S(2)}, u32[]{:S(2)}) collective-permute-start(bf16[128,768]{1,0:T(8,128)(2,1)S(1)} %get-tuple-element.75), channel_id=1, source_target_pairs={{8,0},{16,8},{24,16},{32,24},{40,32},{48,40},{56,48},{64,56},{72,6... | collective-permute-start | bytes 589832 | tf_op jit(solution)/shard_map/ppermute | solution.py:549
  73.4 3.4 %shard_map.129 = (bf16[2,128,1536]{2,1,0:T(8,128)(2,1)}, bf16[2,128,1536]{2,1,0:T(8,128)(2,1)}, bf16[128,1536]{1,0:T(8,128)(2,1)S(1)}) custom-call(s32[3]{0:T(128)S(1)} %pad_add_fusion.place_ref, f32[3]{0:T(128)S(1)} %get-tuple-element.43.size_ref, bf16[400,128]{1,0:T(8,128)(2,1)S(1)} %collective-permute-done.9.refs_0_, ...), custom_call_target="tpu_custom_call" | custom-call | flops 603979776 | bytes 6291456 | tf_op jit(solution)/shard_map/pallas_call | solution.py:385
  76.8 4.0 %collective-permute-done.13.att_ref = bf16[128,768]{1,0:T(8,128)(2,1)S(1)} collective-permute-done((bf16[128,768]{1,0:T(8,128)(2,1)S(1)}, bf16[128,768]{1,0:T(8,128)(2,1)S(1)}, u32[]{:S(2)}, u32[]{:S(2)}) %collective-permute-start.13) | collective-permute-done | bytes 196640 | tf_op jit(solution)/shard_map/ppermute | solution.py:549
  80.8 1.7 %shard_map.130 = bf16[2,128,1536]{2,1,0:T(8,128)(2,1)} custom-call(f32[3]{0:T(128)S(1)} %get-tuple-element.43.size_ref, bf16[128,768]{1,0:T(8,128)(2,1)S(1)} %collective-permute-done.13.att_ref, bf16[768,1536]{1,0:T(8,128)(2,1)S(1)} %get-tuple-element.71.refs_7_.wo_ref, ...), custom_call_target="tpu_custom_call", output_to_operand_aliasing={{}: (5, {})} | custom-call | flops 301989888 | bytes 4194304 | tf_op jit(solution)/shard_map/pallas_call | solution.py:385
  (1 shorter events, 0.0 us)
Async XLA Ops:
  0.6 14.8 %copy-start.2 = (f32[32]{0:T(128)S(1)}, f32[32]{0:T(128)}, u32[]{:S(2)}) copy-start(f32[32]{0:T(128)} %step_ref.1) | copy-start | bytes 388
  0.6 14.8 %copy-start.1 = (s32[64]{0:T(128)S(1)}, s32[64]{0:T(128)}, u32[]{:S(2)}) copy-start(s32[64]{0:T(128)} %blocks_ref.1) | copy-start | bytes 772
  0.7 14.8 %copy-start = (s32[64]{0:T(128)S(1)}, s32[64]{0:T(128)}, u32[]{:S(2)}) copy-start(s32[64]{0:T(128)} %noise_ref.1) | copy-start | bytes 772
  2.8 34.8 %all-to-all-start = ((bf16[32,8,1536]{2,1,0:T(8,128)(2,1)}), bf16[32,8,1536]{2,1,0:T(8,128)(2,1)S(1)}, u32[]{:S(2)}, u32[]{:S(2)}) async-start(bf16[32,8,1536]{2,1,0:T(8,128)(2,1)} %bitcast.9), calls=%async_computation | async-start | bytes 1572864 | tf_op jit(solution)/shard_map/all_to_all | solution.py:441
  21.9 27.7 %collective-permute-start.1 = (bf16[1152,128]{1,0:T(8,128)(2,1)}, bf16[1152,128]{1,0:T(8,128)(2,1)S(1)}, u32[]{:S(2)}, u32[]{:S(2)}) collective-permute-start(bf16[1152,128]{1,0:T(8,128)(2,1)} %get-tuple-element.49), channel_id=1, source_target_pairs={{0,0},{1,1},{2,2},{3,3},{4,8},{5,9},{6,10},{7,11},{8,4},{9,5},{10,... | collective-permute-start | bytes 884744 | tf_op jit(solution)/shard_map/ppermute | solution.py:426
  25.0 24.7 %collective-permute-start.2 = (bf16[1152,128]{1,0:T(8,128)(2,1)S(1)}, bf16[1152,128]{1,0:T(8,128)(2,1)S(1)}, u32[]{:S(2)}, u32[]{:S(2)}) collective-permute-start(bf16[1152,128]{1,0:T(8,128)(2,1)S(1)} %get-tuple-element.50), channel_id=1, source_target_pairs={{0,1},{1,0},{2,3},{3,2},{4,9},{5,8},{6,11},{7,10},{8,5},{9,4},{10,... | collective-permute-start | bytes 884744 | tf_op jit(solution)/shard_map/ppermute | solution.py:426
  26.7 23.0 %collective-permute-start.3 = (bf16[1152,128]{1,0:T(8,128)(2,1)S(1)}, bf16[1152,128]{1,0:T(8,128)(2,1)S(1)}, u32[]{:S(2)}, u32[]{:S(2)}) collective-permute-start(bf16[1152,128]{1,0:T(8,128)(2,1)S(1)} %get-tuple-element.51), channel_id=1, source_target_pairs={{0,2},{1,3},{2,0},{3,1},{4,10},{5,11},{6,8},{7,9},{8,6},{9,7},{10,... | collective-permute-start | bytes 884744 | tf_op jit(solution)/shard_map/ppermute | solution.py:426
  30.2 19.5 %collective-permute-start.4 = (bf16[1152,128]{1,0:T(8,128)(2,1)S(1)}, bf16[1152,128]{1,0:T(8,128)(2,1)S(1)}, u32[]{:S(2)}, u32[]{:S(2)}) collective-permute-start(bf16[1152,128]{1,0:T(8,128)(2,1)S(1)} %get-tuple-element.52), channel_id=1, source_target_pairs={{0,3},{1,2},{2,1},{3,0},{4,11},{5,10},{6,9},{7,8},{8,7},{9,6},{10,... | collective-permute-start | bytes 884744 | tf_op jit(solution)/shard_map/ppermute | solution.py:426
  30.4 19.3 %collective-permute-start = (bf16[128,1536]{1,0:T(8,128)(2,1)}, bf16[128,1536]{1,0:T(8,128)(2,1)S(1)}, u32[]{:S(2)}, u32[]{:S(2)}) collective-permute-start(bf16[128,1536]{1,0:T(8,128)(2,1)} %get-tuple-element.48), channel_id=1, source_target_pairs={{8,0},{16,8},{24,16},{32,24},{40,32},{48,40},{56,48},{64,56},{72,6... | collective-permute-start | bytes 1179656 | tf_op jit(solution)/shard_map/ppermute | solution.py:485
  44.2 20.8 %all-to-all-start.1 = ((bf16[32,8,896]{2,1,0:T(8,128)(2,1)}), bf16[32,8,896]{2,1,0:T(8,128)(2,1)S(1)}, u32[]{:S(2)}, u32[]{:S(2)}) async-start(bf16[32,8,896]{2,1,0:T(8,128)(2,1)} %bitcast.10), calls=%async_computation.1 | async-start | bytes 917504 | tf_op jit(solution)/shard_map/all_to_all | solution.py:510
  49.7 1.7 %collective-permute-start.5 = (bf16[1152,128]{1,0:T(8,128)(2,1)S(1)}, bf16[1152,128]{1,0:T(8,128)(2,1)S(1)}, u32[]{:S(2)}, u32[]{:S(2)}) collective-permute-start(bf16[1152,128]{1,0:T(8,128)(2,1)S(1)} %collective-permute-done.1.refs_0_), channel_id=1, source_target_pairs={{0,8},{8,0},{16,24},{24,16},{32,40},{40,32},{48,56},{56,48},{64,72... | collective-permute-start | bytes 884744 | tf_op jit(solution)/shard_map/ppermute | solution.py:509
  50.2 1.6 %collective-permute-start.6 = (bf16[1152,128]{1,0:T(8,128)(2,1)S(1)}, bf16[1152,128]{1,0:T(8,128)(2,1)S(1)}, u32[]{:S(2)}, u32[]{:S(2)}) collective-permute-start(bf16[1152,128]{1,0:T(8,128)(2,1)S(1)} %collective-permute-done.2.refs_1_), channel_id=1, source_target_pairs={{0,8},{8,0},{16,24},{24,16},{32,40},{40,32},{48,56},{56,48},{64,72... | collective-permute-start | bytes 884744 | tf_op jit(solution)/shard_map/ppermute | solution.py:509
  50.3 1.9 %collective-permute-start.7 = (bf16[1152,128]{1,0:T(8,128)(2,1)S(1)}, bf16[1152,128]{1,0:T(8,128)(2,1)S(1)}, u32[]{:S(2)}, u32[]{:S(2)}) collective-permute-start(bf16[1152,128]{1,0:T(8,128)(2,1)S(1)} %collective-permute-done.3.refs_2_), channel_id=1, source_target_pairs={{0,8},{8,0},{16,24},{24,16},{32,40},{40,32},{48,56},{56,48},{64,72... | collective-permute-start | bytes 884744 | tf_op jit(solution)/shard_map/ppermute | solution.py:509
  50.7 2.0 %collective-permute-start.8 = (bf16[1152,128]{1,0:T(8,128)(2,1)S(1)}, bf16[1152,128]{1,0:T(8,128)(2,1)S(1)}, u32[]{:S(2)}, u32[]{:S(2)}) collective-permute-start(bf16[1152,128]{1,0:T(8,128)(2,1)S(1)} %collective-permute-done.4.refs_3_), channel_id=1, source_target_pairs={{0,8},{8,0},{16,24},{24,16},{32,40},{40,32},{48,56},{56,48},{64,72... | collective-permute-start | bytes 884744 | tf_op jit(solution)/shard_map/ppermute | solution.py:509
  56.0 10.8 %collective-permute-start.9 = (bf16[400,128]{1,0:T(8,128)(2,1)S(1)}, bf16[400,128]{1,0:T(8,128)(2,1)S(1)}, u32[]{:S(2)}, u32[]{:S(2)}) collective-permute-start(bf16[400,128]{1,0:T(8,128)(2,1)S(1)} %get-tuple-element.62), channel_id=1, source_target_pairs={{0,0},{1,1},{2,2},{3,3},{4,8},{5,9},{6,10},{7,11},{8,4},{9,5},{10,... | collective-permute-start | bytes 307208 | tf_op jit(solution)/shard_map/ppermute | solution.py:426
  59.6 7.2 %collective-permute-start.10 = (bf16[400,128]{1,0:T(8,128)(2,1)S(1)}, bf16[400,128]{1,0:T(8,128)(2,1)S(1)}, u32[]{:S(2)}, u32[]{:S(2)}) collective-permute-start(bf16[400,128]{1,0:T(8,128)(2,1)S(1)} %get-tuple-element.63), channel_id=1, source_target_pairs={{0,1},{1,0},{2,3},{3,2},{4,9},{5,8},{6,11},{7,10},{8,5},{9,4},{10,... | collective-permute-start | bytes 307208 | tf_op jit(solution)/shard_map/ppermute | solution.py:426
  60.7 7.1 %collective-permute-start.11 = (bf16[400,128]{1,0:T(8,128)(2,1)S(1)}, bf16[400,128]{1,0:T(8,128)(2,1)S(1)}, u32[]{:S(2)}, u32[]{:S(2)}) collective-permute-start(bf16[400,128]{1,0:T(8,128)(2,1)S(1)} %get-tuple-element.64), channel_id=1, source_target_pairs={{0,2},{1,3},{2,0},{3,1},{4,10},{5,11},{6,8},{7,9},{8,6},{9,7},{10,... | collective-permute-start | bytes 307208 | tf_op jit(solution)/shard_map/ppermute | solution.py:426
  64.2 6.2 %collective-permute-start.12 = (bf16[400,128]{1,0:T(8,128)(2,1)S(1)}, bf16[400,128]{1,0:T(8,128)(2,1)S(1)}, u32[]{:S(2)}, u32[]{:S(2)}) collective-permute-start(bf16[400,128]{1,0:T(8,128)(2,1)S(1)} %get-tuple-element.65), channel_id=1, source_target_pairs={{0,3},{1,2},{2,1},{3,0},{4,11},{5,10},{6,9},{7,8},{8,7},{9,6},{10,... | collective-permute-start | bytes 307208 | tf_op jit(solution)/shard_map/ppermute | solution.py:426
  71.4 9.4 %collective-permute-start.13 = (bf16[128,768]{1,0:T(8,128)(2,1)S(1)}, bf16[128,768]{1,0:T(8,128)(2,1)S(1)}, u32[]{:S(2)}, u32[]{:S(2)}) collective-permute-start(bf16[128,768]{1,0:T(8,128)(2,1)S(1)} %get-tuple-element.75), channel_id=1, source_target_pairs={{8,0},{16,8},{24,16},{32,24},{40,32},{48,40},{56,48},{64,56},{72,6... | collective-permute-start | bytes 589832 | tf_op jit(solution)/shard_map/ppermute | solution.py:549

commit v7 on v6

--- a/solution.py
+++ b/solution.py
@@ -48,10 +48,10 @@
 def finish(weights, total, top, v, may_be_empty):
     mixed = matmul(weights, v)
     if not may_be_empty:
-        return mixed / total, top * BASE2 + jnp.log2(total)
+        return mixed * (1.0 / total), top * BASE2 + jnp.log2(total)
     some = total > 0.0
     safe = jnp.where(some, total, 1.0)
-    return mixed / safe, jnp.where(some, top * BASE2 + jnp.log2(safe), MASKED)
+    return mixed * (1.0 / safe), jnp.where(some, top * BASE2 + jnp.log2(safe), MASKED)
 
 
 def attend(q, k, v):
@@ -63,6 +63,11 @@
     rest = x - one
     two = rest.astype(BF16).astype(F32)
     return one, two, rest - two
+
+
+def packed(tile, step):
+    one, two, three = split3(tile)
+    return one + pltpu.roll(two, step, 1) + pltpu.roll(three, 2 * step, 1)
 
 
 def swap_halves(even, odd):
@@ -199,10 +204,9 @@
             for d in range(2):
                 half = slice(d * tokens, (d + 1) * tokens)
                 outs[s + d][r] = mixed[half]
-                for n, piece in enumerate(split3(logs[half])):
-                    stats[s + d] = jnp.where(lane == SPAN * u + n, piece, stats[s + d])
+                stats[s + d] = jnp.where(lane == u, logs[half], stats[s + d])
     for d in range(RANKS):
-        turned = jnp.transpose(stats[d])[0:STAT_ROWS]
+        turned = jnp.transpose(packed(stats[d], 4))[0:STAT_ROWS]
         outs[d][SPAN * tokens : SPAN * tokens + STAT_ROWS] = turned.astype(BF16)
 
 
@@ -247,9 +251,8 @@
         mixed, logs = finish(weights, total, top, v[:, own], True)
         out_ref[:, own] = mixed.astype(BF16)
         send(h)
-        for m, piece in enumerate(split3(logs)):
-            stats = jnp.where(lane == 8 * m + h, piece, stats)
-    out_ref[:, HEADS * HEAD_DIM :] = stats.astype(BF16)
+        stats = jnp.where(lane == h, logs, stats)
+    out_ref[:, HEADS * HEAD_DIM :] = packed(stats, 8).astype(BF16)
     send(HEADS)
     for copy in copies:
         copy.wait()
@@ -280,8 +283,8 @@
     log_rows = []
     for h in range(HEADS):
         st = space_ref[2 * f + h // SPAN, SPAN * tokens : SPAN * tokens + STAT_ROWS].astype(F32)
-        b = SPAN * (h % SPAN)
-        log_rows.append(st[b : b + 1] + st[b + 1 : b + 2] + st[b + 2 : b + 3])
+        b = h % SPAN
+        log_rows.append(st[b : b + 1] + st[b + 4 : b + 5] + st[b + 8 : b + 9])
     log_rows.append(jnp.zeros((8 - HEADS, HEAD_DIM), F32))
     space_log = jnp.transpose(jnp.concatenate(log_rows, axis=0))
     of_space = 1.0 / (1.0 + jnp.exp2(time_log - space_log))

time: 83.2 us -> 83 us (level)
  no operation moved by 1% of the time
where the time goes in v7:
time: 83 us; the launch traced here: 82.6 us
  starting transfers between devices  39.3 us (47%)
  Pallas kernels  26.2 us (32%)
  waiting for transfers between devices  15.4 us (19%)
  between operations  1.64 us (2%)
    pallas_call x9, Pallas kernels, call(): pl.pallas_call(kernel, out_shape=outs, in_specs=in_specs, out_specs=out_s...  26.2 us
    ppermute x8, starting transfers between devices, exchange(): return lax.ppermute(x, ('tm', 'tok'), pairs)  17 us
    all_to_all x1, starting transfers between devices, body(): lax.all_to_all(outgoing.reshape(times, frames * share, width), 'tm', 0, 0)  11.9 us
    all_to_all x1, starting transfers between devices, body(): lax.all_to_all(back.reshape(times, frames * share, inner + HEAD_DIM), 'tm...  5.42 us
    all_to_all x1, waiting for transfers between devices, body(): lax.all_to_all(outgoing.reshape(times, frames * share, width), 'tm', 0, 0)  5.3 us
    ppermute x1, waiting for transfers between devices, body(): next_first = lax.ppermute(sent, 'tm', back_perm)  4.01 us
    ppermute x8, waiting for transfers between devices, exchange(): return lax.ppermute(x, ('tm', 'tok'), pairs)  3.54 us
    ppermute x1, starting transfers between devices, body(): next_first = lax.ppermute(sent, 'tm', back_perm)  1.92 us
  transfers between devices with their start and end apart: 16, of which 9 were waited for; matrix products, arithmetic and copies ran while one was open for 0% of the time, Pallas kernels for 26%

profile of v7, /device:TPU:5, one launch (start us, length us, event | category | flops | bytes accessed | tf_op | source)
XLA Modules:
  0.0 82.6 jit_solution(16347171779070856956)
XLA Ops:
  0.6 0.0 copy-start.2
  0.6 0.0 copy-start.1
  0.7 0.0 copy-start
  0.7 2.1 %shard_map.122 = (bf16[16,2,8,1536]{3,2,1,0:T(8,128)(2,1)}, bf16[128,1536]{1,0:T(8,128)(2,1)}, bf16[2,128,1536]{2,1,0:T(8,128)(2,1)S(1)}) custom-call(bf16[2,128,1536]{2,1,0:T(8,128)(2,1)} %refs_10_.1), custom_call_target="tpu_custom_call" | custom-call | bytes 2097152 | tf_op jit(solution)/shard_map/pallas_call | solution.py:388
  2.8 11.9 %all-to-all-start = ((bf16[32,8,1536]{2,1,0:T(8,128)(2,1)}), bf16[32,8,1536]{2,1,0:T(8,128)(2,1)S(1)}, u32[]{:S(2)}, u32[]{:S(2)}) async-start(bf16[32,8,1536]{2,1,0:T(8,128)(2,1)} %bitcast.9), calls=%async_computation | async-start | bytes 1572864 | tf_op jit(solution)/shard_map/all_to_all | solution.py:444
  15.4 0.1 pad_add_fusion.place_ref
  15.5 0.0 copy-done.2
  15.5 0.0 copy-done.1
  15.5 0.0 copy-done
  15.5 6.4 %shard_map.123 = (f32[3]{0:T(128)S(1)}, f32[16,1536]{1,0:T(8,128)}, f32[32,2,1536]{2,1,0:T(2,128)}, f32[32,2,1536]{2,1,0:T(2,128)}, f32[256,256]{1,0:T(8,128)}, ...) custom-call(s32[64]{0:T(128)S(1)} %copy-done, ...), custom_call_target="tpu_custom_call" | custom-call | flops 60000002048 | bytes 10485760 | tf_op jit(solution)/shard_map/pallas_call | solution.py:388
  21.9 3.1 %collective-permute-start.1 = (bf16[1152,128]{1,0:T(8,128)(2,1)}, bf16[1152,128]{1,0:T(8,128)(2,1)S(1)}, u32[]{:S(2)}, u32[]{:S(2)}) collective-permute-start(bf16[1152,128]{1,0:T(8,128)(2,1)} %get-tuple-element.49), channel_id=1, source_target_pairs={{0,0},{1,1},{2,2},{3,3},{4,8},{5,9},{6,10},{7,11},{8,4},{9,5},{10,... | collective-permute-start | bytes 884744 | tf_op jit(solution)/shard_map/ppermute | solution.py:429
  25.0 1.7 %collective-permute-start.2 = (bf16[1152,128]{1,0:T(8,128)(2,1)S(1)}, bf16[1152,128]{1,0:T(8,128)(2,1)S(1)}, u32[]{:S(2)}, u32[]{:S(2)}) collective-permute-start(bf16[1152,128]{1,0:T(8,128)(2,1)S(1)} %get-tuple-element.50), channel_id=1, source_target_pairs={{0,1},{1,0},{2,3},{3,2},{4,9},{5,8},{6,11},{7,10},{8,5},{9,4},{10,... | collective-permute-start | bytes 884744 | tf_op jit(solution)/shard_map/ppermute | solution.py:429
  26.7 3.5 %collective-permute-start.3 = (bf16[1152,128]{1,0:T(8,128)(2,1)S(1)}, bf16[1152,128]{1,0:T(8,128)(2,1)S(1)}, u32[]{:S(2)}, u32[]{:S(2)}) collective-permute-start(bf16[1152,128]{1,0:T(8,128)(2,1)S(1)} %get-tuple-element.51), channel_id=1, source_target_pairs={{0,2},{1,3},{2,0},{3,1},{4,10},{5,11},{6,8},{7,9},{8,6},{9,7},{10,... | collective-permute-start | bytes 884744 | tf_op jit(solution)/shard_map/ppermute | solution.py:429
  30.2 0.2 collective-permute-start.4
  30.4 1.9 %collective-permute-start = (bf16[128,1536]{1,0:T(8,128)(2,1)}, bf16[128,1536]{1,0:T(8,128)(2,1)S(1)}, u32[]{:S(2)}, u32[]{:S(2)}) collective-permute-start(bf16[128,1536]{1,0:T(8,128)(2,1)} %get-tuple-element.48), channel_id=1, source_target_pairs={{8,0},{16,8},{24,16},{32,24},{40,32},{48,40},{56,48},{64,56},{72,6... | collective-permute-start | bytes 1179656 | tf_op jit(solution)/shard_map/ppermute | solution.py:488
  32.3 5.3 %all-to-all-done.x_ref = bf16[32,8,1536]{2,1,0:T(8,128)(2,1)S(1)} async-done(((bf16[32,8,1536]{2,1,0:T(8,128)(2,1)}), bf16[32,8,1536]{2,1,0:T(8,128)(2,1)S(1)}, u32[]{:S(2)}, u32[]{:S(2)}) %all-to-all-start) | async-done | bytes 786464 | tf_op jit(solution)/shard_map/all_to_all | solution.py:444
  37.6 6.6 %shard_map.124 = bf16[256,896]{1,0:T(8,128)(2,1)} custom-call(bf16[32,8,1536]{2,1,0:T(8,128)(2,1)S(1)} %all-to-all-done.x_ref, f32[32,2,1536]{2,1,0:T(2,128)} %get-tuple-element.45.refs_0_, f32[32,2,1536]{2,1,0:T(2,128)} %get-tuple-element.46.refs_1_, bf16[1536,768]{1,0:T(8,128)(2,1)} %refs_2_.1, bf16[1536,768]{1,0:T(8,128)(2,1)} %refs_3_.1, ...), custom_call_target="tpu_custom_call" | custom-call | flops 60000002048 | bytes 10485760 | tf_op jit(solution)/shard_map/pallas_call | solution.py:388
  44.2 5.4 %all-to-all-start.1 = ((bf16[32,8,896]{2,1,0:T(8,128)(2,1)}), bf16[32,8,896]{2,1,0:T(8,128)(2,1)S(1)}, u32[]{:S(2)}, u32[]{:S(2)}) async-start(bf16[32,8,896]{2,1,0:T(8,128)(2,1)} %bitcast.10), calls=%async_computation.1 | async-start | bytes 917504 | tf_op jit(solution)/shard_map/all_to_all | solution.py:513
  49.6 0.0 collective-permute-done.1.refs_0_
  49.7 0.0 collective-permute-done.2.refs_1_
  49.7 0.0 collective-permute-done.3.refs_2_
  49.7 0.0 collective-permute-done.4.refs_3_
  49.7 0.0 collective-permute-done.refs_9_
  49.7 0.4 collective-permute-start.5
  50.2 0.1 collective-permute-start.6
  50.3 0.4 collective-permute-start.7
  50.7 0.1 collective-permute-start.8
  50.8 0.6 collective-permute-done.5.refs_4_
  51.4 0.4 collective-permute-done.6.refs_5_
  51.8 0.4 collective-permute-done.7.refs_6_
  52.2 0.4 collective-permute-done.8.refs_7_
  52.6 3.2 %shard_map.126 = (bf16[400,128]{1,0:T(8,128)(2,1)S(1)}, bf16[400,128]{1,0:T(8,128)(2,1)S(1)}, bf16[400,128]{1,0:T(8,128)(2,1)S(1)}, bf16[400,128]{1,0:T(8,128)(2,1)S(1)}) custom-call(bf16[1152,128]{1,0:T(8,128)(2,1)S(1)} %collective-permute-done.1.refs_0_, bf16[1152,128]{1,0:T(8,128)(2,1)S(1)} %collective-permute-done.2.refs_1_, ...), custom_call_target="tpu_custom_call" | custom-call | flops 805306368 | bytes 3145728 | tf_op jit(solution)/shard_map/pallas_call | solution.py:388
  55.8 3.6 %collective-permute-start.9 = (bf16[400,128]{1,0:T(8,128)(2,1)S(1)}, bf16[400,128]{1,0:T(8,128)(2,1)S(1)}, u32[]{:S(2)}, u32[]{:S(2)}) collective-permute-start(bf16[400,128]{1,0:T(8,128)(2,1)S(1)} %get-tuple-element.62), channel_id=1, source_target_pairs={{0,0},{1,1},{2,2},{3,3},{4,8},{5,9},{6,10},{7,11},{8,4},{9,5},{10,... | collective-permute-start | bytes 307208 | tf_op jit(solution)/shard_map/ppermute | solution.py:429
  59.5 1.1 %collective-permute-start.10 = (bf16[400,128]{1,0:T(8,128)(2,1)S(1)}, bf16[400,128]{1,0:T(8,128)(2,1)S(1)}, u32[]{:S(2)}, u32[]{:S(2)}) collective-permute-start(bf16[400,128]{1,0:T(8,128)(2,1)S(1)} %get-tuple-element.63), channel_id=1, source_target_pairs={{0,1},{1,0},{2,3},{3,2},{4,9},{5,8},{6,11},{7,10},{8,5},{9,4},{10,... | collective-permute-start | bytes 307208 | tf_op jit(solution)/shard_map/ppermute | solution.py:429
  60.6 3.5 %collective-permute-start.11 = (bf16[400,128]{1,0:T(8,128)(2,1)S(1)}, bf16[400,128]{1,0:T(8,128)(2,1)S(1)}, u32[]{:S(2)}, u32[]{:S(2)}) collective-permute-start(bf16[400,128]{1,0:T(8,128)(2,1)S(1)} %get-tuple-element.64), channel_id=1, source_target_pairs={{0,2},{1,3},{2,0},{3,1},{4,10},{5,11},{6,8},{7,9},{8,6},{9,7},{10,... | collective-permute-start | bytes 307208 | tf_op jit(solution)/shard_map/ppermute | solution.py:429
  64.1 0.2 collective-permute-start.12
  64.3 0.7 all-to-all-done.1
  65.0 1.7 %shard_map.127 = (bf16[2,128,768]{2,1,0:T(8,128)(2,1)S(1)}, f32[2,128,128]{2,1,0:T(8,128)S(1)}, bf16[768,1536]{1,0:T(8,128)(2,1)S(1)}, f32[16,1536]{1,0:T(8,128)S(1)}) custom-call(bf16[256,896]{1,0:T(8,128)(2,1)S(1)} %bitcast.7, bf16[768,1536]{1,0:T(8,128)(2,1)} %wo_hbm.1, f32[16,1536]{1,0:T(8,128)} %get-tuple-element.66.own_hbm), custom_call_target="tpu_custom_call" | custom-call | flops 60000002048 | bytes 1048576 | tf_op jit(solution)/shard_map/pallas_call | solution.py:388
  66.7 0.0 collective-permute-done.9.refs_0_
  66.8 0.0 collective-permute-done.10.refs_1_
  66.8 0.9 %collective-permute-done.11.refs_2_ = bf16[400,128]{1,0:T(8,128)(2,1)S(1)} collective-permute-done((bf16[400,128]{1,0:T(8,128)(2,1)S(1)}, bf16[400,128]{1,0:T(8,128)(2,1)S(1)}, u32[]{:S(2)}, u32[]{:S(2)}) %collective-permute-start.11) | collective-permute-done | bytes 102432 | tf_op jit(solution)/shard_map/ppermute | solution.py:429
  67.7 2.6 %collective-permute-done.12.refs_3_ = bf16[400,128]{1,0:T(8,128)(2,1)S(1)} collective-permute-done((bf16[400,128]{1,0:T(8,128)(2,1)S(1)}, bf16[400,128]{1,0:T(8,128)(2,1)S(1)}, u32[]{:S(2)}, u32[]{:S(2)}) %collective-permute-start.12) | collective-permute-done | bytes 102432 | tf_op jit(solution)/shard_map/ppermute | solution.py:429
  70.3 1.0 %shard_map.128 = (bf16[128,768]{1,0:T(8,128)(2,1)S(1)}, bf16[128,768]{1,0:T(8,128)(2,1)S(1)}) custom-call(s32[3]{0:T(128)S(1)} %pad_add_fusion.place_ref, f32[1,32]{1,0:T(1,128)S(1)} %shard_map.125.mark_ref, bf16[400,128]{1,0:T(8,128)(2,1)S(1)} %collective-permute-done.9.refs_0_, bf16[400,128]{1,0:T(8,128)(2,1)S(1)} %collective-permute-done.10.refs_1_, ...), custom_call_target="tpu_custom_call" | custom-call | bytes 2097152 | tf_op jit(solution)/shard_map/pallas_call | solution.py:388
  71.3 1.9 %collective-permute-start.13 = (bf16[128,768]{1,0:T(8,128)(2,1)S(1)}, bf16[128,768]{1,0:T(8,128)(2,1)S(1)}, u32[]{:S(2)}, u32[]{:S(2)}) collective-permute-start(bf16[128,768]{1,0:T(8,128)(2,1)S(1)} %get-tuple-element.75), channel_id=1, source_target_pairs={{8,0},{16,8},{24,16},{32,24},{40,32},{48,40},{56,48},{64,56},{72,6... | collective-permute-start | bytes 589832 | tf_op jit(solution)/shard_map/ppermute | solution.py:552
  73.2 3.4 %shard_map.129 = (bf16[2,128,1536]{2,1,0:T(8,128)(2,1)}, bf16[2,128,1536]{2,1,0:T(8,128)(2,1)}, bf16[128,1536]{1,0:T(8,128)(2,1)S(1)}) custom-call(s32[3]{0:T(128)S(1)} %pad_add_fusion.place_ref, f32[3]{0:T(128)S(1)} %get-tuple-element.43.size_ref, bf16[400,128]{1,0:T(8,128)(2,1)S(1)} %collective-permute-done.9.refs_0_, ...), custom_call_target="tpu_custom_call" | custom-call | flops 603979776 | bytes 6291456 | tf_op jit(solution)/shard_map/pallas_call | solution.py:388
  76.7 4.0 %collective-permute-done.13.att_ref = bf16[128,768]{1,0:T(8,128)(2,1)S(1)} collective-permute-done((bf16[128,768]{1,0:T(8,128)(2,1)S(1)}, bf16[128,768]{1,0:T(8,128)(2,1)S(1)}, u32[]{:S(2)}, u32[]{:S(2)}) %collective-permute-start.13) | collective-permute-done | bytes 196640 | tf_op jit(solution)/shard_map/ppermute | solution.py:552
  80.7 1.7 %shard_map.130 = bf16[2,128,1536]{2,1,0:T(8,128)(2,1)} custom-call(f32[3]{0:T(128)S(1)} %get-tuple-element.43.size_ref, bf16[128,768]{1,0:T(8,128)(2,1)S(1)} %collective-permute-done.13.att_ref, bf16[768,1536]{1,0:T(8,128)(2,1)S(1)} %get-tuple-element.71.refs_7_.wo_ref, ...), custom_call_target="tpu_custom_call", output_to_operand_aliasing={{}: (5, {})} | custom-call | flops 301989888 | bytes 4194304 | tf_op jit(solution)/shard_map/pallas_call | solution.py:388
  (1 shorter events, 0.0 us)
Async XLA Ops:
  0.6 14.8 %copy-start.2 = (f32[32]{0:T(128)S(1)}, f32[32]{0:T(128)}, u32[]{:S(2)}) copy-start(f32[32]{0:T(128)} %step_ref.1) | copy-start | bytes 388
  0.6 14.8 %copy-start.1 = (s32[64]{0:T(128)S(1)}, s32[64]{0:T(128)}, u32[]{:S(2)}) copy-start(s32[64]{0:T(128)} %blocks_ref.1) | copy-start | bytes 772
  0.7 14.8 %copy-start = (s32[64]{0:T(128)S(1)}, s32[64]{0:T(128)}, u32[]{:S(2)}) copy-start(s32[64]{0:T(128)} %noise_ref.1) | copy-start | bytes 772
  2.8 34.8 %all-to-all-start = ((bf16[32,8,1536]{2,1,0:T(8,128)(2,1)}), bf16[32,8,1536]{2,1,0:T(8,128)(2,1)S(1)}, u32[]{:S(2)}, u32[]{:S(2)}) async-start(bf16[32,8,1536]{2,1,0:T(8,128)(2,1)} %bitcast.9), calls=%async_computation | async-start | bytes 1572864 | tf_op jit(solution)/shard_map/all_to_all | solution.py:444
  21.9 27.7 %collective-permute-start.1 = (bf16[1152,128]{1,0:T(8,128)(2,1)}, bf16[1152,128]{1,0:T(8,128)(2,1)S(1)}, u32[]{:S(2)}, u32[]{:S(2)}) collective-permute-start(bf16[1152,128]{1,0:T(8,128)(2,1)} %get-tuple-element.49), channel_id=1, source_target_pairs={{0,0},{1,1},{2,2},{3,3},{4,8},{5,9},{6,10},{7,11},{8,4},{9,5},{10,... | collective-permute-start | bytes 884744 | tf_op jit(solution)/shard_map/ppermute | solution.py:429
  25.0 24.7 %collective-permute-start.2 = (bf16[1152,128]{1,0:T(8,128)(2,1)S(1)}, bf16[1152,128]{1,0:T(8,128)(2,1)S(1)}, u32[]{:S(2)}, u32[]{:S(2)}) collective-permute-start(bf16[1152,128]{1,0:T(8,128)(2,1)S(1)} %get-tuple-element.50), channel_id=1, source_target_pairs={{0,1},{1,0},{2,3},{3,2},{4,9},{5,8},{6,11},{7,10},{8,5},{9,4},{10,... | collective-permute-start | bytes 884744 | tf_op jit(solution)/shard_map/ppermute | solution.py:429
  26.7 23.0 %collective-permute-start.3 = (bf16[1152,128]{1,0:T(8,128)(2,1)S(1)}, bf16[1152,128]{1,0:T(8,128)(2,1)S(1)}, u32[]{:S(2)}, u32[]{:S(2)}) collective-permute-start(bf16[1152,128]{1,0:T(8,128)(2,1)S(1)} %get-tuple-element.51), channel_id=1, source_target_pairs={{0,2},{1,3},{2,0},{3,1},{4,10},{5,11},{6,8},{7,9},{8,6},{9,7},{10,... | collective-permute-start | bytes 884744 | tf_op jit(solution)/shard_map/ppermute | solution.py:429
  30.2 19.5 %collective-permute-start.4 = (bf16[1152,128]{1,0:T(8,128)(2,1)S(1)}, bf16[1152,128]{1,0:T(8,128)(2,1)S(1)}, u32[]{:S(2)}, u32[]{:S(2)}) collective-permute-start(bf16[1152,128]{1,0:T(8,128)(2,1)S(1)} %get-tuple-element.52), channel_id=1, source_target_pairs={{0,3},{1,2},{2,1},{3,0},{4,11},{5,10},{6,9},{7,8},{8,7},{9,6},{10,... | collective-permute-start | bytes 884744 | tf_op jit(solution)/shard_map/ppermute | solution.py:429
  30.4 19.3 %collective-permute-start = (bf16[128,1536]{1,0:T(8,128)(2,1)}, bf16[128,1536]{1,0:T(8,128)(2,1)S(1)}, u32[]{:S(2)}, u32[]{:S(2)}) collective-permute-start(bf16[128,1536]{1,0:T(8,128)(2,1)} %get-tuple-element.48), channel_id=1, source_target_pairs={{8,0},{16,8},{24,16},{32,24},{40,32},{48,40},{56,48},{64,56},{72,6... | collective-permute-start | bytes 1179656 | tf_op jit(solution)/shard_map/ppermute | solution.py:488
  44.2 20.8 %all-to-all-start.1 = ((bf16[32,8,896]{2,1,0:T(8,128)(2,1)}), bf16[32,8,896]{2,1,0:T(8,128)(2,1)S(1)}, u32[]{:S(2)}, u32[]{:S(2)}) async-start(bf16[32,8,896]{2,1,0:T(8,128)(2,1)} %bitcast.10), calls=%async_computation.1 | async-start | bytes 917504 | tf_op jit(solution)/shard_map/all_to_all | solution.py:513
  49.7 1.7 %collective-permute-start.5 = (bf16[1152,128]{1,0:T(8,128)(2,1)S(1)}, bf16[1152,128]{1,0:T(8,128)(2,1)S(1)}, u32[]{:S(2)}, u32[]{:S(2)}) collective-permute-start(bf16[1152,128]{1,0:T(8,128)(2,1)S(1)} %collective-permute-done.1.refs_0_), channel_id=1, source_target_pairs={{0,8},{8,0},{16,24},{24,16},{32,40},{40,32},{48,56},{56,48},{64,72... | collective-permute-start | bytes 884744 | tf_op jit(solution)/shard_map/ppermute | solution.py:512
  50.2 1.6 %collective-permute-start.6 = (bf16[1152,128]{1,0:T(8,128)(2,1)S(1)}, bf16[1152,128]{1,0:T(8,128)(2,1)S(1)}, u32[]{:S(2)}, u32[]{:S(2)}) collective-permute-start(bf16[1152,128]{1,0:T(8,128)(2,1)S(1)} %collective-permute-done.2.refs_1_), channel_id=1, source_target_pairs={{0,8},{8,0},{16,24},{24,16},{32,40},{40,32},{48,56},{56,48},{64,72... | collective-permute-start | bytes 884744 | tf_op jit(solution)/shard_map/ppermute | solution.py:512
  50.3 1.9 %collective-permute-start.7 = (bf16[1152,128]{1,0:T(8,128)(2,1)S(1)}, bf16[1152,128]{1,0:T(8,128)(2,1)S(1)}, u32[]{:S(2)}, u32[]{:S(2)}) collective-permute-start(bf16[1152,128]{1,0:T(8,128)(2,1)S(1)} %collective-permute-done.3.refs_2_), channel_id=1, source_target_pairs={{0,8},{8,0},{16,24},{24,16},{32,40},{40,32},{48,56},{56,48},{64,72... | collective-permute-start | bytes 884744 | tf_op jit(solution)/shard_map/ppermute | solution.py:512
  50.7 2.0 %collective-permute-start.8 = (bf16[1152,128]{1,0:T(8,128)(2,1)S(1)}, bf16[1152,128]{1,0:T(8,128)(2,1)S(1)}, u32[]{:S(2)}, u32[]{:S(2)}) collective-permute-start(bf16[1152,128]{1,0:T(8,128)(2,1)S(1)} %collective-permute-done.4.refs_3_), channel_id=1, source_target_pairs={{0,8},{8,0},{16,24},{24,16},{32,40},{40,32},{48,56},{56,48},{64,72... | collective-permute-start | bytes 884744 | tf_op jit(solution)/shard_map/ppermute | solution.py:512
  55.8 10.9 %collective-permute-start.9 = (bf16[400,128]{1,0:T(8,128)(2,1)S(1)}, bf16[400,128]{1,0:T(8,128)(2,1)S(1)}, u32[]{:S(2)}, u32[]{:S(2)}) collective-permute-start(bf16[400,128]{1,0:T(8,128)(2,1)S(1)} %get-tuple-element.62), channel_id=1, source_target_pairs={{0,0},{1,1},{2,2},{3,3},{4,8},{5,9},{6,10},{7,11},{8,4},{9,5},{10,... | collective-permute-start | bytes 307208 | tf_op jit(solution)/shard_map/ppermute | solution.py:429
  59.5 7.3 %collective-permute-start.10 = (bf16[400,128]{1,0:T(8,128)(2,1)S(1)}, bf16[400,128]{1,0:T(8,128)(2,1)S(1)}, u32[]{:S(2)}, u32[]{:S(2)}) collective-permute-start(bf16[400,128]{1,0:T(8,128)(2,1)S(1)} %get-tuple-element.63), channel_id=1, source_target_pairs={{0,1},{1,0},{2,3},{3,2},{4,9},{5,8},{6,11},{7,10},{8,5},{9,4},{10,... | collective-permute-start | bytes 307208 | tf_op jit(solution)/shard_map/ppermute | solution.py:429
  60.6 7.1 %collective-permute-start.11 = (bf16[400,128]{1,0:T(8,128)(2,1)S(1)}, bf16[400,128]{1,0:T(8,128)(2,1)S(1)}, u32[]{:S(2)}, u32[]{:S(2)}) collective-permute-start(bf16[400,128]{1,0:T(8,128)(2,1)S(1)} %get-tuple-element.64), channel_id=1, source_target_pairs={{0,2},{1,3},{2,0},{3,1},{4,10},{5,11},{6,8},{7,9},{8,6},{9,7},{10,... | collective-permute-start | bytes 307208 | tf_op jit(solution)/shard_map/ppermute | solution.py:429
  64.1 6.2 %collective-permute-start.12 = (bf16[400,128]{1,0:T(8,128)(2,1)S(1)}, bf16[400,128]{1,0:T(8,128)(2,1)S(1)}, u32[]{:S(2)}, u32[]{:S(2)}) collective-permute-start(bf16[400,128]{1,0:T(8,128)(2,1)S(1)} %get-tuple-element.65), channel_id=1, source_target_pairs={{0,3},{1,2},{2,1},{3,0},{4,11},{5,10},{6,9},{7,8},{8,7},{9,6},{10,... | collective-permute-start | bytes 307208 | tf_op jit(solution)/shard_map/ppermute | solution.py:429
  71.3 9.4 %collective-permute-start.13 = (bf16[128,768]{1,0:T(8,128)(2,1)S(1)}, bf16[128,768]{1,0:T(8,128)(2,1)S(1)}, u32[]{:S(2)}, u32[]{:S(2)}) collective-permute-start(bf16[128,768]{1,0:T(8,128)(2,1)S(1)} %get-tuple-element.75), channel_id=1, source_target_pairs={{8,0},{16,8},{24,16},{32,24},{40,32},{48,40},{56,48},{64,56},{72,6... | collective-permute-start | bytes 589832 | tf_op jit(solution)/shard_map/ppermute | solution.py:552

commit v8 on v7

--- a/solution.py
+++ b/solution.py
@@ -237,9 +237,9 @@
     lane = lax.broadcasted_iota(jnp.int32, (groups * rows, HEAD_DIM), 1)
     stats = jnp.zeros((groups * rows, HEAD_DIM), F32)
     heads = [slice(h * HEAD_DIM, (h + 1) * HEAD_DIM) for h in range(HEADS)]
-    parts = [softmax_parts(q[:, own], k[:, own], bias_ref[...]) for own in heads]
     loads[5].wait()
     v = matmul(normed, wv_ref[...]).astype(BF16)
+    parts = [softmax_parts(q[:, own], k[:, own], bias_ref[...]) for own in heads]
     copies = []
 
     def send(n):
@@ -439,7 +439,7 @@
         ),
         (anywhere(), anywhere(), whole()),
         nbytes=2 * MIB,
-        scratch_shapes=[pltpu.VMEM((tokens // 8, 2, 8, width), BF16), dma((4,)), dma((4,)), dma],
+        scratch_shapes=[pltpu.VMEM((tokens // 8, 2, 8, width), BF16), dma((8,)), dma((8,)), dma],
     )
     column = lax.all_to_all(outgoing.reshape(times, frames * share, width), "tm", 0, 0)
 

time: 83 us -> 82.6 us (level)
  transfers between devices with their start and end apart: 16 -> 16, of which waited for: 9 -> 9; matrix products, arithmetic and copies ran while one was open for 0% -> 0% of each run, Pallas kernels for 26% -> 25%
where the time goes in v8:
time: 82.6 us; the launch traced here: 82.1 us
  starting transfers between devices  39.7 us (48%)
  Pallas kernels  25.7 us (31%)
  waiting for transfers between devices  14.9 us (18%)
  between operations  1.64 us (2%)
    pallas_call x9, Pallas kernels, call(): pl.pallas_call(kernel, out_shape=outs, in_specs=in_specs, out_specs=out_s...  25.7 us
    ppermute x8, starting transfers between devices, exchange(): return lax.ppermute(x, ('tm', 'tok'), pairs)  17.5 us
    all_to_all x1, starting transfers between devices, body(): lax.all_to_all(outgoing.reshape(times, frames * share, width), 'tm', 0, 0)  11.9 us
    all_to_all x1, starting transfers between devices, body(): lax.all_to_all(back.reshape(times, frames * share, inner + HEAD_DIM), 'tm...  5.42 us
    all_to_all x1, waiting for transfers between devices, body(): lax.all_to_all(outgoing.reshape(times, frames * share, width), 'tm', 0, 0)  5.3 us
    ppermute x1, waiting for transfers between devices, body(): next_first = lax.ppermute(sent, 'tm', back_perm)  4.01 us
    ppermute x8, waiting for transfers between devices, exchange(): return lax.ppermute(x, ('tm', 'tok'), pairs)  3.52 us
    ppermute x1, starting transfers between devices, body(): next_first = lax.ppermute(sent, 'tm', back_perm)  1.92 us
  transfers between devices with their start and end apart: 16, of which 9 were waited for; matrix products, arithmetic and copies ran while one was open for 0% of the time, Pallas kernels for 25%

profile of v8, /device:TPU:5, one launch (start us, length us, event | category | flops | bytes accessed | tf_op | source)
XLA Modules:
  0.0 82.1 jit_solution(15177464532436255292)
XLA Ops:
  0.6 0.0 copy-start.2
  0.6 0.0 copy-start.1
  0.7 0.0 copy-start
  0.7 2.2 %shard_map.122 = (bf16[16,2,8,1536]{3,2,1,0:T(8,128)(2,1)}, bf16[128,1536]{1,0:T(8,128)(2,1)}, bf16[2,128,1536]{2,1,0:T(8,128)(2,1)S(1)}) custom-call(bf16[2,128,1536]{2,1,0:T(8,128)(2,1)} %refs_10_.1), custom_call_target="tpu_custom_call" | custom-call | bytes 2097152 | tf_op jit(solution)/shard_map/pallas_call | solution.py:388
  2.8 11.9 %all-to-all-start = ((bf16[32,8,1536]{2,1,0:T(8,128)(2,1)}), bf16[32,8,1536]{2,1,0:T(8,128)(2,1)S(1)}, u32[]{:S(2)}, u32[]{:S(2)}) async-start(bf16[32,8,1536]{2,1,0:T(8,128)(2,1)} %bitcast.9), calls=%async_computation | async-start | bytes 1572864 | tf_op jit(solution)/shard_map/all_to_all | solution.py:444
  15.4 0.1 pad_add_fusion.place_ref
  15.5 0.0 copy-done.2
  15.5 0.0 copy-done.1
  15.5 0.0 copy-done
  15.5 6.4 %shard_map.123 = (f32[3]{0:T(128)S(1)}, f32[16,1536]{1,0:T(8,128)}, f32[32,2,1536]{2,1,0:T(2,128)}, f32[32,2,1536]{2,1,0:T(2,128)}, f32[256,256]{1,0:T(8,128)}, ...) custom-call(s32[64]{0:T(128)S(1)} %copy-done, ...), custom_call_target="tpu_custom_call" | custom-call | flops 60000002048 | bytes 10485760 | tf_op jit(solution)/shard_map/pallas_call | solution.py:388
  21.9 3.1 %collective-permute-start.1 = (bf16[1152,128]{1,0:T(8,128)(2,1)}, bf16[1152,128]{1,0:T(8,128)(2,1)S(1)}, u32[]{:S(2)}, u32[]{:S(2)}) collective-permute-start(bf16[1152,128]{1,0:T(8,128)(2,1)} %get-tuple-element.49), channel_id=1, source_target_pairs={{0,0},{1,1},{2,2},{3,3},{4,8},{5,9},{6,10},{7,11},{8,4},{9,5},{10,... | collective-permute-start | bytes 884744 | tf_op jit(solution)/shard_map/ppermute | solution.py:429
  25.0 1.7 %collective-permute-start.2 = (bf16[1152,128]{1,0:T(8,128)(2,1)S(1)}, bf16[1152,128]{1,0:T(8,128)(2,1)S(1)}, u32[]{:S(2)}, u32[]{:S(2)}) collective-permute-start(bf16[1152,128]{1,0:T(8,128)(2,1)S(1)} %get-tuple-element.50), channel_id=1, source_target_pairs={{0,1},{1,0},{2,3},{3,2},{4,9},{5,8},{6,11},{7,10},{8,5},{9,4},{10,... | collective-permute-start | bytes 884744 | tf_op jit(solution)/shard_map/ppermute | solution.py:429
  26.7 3.5 %collective-permute-start.3 = (bf16[1152,128]{1,0:T(8,128)(2,1)S(1)}, bf16[1152,128]{1,0:T(8,128)(2,1)S(1)}, u32[]{:S(2)}, u32[]{:S(2)}) collective-permute-start(bf16[1152,128]{1,0:T(8,128)(2,1)S(1)} %get-tuple-element.51), channel_id=1, source_target_pairs={{0,2},{1,3},{2,0},{3,1},{4,10},{5,11},{6,8},{7,9},{8,6},{9,7},{10,... | collective-permute-start | bytes 884744 | tf_op jit(solution)/shard_map/ppermute | solution.py:429
  30.2 0.2 collective-permute-start.4
  30.4 1.9 %collective-permute-start = (bf16[128,1536]{1,0:T(8,128)(2,1)}, bf16[128,1536]{1,0:T(8,128)(2,1)S(1)}, u32[]{:S(2)}, u32[]{:S(2)}) collective-permute-start(bf16[128,1536]{1,0:T(8,128)(2,1)} %get-tuple-element.48), channel_id=1, source_target_pairs={{8,0},{16,8},{24,16},{32,24},{40,32},{48,40},{56,48},{64,56},{72,6... | collective-permute-start | bytes 1179656 | tf_op jit(solution)/shard_map/ppermute | solution.py:488
  32.4 5.3 %all-to-all-done.x_ref = bf16[32,8,1536]{2,1,0:T(8,128)(2,1)S(1)} async-done(((bf16[32,8,1536]{2,1,0:T(8,128)(2,1)}), bf16[32,8,1536]{2,1,0:T(8,128)(2,1)S(1)}, u32[]{:S(2)}, u32[]{:S(2)}) %all-to-all-start) | async-done | bytes 786464 | tf_op jit(solution)/shard_map/all_to_all | solution.py:444
  37.7 6.1 %shard_map.124 = bf16[256,896]{1,0:T(8,128)(2,1)} custom-call(bf16[32,8,1536]{2,1,0:T(8,128)(2,1)S(1)} %all-to-all-done.x_ref, f32[32,2,1536]{2,1,0:T(2,128)} %get-tuple-element.45.refs_0_, f32[32,2,1536]{2,1,0:T(2,128)} %get-tuple-element.46.refs_1_, bf16[1536,768]{1,0:T(8,128)(2,1)} %refs_2_.1, bf16[1536,768]{1,0:T(8,128)(2,1)} %refs_3_.1, ...), custom_call_target="tpu_custom_call" | custom-call | flops 60000002048 | bytes 10485760 | tf_op jit(solution)/shard_map/pallas_call | solution.py:388
  43.8 5.4 %all-to-all-start.1 = ((bf16[32,8,896]{2,1,0:T(8,128)(2,1)}), bf16[32,8,896]{2,1,0:T(8,128)(2,1)S(1)}, u32[]{:S(2)}, u32[]{:S(2)}) async-start(bf16[32,8,896]{2,1,0:T(8,128)(2,1)} %bitcast.10), calls=%async_computation.1 | async-start | bytes 917504 | tf_op jit(solution)/shard_map/all_to_all | solution.py:513
  49.2 0.0 collective-permute-done.1.refs_0_
  49.2 0.0 collective-permute-done.2.refs_1_
  49.2 0.0 collective-permute-done.3.refs_2_
  49.2 0.0 collective-permute-done.4.refs_3_
  49.2 0.0 collective-permute-done.refs_9_
  49.2 0.4 collective-permute-start.5
  49.7 0.1 collective-permute-start.6
  49.8 0.4 collective-permute-start.7
  50.2 0.1 collective-permute-start.8
  50.4 0.6 collective-permute-done.5.refs_4_
  50.9 0.4 collective-permute-done.6.refs_5_
  51.3 0.4 collective-permute-done.7.refs_6_
  51.8 0.4 collective-permute-done.8.refs_7_
  52.2 3.2 %shard_map.126 = (bf16[400,128]{1,0:T(8,128)(2,1)S(1)}, bf16[400,128]{1,0:T(8,128)(2,1)S(1)}, bf16[400,128]{1,0:T(8,128)(2,1)S(1)}, bf16[400,128]{1,0:T(8,128)(2,1)S(1)}) custom-call(bf16[1152,128]{1,0:T(8,128)(2,1)S(1)} %collective-permute-done.1.refs_0_, bf16[1152,128]{1,0:T(8,128)(2,1)S(1)} %collective-permute-done.2.refs_1_, ...), custom_call_target="tpu_custom_call" | custom-call | flops 805306368 | bytes 3145728 | tf_op jit(solution)/shard_map/pallas_call | solution.py:388
  55.4 4.1 %collective-permute-start.9 = (bf16[400,128]{1,0:T(8,128)(2,1)S(1)}, bf16[400,128]{1,0:T(8,128)(2,1)S(1)}, u32[]{:S(2)}, u32[]{:S(2)}) collective-permute-start(bf16[400,128]{1,0:T(8,128)(2,1)S(1)} %get-tuple-element.62), channel_id=1, source_target_pairs={{0,0},{1,1},{2,2},{3,3},{4,8},{5,9},{6,10},{7,11},{8,4},{9,5},{10,... | collective-permute-start | bytes 307208 | tf_op jit(solution)/shard_map/ppermute | solution.py:429
  59.5 0.6 collective-permute-start.10
  60.1 3.5 %collective-permute-start.11 = (bf16[400,128]{1,0:T(8,128)(2,1)S(1)}, bf16[400,128]{1,0:T(8,128)(2,1)S(1)}, u32[]{:S(2)}, u32[]{:S(2)}) collective-permute-start(bf16[400,128]{1,0:T(8,128)(2,1)S(1)} %get-tuple-element.64), channel_id=1, source_target_pairs={{0,2},{1,3},{2,0},{3,1},{4,10},{5,11},{6,8},{7,9},{8,6},{9,7},{10,... | collective-permute-start | bytes 307208 | tf_op jit(solution)/shard_map/ppermute | solution.py:429
  63.6 0.7 collective-permute-start.12
  64.3 0.2 all-to-all-done.1
  64.6 1.7 %shard_map.127 = (bf16[2,128,768]{2,1,0:T(8,128)(2,1)S(1)}, f32[2,128,128]{2,1,0:T(8,128)S(1)}, bf16[768,1536]{1,0:T(8,128)(2,1)S(1)}, f32[16,1536]{1,0:T(8,128)S(1)}) custom-call(bf16[256,896]{1,0:T(8,128)(2,1)S(1)} %bitcast.7, bf16[768,1536]{1,0:T(8,128)(2,1)} %wo_hbm.1, f32[16,1536]{1,0:T(8,128)} %get-tuple-element.66.own_hbm), custom_call_target="tpu_custom_call" | custom-call | flops 60000002048 | bytes 1048576 | tf_op jit(solution)/shard_map/pallas_call | solution.py:388
  66.3 0.0 collective-permute-done.9.refs_0_
  66.3 0.0 collective-permute-done.10.refs_1_
  66.3 0.9 %collective-permute-done.11.refs_2_ = bf16[400,128]{1,0:T(8,128)(2,1)S(1)} collective-permute-done((bf16[400,128]{1,0:T(8,128)(2,1)S(1)}, bf16[400,128]{1,0:T(8,128)(2,1)S(1)}, u32[]{:S(2)}, u32[]{:S(2)}) %collective-permute-start.11) | collective-permute-done | bytes 102432 | tf_op jit(solution)/shard_map/ppermute | solution.py:429
  67.2 2.6 %collective-permute-done.12.refs_3_ = bf16[400,128]{1,0:T(8,128)(2,1)S(1)} collective-permute-done((bf16[400,128]{1,0:T(8,128)(2,1)S(1)}, bf16[400,128]{1,0:T(8,128)(2,1)S(1)}, u32[]{:S(2)}, u32[]{:S(2)}) %collective-permute-start.12) | collective-permute-done | bytes 102432 | tf_op jit(solution)/shard_map/ppermute | solution.py:429
  69.8 1.0 %shard_map.128 = (bf16[128,768]{1,0:T(8,128)(2,1)S(1)}, bf16[128,768]{1,0:T(8,128)(2,1)S(1)}) custom-call(s32[3]{0:T(128)S(1)} %pad_add_fusion.place_ref, f32[1,32]{1,0:T(1,128)S(1)} %shard_map.125.mark_ref, bf16[400,128]{1,0:T(8,128)(2,1)S(1)} %collective-permute-done.9.refs_0_, bf16[400,128]{1,0:T(8,128)(2,1)S(1)} %collective-permute-done.10.refs_1_, ...), custom_call_target="tpu_custom_call" | custom-call | bytes 2097152 | tf_op jit(solution)/shard_map/pallas_call | solution.py:388
  70.8 1.9 %collective-permute-start.13 = (bf16[128,768]{1,0:T(8,128)(2,1)S(1)}, bf16[128,768]{1,0:T(8,128)(2,1)S(1)}, u32[]{:S(2)}, u32[]{:S(2)}) collective-permute-start(bf16[128,768]{1,0:T(8,128)(2,1)S(1)} %get-tuple-element.75), channel_id=1, source_target_pairs={{8,0},{16,8},{24,16},{32,24},{40,32},{48,40},{56,48},{64,56},{72,6... | collective-permute-start | bytes 589832 | tf_op jit(solution)/shard_map/ppermute | solution.py:552
  72.8 3.4 %shard_map.129 = (bf16[2,128,1536]{2,1,0:T(8,128)(2,1)}, bf16[2,128,1536]{2,1,0:T(8,128)(2,1)}, bf16[128,1536]{1,0:T(8,128)(2,1)S(1)}) custom-call(s32[3]{0:T(128)S(1)} %pad_add_fusion.place_ref, f32[3]{0:T(128)S(1)} %get-tuple-element.43.size_ref, bf16[400,128]{1,0:T(8,128)(2,1)S(1)} %collective-permute-done.9.refs_0_, ...), custom_call_target="tpu_custom_call" | custom-call | flops 603979776 | bytes 6291456 | tf_op jit(solution)/shard_map/pallas_call | solution.py:388
  76.2 4.0 %collective-permute-done.13.att_ref = bf16[128,768]{1,0:T(8,128)(2,1)S(1)} collective-permute-done((bf16[128,768]{1,0:T(8,128)(2,1)S(1)}, bf16[128,768]{1,0:T(8,128)(2,1)S(1)}, u32[]{:S(2)}, u32[]{:S(2)}) %collective-permute-start.13) | collective-permute-done | bytes 196640 | tf_op jit(solution)/shard_map/ppermute | solution.py:552
  80.2 1.7 %shard_map.130 = bf16[2,128,1536]{2,1,0:T(8,128)(2,1)} custom-call(f32[3]{0:T(128)S(1)} %get-tuple-element.43.size_ref, bf16[128,768]{1,0:T(8,128)(2,1)S(1)} %collective-permute-done.13.att_ref, bf16[768,1536]{1,0:T(8,128)(2,1)S(1)} %get-tuple-element.71.refs_7_.wo_ref, ...), custom_call_target="tpu_custom_call", output_to_operand_aliasing={{}: (5, {})} | custom-call | flops 301989888 | bytes 4194304 | tf_op jit(solution)/shard_map/pallas_call | solution.py:388
  (1 shorter events, 0.0 us)
Async XLA Ops:
  0.6 14.9 %copy-start.2 = (f32[32]{0:T(128)S(1)}, f32[32]{0:T(128)}, u32[]{:S(2)}) copy-start(f32[32]{0:T(128)} %step_ref.1) | copy-start | bytes 388
  0.6 14.9 %copy-start.1 = (s32[64]{0:T(128)S(1)}, s32[64]{0:T(128)}, u32[]{:S(2)}) copy-start(s32[64]{0:T(128)} %blocks_ref.1) | copy-start | bytes 772
  0.7 14.9 %copy-start = (s32[64]{0:T(128)S(1)}, s32[64]{0:T(128)}, u32[]{:S(2)}) copy-start(s32[64]{0:T(128)} %noise_ref.1) | copy-start | bytes 772
  2.8 34.8 %all-to-all-start = ((bf16[32,8,1536]{2,1,0:T(8,128)(2,1)}), bf16[32,8,1536]{2,1,0:T(8,128)(2,1)S(1)}, u32[]{:S(2)}, u32[]{:S(2)}) async-start(bf16[32,8,1536]{2,1,0:T(8,128)(2,1)} %bitcast.9), calls=%async_computation | async-start | bytes 1572864 | tf_op jit(solution)/shard_map/all_to_all | solution.py:444
  21.9 27.2 %collective-permute-start.1 = (bf16[1152,128]{1,0:T(8,128)(2,1)}, bf16[1152,128]{1,0:T(8,128)(2,1)S(1)}, u32[]{:S(2)}, u32[]{:S(2)}) collective-permute-start(bf16[1152,128]{1,0:T(8,128)(2,1)} %get-tuple-element.49), channel_id=1, source_target_pairs={{0,0},{1,1},{2,2},{3,3},{4,8},{5,9},{6,10},{7,11},{8,4},{9,5},{10,... | collective-permute-start | bytes 884744 | tf_op jit(solution)/shard_map/ppermute | solution.py:429
  25.0 24.2 %collective-permute-start.2 = (bf16[1152,128]{1,0:T(8,128)(2,1)S(1)}, bf16[1152,128]{1,0:T(8,128)(2,1)S(1)}, u32[]{:S(2)}, u32[]{:S(2)}) collective-permute-start(bf16[1152,128]{1,0:T(8,128)(2,1)S(1)} %get-tuple-element.50), channel_id=1, source_target_pairs={{0,1},{1,0},{2,3},{3,2},{4,9},{5,8},{6,11},{7,10},{8,5},{9,4},{10,... | collective-permute-start | bytes 884744 | tf_op jit(solution)/shard_map/ppermute | solution.py:429
  26.7 22.5 %collective-permute-start.3 = (bf16[1152,128]{1,0:T(8,128)(2,1)S(1)}, bf16[1152,128]{1,0:T(8,128)(2,1)S(1)}, u32[]{:S(2)}, u32[]{:S(2)}) collective-permute-start(bf16[1152,128]{1,0:T(8,128)(2,1)S(1)} %get-tuple-element.51), channel_id=1, source_target_pairs={{0,2},{1,3},{2,0},{3,1},{4,10},{5,11},{6,8},{7,9},{8,6},{9,7},{10,... | collective-permute-start | bytes 884744 | tf_op jit(solution)/shard_map/ppermute | solution.py:429
  30.2 19.0 %collective-permute-start.4 = (bf16[1152,128]{1,0:T(8,128)(2,1)S(1)}, bf16[1152,128]{1,0:T(8,128)(2,1)S(1)}, u32[]{:S(2)}, u32[]{:S(2)}) collective-permute-start(bf16[1152,128]{1,0:T(8,128)(2,1)S(1)} %get-tuple-element.52), channel_id=1, source_target_pairs={{0,3},{1,2},{2,1},{3,0},{4,11},{5,10},{6,9},{7,8},{8,7},{9,6},{10,... | collective-permute-start | bytes 884744 | tf_op jit(solution)/shard_map/ppermute | solution.py:429
  30.4 18.8 %collective-permute-start = (bf16[128,1536]{1,0:T(8,128)(2,1)}, bf16[128,1536]{1,0:T(8,128)(2,1)S(1)}, u32[]{:S(2)}, u32[]{:S(2)}) collective-permute-start(bf16[128,1536]{1,0:T(8,128)(2,1)} %get-tuple-element.48), channel_id=1, source_target_pairs={{8,0},{16,8},{24,16},{32,24},{40,32},{48,40},{56,48},{64,56},{72,6... | collective-permute-start | bytes 1179656 | tf_op jit(solution)/shard_map/ppermute | solution.py:488
  43.8 20.8 %all-to-all-start.1 = ((bf16[32,8,896]{2,1,0:T(8,128)(2,1)}), bf16[32,8,896]{2,1,0:T(8,128)(2,1)S(1)}, u32[]{:S(2)}, u32[]{:S(2)}) async-start(bf16[32,8,896]{2,1,0:T(8,128)(2,1)} %bitcast.10), calls=%async_computation.1 | async-start | bytes 917504 | tf_op jit(solution)/shard_map/all_to_all | solution.py:513
  49.2 1.7 %collective-permute-start.5 = (bf16[1152,128]{1,0:T(8,128)(2,1)S(1)}, bf16[1152,128]{1,0:T(8,128)(2,1)S(1)}, u32[]{:S(2)}, u32[]{:S(2)}) collective-permute-start(bf16[1152,128]{1,0:T(8,128)(2,1)S(1)} %collective-permute-done.1.refs_0_), channel_id=1, source_target_pairs={{0,8},{8,0},{16,24},{24,16},{32,40},{40,32},{48,56},{56,48},{64,72... | collective-permute-start | bytes 884744 | tf_op jit(solution)/shard_map/ppermute | solution.py:512
  49.7 1.6 %collective-permute-start.6 = (bf16[1152,128]{1,0:T(8,128)(2,1)S(1)}, bf16[1152,128]{1,0:T(8,128)(2,1)S(1)}, u32[]{:S(2)}, u32[]{:S(2)}) collective-permute-start(bf16[1152,128]{1,0:T(8,128)(2,1)S(1)} %collective-permute-done.2.refs_1_), channel_id=1, source_target_pairs={{0,8},{8,0},{16,24},{24,16},{32,40},{40,32},{48,56},{56,48},{64,72... | collective-permute-start | bytes 884744 | tf_op jit(solution)/shard_map/ppermute | solution.py:512
  49.8 1.9 %collective-permute-start.7 = (bf16[1152,128]{1,0:T(8,128)(2,1)S(1)}, bf16[1152,128]{1,0:T(8,128)(2,1)S(1)}, u32[]{:S(2)}, u32[]{:S(2)}) collective-permute-start(bf16[1152,128]{1,0:T(8,128)(2,1)S(1)} %collective-permute-done.3.refs_2_), channel_id=1, source_target_pairs={{0,8},{8,0},{16,24},{24,16},{32,40},{40,32},{48,56},{56,48},{64,72... | collective-permute-start | bytes 884744 | tf_op jit(solution)/shard_map/ppermute | solution.py:512
  50.2 2.0 %collective-permute-start.8 = (bf16[1152,128]{1,0:T(8,128)(2,1)S(1)}, bf16[1152,128]{1,0:T(8,128)(2,1)S(1)}, u32[]{:S(2)}, u32[]{:S(2)}) collective-permute-start(bf16[1152,128]{1,0:T(8,128)(2,1)S(1)} %collective-permute-done.4.refs_3_), channel_id=1, source_target_pairs={{0,8},{8,0},{16,24},{24,16},{32,40},{40,32},{48,56},{56,48},{64,72... | collective-permute-start | bytes 884744 | tf_op jit(solution)/shard_map/ppermute | solution.py:512
  55.4 10.9 %collective-permute-start.9 = (bf16[400,128]{1,0:T(8,128)(2,1)S(1)}, bf16[400,128]{1,0:T(8,128)(2,1)S(1)}, u32[]{:S(2)}, u32[]{:S(2)}) collective-permute-start(bf16[400,128]{1,0:T(8,128)(2,1)S(1)} %get-tuple-element.62), channel_id=1, source_target_pairs={{0,0},{1,1},{2,2},{3,3},{4,8},{5,9},{6,10},{7,11},{8,4},{9,5},{10,... | collective-permute-start | bytes 307208 | tf_op jit(solution)/shard_map/ppermute | solution.py:429
  59.5 6.8 %collective-permute-start.10 = (bf16[400,128]{1,0:T(8,128)(2,1)S(1)}, bf16[400,128]{1,0:T(8,128)(2,1)S(1)}, u32[]{:S(2)}, u32[]{:S(2)}) collective-permute-start(bf16[400,128]{1,0:T(8,128)(2,1)S(1)} %get-tuple-element.63), channel_id=1, source_target_pairs={{0,1},{1,0},{2,3},{3,2},{4,9},{5,8},{6,11},{7,10},{8,5},{9,4},{10,... | collective-permute-start | bytes 307208 | tf_op jit(solution)/shard_map/ppermute | solution.py:429
  60.1 7.1 %collective-permute-start.11 = (bf16[400,128]{1,0:T(8,128)(2,1)S(1)}, bf16[400,128]{1,0:T(8,128)(2,1)S(1)}, u32[]{:S(2)}, u32[]{:S(2)}) collective-permute-start(bf16[400,128]{1,0:T(8,128)(2,1)S(1)} %get-tuple-element.64), channel_id=1, source_target_pairs={{0,2},{1,3},{2,0},{3,1},{4,10},{5,11},{6,8},{7,9},{8,6},{9,7},{10,... | collective-permute-start | bytes 307208 | tf_op jit(solution)/shard_map/ppermute | solution.py:429
  63.6 6.2 %collective-permute-start.12 = (bf16[400,128]{1,0:T(8,128)(2,1)S(1)}, bf16[400,128]{1,0:T(8,128)(2,1)S(1)}, u32[]{:S(2)}, u32[]{:S(2)}) collective-permute-start(bf16[400,128]{1,0:T(8,128)(2,1)S(1)} %get-tuple-element.65), channel_id=1, source_target_pairs={{0,3},{1,2},{2,1},{3,0},{4,11},{5,10},{6,9},{7,8},{8,7},{9,6},{10,... | collective-permute-start | bytes 307208 | tf_op jit(solution)/shard_map/ppermute | solution.py:429
  70.8 9.4 %collective-permute-start.13 = (bf16[128,768]{1,0:T(8,128)(2,1)S(1)}, bf16[128,768]{1,0:T(8,128)(2,1)S(1)}, u32[]{:S(2)}, u32[]{:S(2)}) collective-permute-start(bf16[128,768]{1,0:T(8,128)(2,1)S(1)} %get-tuple-element.75), channel_id=1, source_target_pairs={{8,0},{16,8},{24,16},{32,24},{40,32},{48,40},{56,48},{64,56},{72,6... | collective-permute-start | bytes 589832 | tf_op jit(solution)/shard_map/ppermute | solution.py:552

commit v9 on v8

--- a/solution.py
+++ b/solution.py
@@ -582,7 +582,7 @@
             pltpu.VMEM((frames, tokens, width), BF16),
             pltpu.VMEM((frames - 1, tokens, width), BF16),
             dma((2,)),
-            *[dma((3,))] * 2,
+            *[dma((6,))] * 2,
         ],
     )
     following = call(
@@ -593,7 +593,7 @@
         anywhere(),
         flops=project_flops // 2,
         nbytes=4 * MIB,
-        scratch_shapes=[pltpu.VMEM((tokens, width), BF16), dma((3,))],
+        scratch_shapes=[pltpu.VMEM((tokens, width), BF16), dma((6,))],
         input_output_aliases={5: 0},
     )
     return velocity, following

time: 82.6 us -> 82.6 us (level)
  no operation moved by 1% of the time
where the time goes in v9:
time: 82.6 us; the launch traced here: 82.1 us
  starting transfers between devices  39.7 us (48%)
  Pallas kernels  25.8 us (31%)
  waiting for transfers between devices  14.8 us (18%)
  between operations  1.64 us (2%)
    pallas_call x9, Pallas kernels, call(): pl.pallas_call(kernel, out_shape=outs, in_specs=in_specs, out_specs=out_s...  25.8 us
    ppermute x8, starting transfers between devices, exchange(): return lax.ppermute(x, ('tm', 'tok'), pairs)  17.5 us
    all_to_all x1, starting transfers between devices, body(): lax.all_to_all(outgoing.reshape(times, frames * share, width), 'tm', 0, 0)  11.9 us
    all_to_all x1, starting transfers between devices, body(): lax.all_to_all(back.reshape(times, frames * share, inner + HEAD_DIM), 'tm...  5.42 us
    all_to_all x1, waiting for transfers between devices, body(): lax.all_to_all(outgoing.reshape(times, frames * share, width), 'tm', 0, 0)  5.3 us
    ppermute x1, waiting for transfers between devices, body(): next_first = lax.ppermute(sent, 'tm', back_perm)  3.95 us
    ppermute x8, waiting for transfers between devices, exchange(): return lax.ppermute(x, ('tm', 'tok'), pairs)  3.52 us
    ppermute x1, starting transfers between devices, body(): next_first = lax.ppermute(sent, 'tm', back_perm)  1.92 us
  transfers between devices with their start and end apart: 16, of which 9 were waited for; matrix products, arithmetic and copies ran while one was open for 0% of the time, Pallas kernels for 25%

profile of v9, /device:TPU:5, one launch (start us, length us, event | category | flops | bytes accessed | tf_op | source)
XLA Modules:
  0.0 82.1 jit_solution(286701905518563055)
XLA Ops:
  0.6 0.0 copy-start.2
  0.6 0.0 copy-start.1
  0.7 0.0 copy-start
  0.7 2.2 %shard_map.122 = (bf16[16,2,8,1536]{3,2,1,0:T(8,128)(2,1)}, bf16[128,1536]{1,0:T(8,128)(2,1)}, bf16[2,128,1536]{2,1,0:T(8,128)(2,1)S(1)}) custom-call(bf16[2,128,1536]{2,1,0:T(8,128)(2,1)} %refs_10_.1), custom_call_target="tpu_custom_call" | custom-call | bytes 2097152 | tf_op jit(solution)/shard_map/pallas_call | solution.py:388
  2.8 11.9 %all-to-all-start = ((bf16[32,8,1536]{2,1,0:T(8,128)(2,1)}), bf16[32,8,1536]{2,1,0:T(8,128)(2,1)S(1)}, u32[]{:S(2)}, u32[]{:S(2)}) async-start(bf16[32,8,1536]{2,1,0:T(8,128)(2,1)} %bitcast.9), calls=%async_computation | async-start | bytes 1572864 | tf_op jit(solution)/shard_map/all_to_all | solution.py:444
  15.4 0.1 pad_add_fusion.place_ref
  15.5 0.0 copy-done.2
  15.5 0.0 copy-done.1
  15.5 0.0 copy-done
  15.5 6.4 %shard_map.123 = (f32[3]{0:T(128)S(1)}, f32[16,1536]{1,0:T(8,128)}, f32[32,2,1536]{2,1,0:T(2,128)}, f32[32,2,1536]{2,1,0:T(2,128)}, f32[256,256]{1,0:T(8,128)}, ...) custom-call(s32[64]{0:T(128)S(1)} %copy-done, ...), custom_call_target="tpu_custom_call" | custom-call | flops 60000002048 | bytes 10485760 | tf_op jit(solution)/shard_map/pallas_call | solution.py:388
  21.9 3.1 %collective-permute-start.1 = (bf16[1152,128]{1,0:T(8,128)(2,1)}, bf16[1152,128]{1,0:T(8,128)(2,1)S(1)}, u32[]{:S(2)}, u32[]{:S(2)}) collective-permute-start(bf16[1152,128]{1,0:T(8,128)(2,1)} %get-tuple-element.49), channel_id=1, source_target_pairs={{0,0},{1,1},{2,2},{3,3},{4,8},{5,9},{6,10},{7,11},{8,4},{9,5},{10,... | collective-permute-start | bytes 884744 | tf_op jit(solution)/shard_map/ppermute | solution.py:429
  25.0 1.7 %collective-permute-start.2 = (bf16[1152,128]{1,0:T(8,128)(2,1)S(1)}, bf16[1152,128]{1,0:T(8,128)(2,1)S(1)}, u32[]{:S(2)}, u32[]{:S(2)}) collective-permute-start(bf16[1152,128]{1,0:T(8,128)(2,1)S(1)} %get-tuple-element.50), channel_id=1, source_target_pairs={{0,1},{1,0},{2,3},{3,2},{4,9},{5,8},{6,11},{7,10},{8,5},{9,4},{10,... | collective-permute-start | bytes 884744 | tf_op jit(solution)/shard_map/ppermute | solution.py:429
  26.7 3.5 %collective-permute-start.3 = (bf16[1152,128]{1,0:T(8,128)(2,1)S(1)}, bf16[1152,128]{1,0:T(8,128)(2,1)S(1)}, u32[]{:S(2)}, u32[]{:S(2)}) collective-permute-start(bf16[1152,128]{1,0:T(8,128)(2,1)S(1)} %get-tuple-element.51), channel_id=1, source_target_pairs={{0,2},{1,3},{2,0},{3,1},{4,10},{5,11},{6,8},{7,9},{8,6},{9,7},{10,... | collective-permute-start | bytes 884744 | tf_op jit(solution)/shard_map/ppermute | solution.py:429
  30.2 0.2 collective-permute-start.4
  30.4 1.9 %collective-permute-start = (bf16[128,1536]{1,0:T(8,128)(2,1)}, bf16[128,1536]{1,0:T(8,128)(2,1)S(1)}, u32[]{:S(2)}, u32[]{:S(2)}) collective-permute-start(bf16[128,1536]{1,0:T(8,128)(2,1)} %get-tuple-element.48), channel_id=1, source_target_pairs={{8,0},{16,8},{24,16},{32,24},{40,32},{48,40},{56,48},{64,56},{72,6... | collective-permute-start | bytes 1179656 | tf_op jit(solution)/shard_map/ppermute | solution.py:488
  32.4 5.3 %all-to-all-done.x_ref = bf16[32,8,1536]{2,1,0:T(8,128)(2,1)S(1)} async-done(((bf16[32,8,1536]{2,1,0:T(8,128)(2,1)}), bf16[32,8,1536]{2,1,0:T(8,128)(2,1)S(1)}, u32[]{:S(2)}, u32[]{:S(2)}) %all-to-all-start) | async-done | bytes 786464 | tf_op jit(solution)/shard_map/all_to_all | solution.py:444
  37.7 6.1 %shard_map.124 = bf16[256,896]{1,0:T(8,128)(2,1)} custom-call(bf16[32,8,1536]{2,1,0:T(8,128)(2,1)S(1)} %all-to-all-done.x_ref, f32[32,2,1536]{2,1,0:T(2,128)} %get-tuple-element.45.refs_0_, f32[32,2,1536]{2,1,0:T(2,128)} %get-tuple-element.46.refs_1_, bf16[1536,768]{1,0:T(8,128)(2,1)} %refs_2_.1, bf16[1536,768]{1,0:T(8,128)(2,1)} %refs_3_.1, ...), custom_call_target="tpu_custom_call" | custom-call | flops 60000002048 | bytes 10485760 | tf_op jit(solution)/shard_map/pallas_call | solution.py:388
  43.8 5.4 %all-to-all-start.1 = ((bf16[32,8,896]{2,1,0:T(8,128)(2,1)}), bf16[32,8,896]{2,1,0:T(8,128)(2,1)S(1)}, u32[]{:S(2)}, u32[]{:S(2)}) async-start(bf16[32,8,896]{2,1,0:T(8,128)(2,1)} %bitcast.10), calls=%async_computation.1 | async-start | bytes 917504 | tf_op jit(solution)/shard_map/all_to_all | solution.py:513
  49.2 0.0 collective-permute-done.1.refs_0_
  49.2 0.0 collective-permute-done.2.refs_1_
  49.2 0.0 collective-permute-done.3.refs_2_
  49.2 0.0 collective-permute-done.4.refs_3_
  49.2 0.0 collective-permute-done.refs_9_
  49.2 0.4 collective-permute-start.5
  49.7 0.1 collective-permute-start.6
  49.8 0.4 collective-permute-start.7
  50.2 0.1 collective-permute-start.8
  50.4 0.6 collective-permute-done.5.refs_4_
  50.9 0.4 collective-permute-done.6.refs_5_
  51.3 0.4 collective-permute-done.7.refs_6_
  51.8 0.4 collective-permute-done.8.refs_7_
  52.2 3.2 %shard_map.126 = (bf16[400,128]{1,0:T(8,128)(2,1)S(1)}, bf16[400,128]{1,0:T(8,128)(2,1)S(1)}, bf16[400,128]{1,0:T(8,128)(2,1)S(1)}, bf16[400,128]{1,0:T(8,128)(2,1)S(1)}) custom-call(bf16[1152,128]{1,0:T(8,128)(2,1)S(1)} %collective-permute-done.1.refs_0_, bf16[1152,128]{1,0:T(8,128)(2,1)S(1)} %collective-permute-done.2.refs_1_, ...), custom_call_target="tpu_custom_call" | custom-call | flops 805306368 | bytes 3145728 | tf_op jit(solution)/shard_map/pallas_call | solution.py:388
  55.4 4.1 %collective-permute-start.9 = (bf16[400,128]{1,0:T(8,128)(2,1)S(1)}, bf16[400,128]{1,0:T(8,128)(2,1)S(1)}, u32[]{:S(2)}, u32[]{:S(2)}) collective-permute-start(bf16[400,128]{1,0:T(8,128)(2,1)S(1)} %get-tuple-element.62), channel_id=1, source_target_pairs={{0,0},{1,1},{2,2},{3,3},{4,8},{5,9},{6,10},{7,11},{8,4},{9,5},{10,... | collective-permute-start | bytes 307208 | tf_op jit(solution)/shard_map/ppermute | solution.py:429
  59.5 0.6 collective-permute-start.10
  60.1 3.5 %collective-permute-start.11 = (bf16[400,128]{1,0:T(8,128)(2,1)S(1)}, bf16[400,128]{1,0:T(8,128)(2,1)S(1)}, u32[]{:S(2)}, u32[]{:S(2)}) collective-permute-start(bf16[400,128]{1,0:T(8,128)(2,1)S(1)} %get-tuple-element.64), channel_id=1, source_target_pairs={{0,2},{1,3},{2,0},{3,1},{4,10},{5,11},{6,8},{7,9},{8,6},{9,7},{10,... | collective-permute-start | bytes 307208 | tf_op jit(solution)/shard_map/ppermute | solution.py:429
  63.6 0.7 collective-permute-start.12
  64.3 0.2 all-to-all-done.1
  64.6 1.7 %shard_map.127 = (bf16[2,128,768]{2,1,0:T(8,128)(2,1)S(1)}, f32[2,128,128]{2,1,0:T(8,128)S(1)}, bf16[768,1536]{1,0:T(8,128)(2,1)S(1)}, f32[16,1536]{1,0:T(8,128)S(1)}) custom-call(bf16[256,896]{1,0:T(8,128)(2,1)S(1)} %bitcast.7, bf16[768,1536]{1,0:T(8,128)(2,1)} %wo_hbm.1, f32[16,1536]{1,0:T(8,128)} %get-tuple-element.66.own_hbm), custom_call_target="tpu_custom_call" | custom-call | flops 60000002048 | bytes 1048576 | tf_op jit(solution)/shard_map/pallas_call | solution.py:388
  66.3 0.0 collective-permute-done.9.refs_0_
  66.3 0.0 collective-permute-done.10.refs_1_
  66.3 0.9 %collective-permute-done.11.refs_2_ = bf16[400,128]{1,0:T(8,128)(2,1)S(1)} collective-permute-done((bf16[400,128]{1,0:T(8,128)(2,1)S(1)}, bf16[400,128]{1,0:T(8,128)(2,1)S(1)}, u32[]{:S(2)}, u32[]{:S(2)}) %collective-permute-start.11) | collective-permute-done | bytes 102432 | tf_op jit(solution)/shard_map/ppermute | solution.py:429
  67.2 2.6 %collective-permute-done.12.refs_3_ = bf16[400,128]{1,0:T(8,128)(2,1)S(1)} collective-permute-done((bf16[400,128]{1,0:T(8,128)(2,1)S(1)}, bf16[400,128]{1,0:T(8,128)(2,1)S(1)}, u32[]{:S(2)}, u32[]{:S(2)}) %collective-permute-start.12) | collective-permute-done | bytes 102432 | tf_op jit(solution)/shard_map/ppermute | solution.py:429
  69.8 1.0 %shard_map.128 = (bf16[128,768]{1,0:T(8,128)(2,1)S(1)}, bf16[128,768]{1,0:T(8,128)(2,1)S(1)}) custom-call(s32[3]{0:T(128)S(1)} %pad_add_fusion.place_ref, f32[1,32]{1,0:T(1,128)S(1)} %shard_map.125.mark_ref, bf16[400,128]{1,0:T(8,128)(2,1)S(1)} %collective-permute-done.9.refs_0_, bf16[400,128]{1,0:T(8,128)(2,1)S(1)} %collective-permute-done.10.refs_1_, ...), custom_call_target="tpu_custom_call" | custom-call | bytes 2097152 | tf_op jit(solution)/shard_map/pallas_call | solution.py:388
  70.8 1.9 %collective-permute-start.13 = (bf16[128,768]{1,0:T(8,128)(2,1)S(1)}, bf16[128,768]{1,0:T(8,128)(2,1)S(1)}, u32[]{:S(2)}, u32[]{:S(2)}) collective-permute-start(bf16[128,768]{1,0:T(8,128)(2,1)S(1)} %get-tuple-element.75), channel_id=1, source_target_pairs={{8,0},{16,8},{24,16},{32,24},{40,32},{48,40},{56,48},{64,56},{72,6... | collective-permute-start | bytes 589832 | tf_op jit(solution)/shard_map/ppermute | solution.py:552
  72.8 3.5 %shard_map.129 = (bf16[2,128,1536]{2,1,0:T(8,128)(2,1)}, bf16[2,128,1536]{2,1,0:T(8,128)(2,1)}, bf16[128,1536]{1,0:T(8,128)(2,1)S(1)}) custom-call(s32[3]{0:T(128)S(1)} %pad_add_fusion.place_ref, f32[3]{0:T(128)S(1)} %get-tuple-element.43.size_ref, bf16[400,128]{1,0:T(8,128)(2,1)S(1)} %collective-permute-done.9.refs_0_, ...), custom_call_target="tpu_custom_call" | custom-call | flops 603979776 | bytes 6291456 | tf_op jit(solution)/shard_map/pallas_call | solution.py:388
  76.3 3.9 %collective-permute-done.13.att_ref = bf16[128,768]{1,0:T(8,128)(2,1)S(1)} collective-permute-done((bf16[128,768]{1,0:T(8,128)(2,1)S(1)}, bf16[128,768]{1,0:T(8,128)(2,1)S(1)}, u32[]{:S(2)}, u32[]{:S(2)}) %collective-permute-start.13) | collective-permute-done | bytes 196640 | tf_op jit(solution)/shard_map/ppermute | solution.py:552
  80.2 1.7 %shard_map.130 = bf16[2,128,1536]{2,1,0:T(8,128)(2,1)} custom-call(f32[3]{0:T(128)S(1)} %get-tuple-element.43.size_ref, bf16[128,768]{1,0:T(8,128)(2,1)S(1)} %collective-permute-done.13.att_ref, bf16[768,1536]{1,0:T(8,128)(2,1)S(1)} %get-tuple-element.71.refs_7_.wo_ref, ...), custom_call_target="tpu_custom_call", output_to_operand_aliasing={{}: (5, {})} | custom-call | flops 301989888 | bytes 4194304 | tf_op jit(solution)/shard_map/pallas_call | solution.py:388
  (1 shorter events, 0.0 us)
Async XLA Ops:
  0.6 14.9 %copy-start.2 = (f32[32]{0:T(128)S(1)}, f32[32]{0:T(128)}, u32[]{:S(2)}) copy-start(f32[32]{0:T(128)} %step_ref.1) | copy-start | bytes 388
  0.6 14.9 %copy-start.1 = (s32[64]{0:T(128)S(1)}, s32[64]{0:T(128)}, u32[]{:S(2)}) copy-start(s32[64]{0:T(128)} %blocks_ref.1) | copy-start | bytes 772
  0.7 14.9 %copy-start = (s32[64]{0:T(128)S(1)}, s32[64]{0:T(128)}, u32[]{:S(2)}) copy-start(s32[64]{0:T(128)} %noise_ref.1) | copy-start | bytes 772
  2.8 34.8 %all-to-all-start = ((bf16[32,8,1536]{2,1,0:T(8,128)(2,1)}), bf16[32,8,1536]{2,1,0:T(8,128)(2,1)S(1)}, u32[]{:S(2)}, u32[]{:S(2)}) async-start(bf16[32,8,1536]{2,1,0:T(8,128)(2,1)} %bitcast.9), calls=%async_computation | async-start | bytes 1572864 | tf_op jit(solution)/shard_map/all_to_all | solution.py:444
  21.9 27.2 %collective-permute-start.1 = (bf16[1152,128]{1,0:T(8,128)(2,1)}, bf16[1152,128]{1,0:T(8,128)(2,1)S(1)}, u32[]{:S(2)}, u32[]{:S(2)}) collective-permute-start(bf16[1152,128]{1,0:T(8,128)(2,1)} %get-tuple-element.49), channel_id=1, source_target_pairs={{0,0},{1,1},{2,2},{3,3},{4,8},{5,9},{6,10},{7,11},{8,4},{9,5},{10,... | collective-permute-start | bytes 884744 | tf_op jit(solution)/shard_map/ppermute | solution.py:429
  25.0 24.2 %collective-permute-start.2 = (bf16[1152,128]{1,0:T(8,128)(2,1)S(1)}, bf16[1152,128]{1,0:T(8,128)(2,1)S(1)}, u32[]{:S(2)}, u32[]{:S(2)}) collective-permute-start(bf16[1152,128]{1,0:T(8,128)(2,1)S(1)} %get-tuple-element.50), channel_id=1, source_target_pairs={{0,1},{1,0},{2,3},{3,2},{4,9},{5,8},{6,11},{7,10},{8,5},{9,4},{10,... | collective-permute-start | bytes 884744 | tf_op jit(solution)/shard_map/ppermute | solution.py:429
  26.7 22.5 %collective-permute-start.3 = (bf16[1152,128]{1,0:T(8,128)(2,1)S(1)}, bf16[1152,128]{1,0:T(8,128)(2,1)S(1)}, u32[]{:S(2)}, u32[]{:S(2)}) collective-permute-start(bf16[1152,128]{1,0:T(8,128)(2,1)S(1)} %get-tuple-element.51), channel_id=1, source_target_pairs={{0,2},{1,3},{2,0},{3,1},{4,10},{5,11},{6,8},{7,9},{8,6},{9,7},{10,... | collective-permute-start | bytes 884744 | tf_op jit(solution)/shard_map/ppermute | solution.py:429
  30.2 19.0 %collective-permute-start.4 = (bf16[1152,128]{1,0:T(8,128)(2,1)S(1)}, bf16[1152,128]{1,0:T(8,128)(2,1)S(1)}, u32[]{:S(2)}, u32[]{:S(2)}) collective-permute-start(bf16[1152,128]{1,0:T(8,128)(2,1)S(1)} %get-tuple-element.52), channel_id=1, source_target_pairs={{0,3},{1,2},{2,1},{3,0},{4,11},{5,10},{6,9},{7,8},{8,7},{9,6},{10,... | collective-permute-start | bytes 884744 | tf_op jit(solution)/shard_map/ppermute | solution.py:429
  30.4 18.8 %collective-permute-start = (bf16[128,1536]{1,0:T(8,128)(2,1)}, bf16[128,1536]{1,0:T(8,128)(2,1)S(1)}, u32[]{:S(2)}, u32[]{:S(2)}) collective-permute-start(bf16[128,1536]{1,0:T(8,128)(2,1)} %get-tuple-element.48), channel_id=1, source_target_pairs={{8,0},{16,8},{24,16},{32,24},{40,32},{48,40},{56,48},{64,56},{72,6... | collective-permute-start | bytes 1179656 | tf_op jit(solution)/shard_map/ppermute | solution.py:488
  43.8 20.8 %all-to-all-start.1 = ((bf16[32,8,896]{2,1,0:T(8,128)(2,1)}), bf16[32,8,896]{2,1,0:T(8,128)(2,1)S(1)}, u32[]{:S(2)}, u32[]{:S(2)}) async-start(bf16[32,8,896]{2,1,0:T(8,128)(2,1)} %bitcast.10), calls=%async_computation.1 | async-start | bytes 917504 | tf_op jit(solution)/shard_map/all_to_all | solution.py:513
  49.2 1.7 %collective-permute-start.5 = (bf16[1152,128]{1,0:T(8,128)(2,1)S(1)}, bf16[1152,128]{1,0:T(8,128)(2,1)S(1)}, u32[]{:S(2)}, u32[]{:S(2)}) collective-permute-start(bf16[1152,128]{1,0:T(8,128)(2,1)S(1)} %collective-permute-done.1.refs_0_), channel_id=1, source_target_pairs={{0,8},{8,0},{16,24},{24,16},{32,40},{40,32},{48,56},{56,48},{64,72... | collective-permute-start | bytes 884744 | tf_op jit(solution)/shard_map/ppermute | solution.py:512
  49.7 1.6 %collective-permute-start.6 = (bf16[1152,128]{1,0:T(8,128)(2,1)S(1)}, bf16[1152,128]{1,0:T(8,128)(2,1)S(1)}, u32[]{:S(2)}, u32[]{:S(2)}) collective-permute-start(bf16[1152,128]{1,0:T(8,128)(2,1)S(1)} %collective-permute-done.2.refs_1_), channel_id=1, source_target_pairs={{0,8},{8,0},{16,24},{24,16},{32,40},{40,32},{48,56},{56,48},{64,72... | collective-permute-start | bytes 884744 | tf_op jit(solution)/shard_map/ppermute | solution.py:512
  49.8 1.9 %collective-permute-start.7 = (bf16[1152,128]{1,0:T(8,128)(2,1)S(1)}, bf16[1152,128]{1,0:T(8,128)(2,1)S(1)}, u32[]{:S(2)}, u32[]{:S(2)}) collective-permute-start(bf16[1152,128]{1,0:T(8,128)(2,1)S(1)} %collective-permute-done.3.refs_2_), channel_id=1, source_target_pairs={{0,8},{8,0},{16,24},{24,16},{32,40},{40,32},{48,56},{56,48},{64,72... | collective-permute-start | bytes 884744 | tf_op jit(solution)/shard_map/ppermute | solution.py:512
  50.2 2.0 %collective-permute-start.8 = (bf16[1152,128]{1,0:T(8,128)(2,1)S(1)}, bf16[1152,128]{1,0:T(8,128)(2,1)S(1)}, u32[]{:S(2)}, u32[]{:S(2)}) collective-permute-start(bf16[1152,128]{1,0:T(8,128)(2,1)S(1)} %collective-permute-done.4.refs_3_), channel_id=1, source_target_pairs={{0,8},{8,0},{16,24},{24,16},{32,40},{40,32},{48,56},{56,48},{64,72... | collective-permute-start | bytes 884744 | tf_op jit(solution)/shard_map/ppermute | solution.py:512
  55.4 10.9 %collective-permute-start.9 = (bf16[400,128]{1,0:T(8,128)(2,1)S(1)}, bf16[400,128]{1,0:T(8,128)(2,1)S(1)}, u32[]{:S(2)}, u32[]{:S(2)}) collective-permute-start(bf16[400,128]{1,0:T(8,128)(2,1)S(1)} %get-tuple-element.62), channel_id=1, source_target_pairs={{0,0},{1,1},{2,2},{3,3},{4,8},{5,9},{6,10},{7,11},{8,4},{9,5},{10,... | collective-permute-start | bytes 307208 | tf_op jit(solution)/shard_map/ppermute | solution.py:429
  59.5 6.8 %collective-permute-start.10 = (bf16[400,128]{1,0:T(8,128)(2,1)S(1)}, bf16[400,128]{1,0:T(8,128)(2,1)S(1)}, u32[]{:S(2)}, u32[]{:S(2)}) collective-permute-start(bf16[400,128]{1,0:T(8,128)(2,1)S(1)} %get-tuple-element.63), channel_id=1, source_target_pairs={{0,1},{1,0},{2,3},{3,2},{4,9},{5,8},{6,11},{7,10},{8,5},{9,4},{10,... | collective-permute-start | bytes 307208 | tf_op jit(solution)/shard_map/ppermute | solution.py:429
  60.1 7.1 %collective-permute-start.11 = (bf16[400,128]{1,0:T(8,128)(2,1)S(1)}, bf16[400,128]{1,0:T(8,128)(2,1)S(1)}, u32[]{:S(2)}, u32[]{:S(2)}) collective-permute-start(bf16[400,128]{1,0:T(8,128)(2,1)S(1)} %get-tuple-element.64), channel_id=1, source_target_pairs={{0,2},{1,3},{2,0},{3,1},{4,10},{5,11},{6,8},{7,9},{8,6},{9,7},{10,... | collective-permute-start | bytes 307208 | tf_op jit(solution)/shard_map/ppermute | solution.py:429
  63.6 6.2 %collective-permute-start.12 = (bf16[400,128]{1,0:T(8,128)(2,1)S(1)}, bf16[400,128]{1,0:T(8,128)(2,1)S(1)}, u32[]{:S(2)}, u32[]{:S(2)}) collective-permute-start(bf16[400,128]{1,0:T(8,128)(2,1)S(1)} %get-tuple-element.65), channel_id=1, source_target_pairs={{0,3},{1,2},{2,1},{3,0},{4,11},{5,10},{6,9},{7,8},{8,7},{9,6},{10,... | collective-permute-start | bytes 307208 | tf_op jit(solution)/shard_map/ppermute | solution.py:429
  70.8 9.4 %collective-permute-start.13 = (bf16[128,768]{1,0:T(8,128)(2,1)S(1)}, bf16[128,768]{1,0:T(8,128)(2,1)S(1)}, u32[]{:S(2)}, u32[]{:S(2)}) collective-permute-start(bf16[128,768]{1,0:T(8,128)(2,1)S(1)} %get-tuple-element.75), channel_id=1, source_target_pairs={{8,0},{16,8},{24,16},{32,24},{40,32},{48,40},{56,48},{64,56},{72,6... | collective-permute-start | bytes 589832 | tf_op jit(solution)/shard_map/ppermute | solution.py:552
